TPU v7x, 512 devices: a whole 4x4x16 slice. The times are simulated.
512 devices in a mesh: feat: 8 (over y, core), node: 64 (over x, z).
Axes of the slice: x: 4, y: 4, z: 16, core: 2. Of those that a mesh axis runs over, the one named last changes fastest.
Arguments:
- node_features: bfloat16 [32768, 1024], P('node', 'feat'), may hold values from -6 to 6
- self_one: bfloat16 [1024, 256], P('feat'), may hold values from -0.1875 to 0.1875
- neighbour_one: bfloat16 [1024, 256], P('feat'), may hold values from -0.75 to 0.75
- sample_ids: int32 [64, 64, 32], P('node'), may hold values from 0 to 511
- dest_slots: int32 [64, 64, 32], P('node'), may hold values from 0 to 127
- send_counts: int32 [64, 64], replicated, may hold values from 1 to 32, as said below
- self_ids: int32 [64, 128], P('node'), may hold values from 0 to 511
- tile_blocks: int32 [64, 4], P('node'), may hold values from 0 to 63, as said below
- tile_weights: bfloat16 [64, 4, 128, 128], P('node'), may hold values from -0.25 to 0.25
- self_two: bfloat16 [256, 256], replicated, may hold values from -0.375 to 0.375
- neighbour_two: bfloat16 [256, 256], replicated, may hold values from -0.375 to 0.375
- out_grad: bfloat16 [8192, 256], P('node'), may hold values from -6 to 6
Outputs:
- layer_output: bfloat16 [8192, 256], P('node')
- grad_self_one: float32 [1024, 256], P('feat')
- grad_neighbour_one: float32 [1024, 256], P('feat')
- grad_self_two: float32 [256, 256], replicated
- grad_neighbour_two: float32 [256, 256], replicated
Inputs may be any that keep to these rules, and one draw needn't show every extreme that they name: `send_counts`: at most 32 slots go from one partition to one owner; in every draw some owner receives 32 from every partition, and every partition fills 32 slots to some owner. `tile_blocks`: the 4 blocks of one owner are distinct.
All inputs are finite; a program needn't handle non-finite values.
Results may differ from a plain program's by a relative error of at most 0.006.
Values may be sent and summed in bfloat16 or wider, within the bound.
No kernel may reach another device: no remote copies, remote signals or barrier semaphores. Data moves between devices by JAX's collectives and lax.ppermute only.
A program may use at most 128 MiB of HBM per device.

v0:
```python
import jax
import jax.numpy as jnp
from jax import lax
from jax.sharding import PartitionSpec as P


def silu_slope(values):
    sigma = jax.nn.sigmoid(values)
    return sigma * (1.0 + values * (1.0 - sigma))


def pick_rows(table, row_ids):
    count = row_ids.shape[0]
    block = 512 if count % 512 == 0 else count
    local_ids = jnp.arange(table.shape[0], dtype=jnp.int32)

    def one_block(ids_block):
        selector = (ids_block[:, None] == local_ids[None, :]).astype(table.dtype)
        return jnp.dot(selector, table, preferred_element_type=jnp.float32).astype(table.dtype)

    picked = lax.map(one_block, row_ids.reshape(-1, block))
    return picked.reshape(count, table.shape[1])


def spread(tile_set, block_ids, row_count):
    block_rows = tile_set.shape[2]
    global_rows = jnp.arange(row_count, dtype=jnp.int32)
    inner = jnp.arange(block_rows, dtype=jnp.int32)
    placed = (
        block_rows * block_ids[:, None, None] + inner[None, :, None] == global_rows[None, None, :]
    ).astype(tile_set.dtype)
    return jnp.einsum("ktb,kbr->tr", tile_set, placed, preferred_element_type=jnp.float32).astype(
        tile_set.dtype
    )


def shards(
    node_features,
    self_one,
    neighbour_one,
    sample_ids,
    dest_slots,
    send_counts,
    self_ids,
    tile_blocks,
    tile_weights,
    self_two,
    neighbour_two,
    out_grad,
):
    groups = lax.axis_size("node")
    device = lax.axis_index("node")
    sampled = sample_ids[0]
    targets_of = dest_slots[0]
    capacity = sampled.shape[1]
    targets = self_ids.shape[1]
    hidden = neighbour_one.shape[1]
    slot_ids = jnp.arange(capacity, dtype=jnp.int32)
    target_ids = jnp.arange(targets, dtype=jnp.int32)
    sent_counts = lax.dynamic_index_in_dim(send_counts, device, 0, keepdims=False)
    came_counts = lax.dynamic_index_in_dim(send_counts, device, 1, keepdims=False)
    sent_valid = slot_ids[None, :] < sent_counts[:, None]
    feature_rows = pick_rows(node_features, sampled.reshape(-1))
    partials = jnp.dot(feature_rows, neighbour_one, preferred_element_type=jnp.float32)
    partials = (
        (partials * sent_valid.reshape(-1, 1).astype(jnp.float32))
        .astype(jnp.bfloat16)
        .reshape(groups, capacity, hidden)
    )
    received, received_slots = (
        lax.all_to_all(partials, "node", split_axis=0, concat_axis=0, tiled=True),
        lax.all_to_all(targets_of, "node", split_axis=0, concat_axis=0, tiled=True),
    )
    came_valid = slot_ids[None, :] < came_counts[:, None]
    selector = (
        ((received_slots[None, :, :] == target_ids[:, None, None]) & came_valid[None, :, :])
        .astype(jnp.bfloat16)
        .reshape(targets, -1)
    )
    summed = jnp.dot(selector, received.reshape(-1, hidden), preferred_element_type=jnp.float32)
    degree = jnp.sum(selector, axis=1, dtype=jnp.float32)
    self_rows = pick_rows(node_features, self_ids[0])
    local_sum = (
        jnp.dot(self_rows, self_one, preferred_element_type=jnp.float32)
        + summed / (degree + 1.0)[:, None]
    )
    pre_one = lax.psum(local_sum, "feat")
    hidden_one = jax.nn.silu(pre_one).astype(jnp.bfloat16)
    block_ids = tile_blocks[0]
    tile_set = tile_weights[0]
    shard_rows = lax.all_gather(hidden_one, "node", axis=0, tiled=True)
    weights_here = spread(tile_set, block_ids, shard_rows.shape[0])
    agg_two = jnp.dot(weights_here, shard_rows, preferred_element_type=jnp.float32)
    agg_round = agg_two.astype(jnp.bfloat16)
    layer_output = (
        jnp.dot(hidden_one, self_two, preferred_element_type=jnp.float32)
        + jnp.dot(agg_round, neighbour_two, preferred_element_type=jnp.float32)
    ).astype(jnp.bfloat16)
    upper_self = jnp.einsum("rh,rk->hk", hidden_one, out_grad, preferred_element_type=jnp.float32)
    upper_others = jnp.einsum("rh,rk->hk", agg_round, out_grad, preferred_element_type=jnp.float32)
    agg_grad = jnp.einsum(
        "rk,hk->rh", out_grad, neighbour_two, preferred_element_type=jnp.float32
    ).astype(jnp.bfloat16)
    self_grad = jnp.einsum("rk,hk->rh", out_grad, self_two, preferred_element_type=jnp.float32)
    weights_all = spread(tile_set, block_ids, groups * targets)
    owner_terms = jnp.einsum(
        "tc,th->ch", weights_all, agg_grad, preferred_element_type=jnp.float32
    ).reshape(groups, targets, hidden)
    returned_terms = lax.all_to_all(owner_terms, "node", split_axis=0, concat_axis=0, tiled=True)
    row_grads = jnp.sum(returned_terms, axis=0)
    pre_grad = (self_grad + row_grads) * silu_slope(pre_one)
    pre_round = pre_grad.astype(jnp.bfloat16)
    mean_grad = (pre_grad / (degree + 1.0)[:, None]).astype(jnp.bfloat16)
    lower_self = jnp.einsum("rs,rh->sh", self_rows, pre_round, preferred_element_type=jnp.float32)
    slot_back = (
        jnp.einsum("tm,th->mh", selector, mean_grad, preferred_element_type=jnp.float32)
        .astype(jnp.bfloat16)
        .reshape(groups, capacity, hidden)
    )
    returned = lax.all_to_all(slot_back, "node", split_axis=0, concat_axis=0, tiled=True)
    grads_rows = returned.reshape(-1, hidden)
    lower_others = jnp.einsum(
        "ms,mh->sh", feature_rows, grads_rows, preferred_element_type=jnp.float32
    )
    upper_self, upper_others, lower_self, lower_others = lax.psum(
        (upper_self, upper_others, lower_self, lower_others), "node"
    )
    return (layer_output, lower_self, lower_others, upper_self, upper_others)


def solution(mesh):
    placed = (
        P("node", "feat"),
        P("feat", None),
        P("feat", None),
        P("node", None, None),
        P("node", None, None),
        P(),
        P("node", None),
        P("node", None),
        P("node", None, None, None),
        P(),
        P(),
        P("node", None),
    )
    return jax.shard_map(
        shards,
        mesh=mesh,
        in_specs=placed,
        out_specs=(P("node", None), P("feat", None), P("feat", None), P(), P()),
        check_vma=False,
    )
```

profile of v0, /device:TPU:1, one launch (start us, length us, event | category | flops | bytes accessed | tf_op | source)
XLA Modules:
  0.0 841.7 jit_solution(12990057395159653233)
XLA Ops:
  7.2 0.0 copy-start
  7.2 0.0 copy-start.9
  7.2 1.5 copy.26
  8.6 19.1 %all-to-all-start = ((s32[64,1,32]{2,1,0:T(1,128)}), s32[64,1,32]{2,1,0:T(1,128)S(1)}, u32[]{:S(2)}, u32[]{:S(2)}) async-start(s32[64,1,32]{2,1,0:T(1,128)} %bitcast.1), calls=%async_computation | async-start | bytes 65536 | tf_op jit(solution)/shard_map/all_to_all | solution.py:72
  27.8 0.9 dynamic-slice_reduce_fusion
  28.7 0.7 dynamic-slice_bitcast_fusion
  29.4 0.8 copy.28
  30.2 0.1 reshape_reshape_squeeze.3
  30.3 5.4 while.3
  30.3 1.3 fusion.61
  31.7 1.3 fusion.61
  33.0 1.3 fusion.61
  34.4 1.3 fusion.61
  35.7 0.1 lt.70
  35.8 0.1 lt.75
  35.9 0.1 lt.76
  35.9 0.1 lt.72
  36.0 0.1 lt.73
  36.1 2.3 fusion.9
  38.4 2.5 all-to-all-done
  41.0 12.0 %all-to-all-start.1 = ((bf16[64,32,256]{2,1,0:T(8,128)(2,1)}), bf16[64,32,256]{2,1,0:T(8,128)(2,1)S(1)}, u32[]{:S(2)}, u32[]{:S(2)}) async-start(bf16[64,32,256]{2,1,0:T(8,128)(2,1)} %bitcast.5), calls=%async_computation.1 | async-start | bytes 2097152 | tf_op jit(solution)/shard_map/all_to_all | solution.py:71
  53.1 0.1 iota_add_fusion
  53.1 3.7 fusion.7
  56.8 4.7 fusion.13
  61.5 41.3 %all-to-all-done.1 = bf16[64,32,256]{2,1,0:T(8,128)(2,1)S(1)} async-done(((bf16[64,32,256]{2,1,0:T(8,128)(2,1)}), bf16[64,32,256]{2,1,0:T(8,128)(2,1)S(1)}, u32[]{:S(2)}, u32[]{:S(2)}) %all-to-all-start.1) | async-done | bytes 1048608 | tf_op jit(solution)/shard_map/all_to_all | solution.py:71
  102.8 11.1 %all-to-all-start.2 = ((f32[64,128,256]{2,1,0:T(8,128)}), f32[64,128,256]{2,1,0:T(8,128)}, u32[]{:S(2)}, u32[]{:S(2)}) async-start(f32[64,128,256]{2,1,0:T(8,128)} %bitcast.60), calls=%async_computation.2 | async-start | bytes 16777216 | tf_op jit(solution)/shard_map/all_to_all | solution.py:109
  113.9 0.0 all-reduce.4.cloned.1.call-start
  113.9 0.0 copy-done.10
  113.9 1.1 convolution_convert_fusion.4
  115.1 0.1 copy.27
  115.1 0.5 broadcast.68
  115.7 0.7 reduce.5
  116.4 0.1 eq.90
  116.5 0.3 convert_reduce_fusion
  116.7 1.4 fusion.12
  118.2 0.8 convolution_add_fusion.2
  119.0 0.0 all-reduce.4.cloned.1.call-update
  119.0 0.0 all-gather.2.cloned.1.call-start
  119.0 76.8 %all-reduce.4.cloned.1.call-done = f32[128,256]{1,0:T(8,128)} async-done(((f32[128,256]{1,0:T(8,128)}), f32[128,256]{1,0:T(8,128)}) %all-reduce.4.cloned.1.call-update) | async-done | bytes 131088 | tf_op jit(solution)/shard_map/psum | solution.py:87
  195.8 1.6 multiply_convert_fusion
  197.4 0.0 all-gather.2.cloned.1.call-update
  197.4 0.0 copy-start.5
  197.4 0.0 copy-start.2
  197.4 308.6 %all-to-all-done.2 = f32[64,128,256]{2,1,0:T(8,128)} async-done(((f32[64,128,256]{2,1,0:T(8,128)}), f32[64,128,256]{2,1,0:T(8,128)}, u32[]{:S(2)}, u32[]{:S(2)}) %all-to-all-start.2) | async-done | bytes 8388640 | tf_op jit(solution)/shard_map/all_to_all | solution.py:109
  506.0 3.9 reduce_sum.19
  509.9 0.0 copy-done.5
  509.9 0.2 fusion.10
  510.2 1.5 convolution_convert_fusion.1
  511.7 8.5 %all-to-all-start.3 = ((bf16[64,32,256]{2,1,0:T(8,128)(2,1)}), bf16[64,32,256]{2,1,0:T(8,128)(2,1)S(1)}, u32[]{:S(2)}, u32[]{:S(2)}) async-start(bf16[64,32,256]{2,1,0:T(8,128)(2,1)} %bitcast.64), calls=%async_computation.3 | async-start | bytes 2097152 | tf_op jit(solution)/shard_map/all_to_all | solution.py:120
  520.1 0.0 all-reduce.6.cloned.1.call-start
  520.2 0.9 fusion.32
  521.1 3.2 convolution_convert_fusion.2
  524.3 0.9 fusion.33
  525.2 0.9 fusion.26
  526.1 43.3 %all-to-all-done.3 = bf16[64,32,256]{2,1,0:T(8,128)(2,1)S(1)} async-done(((bf16[64,32,256]{2,1,0:T(8,128)(2,1)}), bf16[64,32,256]{2,1,0:T(8,128)(2,1)S(1)}, u32[]{:S(2)}, u32[]{:S(2)}) %all-to-all-start.3) | async-done | bytes 1048608 | tf_op jit(solution)/shard_map/all_to_all | solution.py:120
  569.4 2.0 fusion.31
  571.5 0.0 all-reduce.6.cloned.1.call-update
  571.5 1.1 fusion.30
  572.6 0.8 fusion.11
  573.4 255.3 %all-reduce.6.cloned.1.call-done = (f32[128,256]{1,0:T(8,128)}, f32[128,256]{1,0:T(8,128)}, f32[256,256]{1,0:T(8,128)}, f32[256,256]{1,0:T(8,128)}) async-done(((f32[128,256]{1,0:T(8,128)}, f32[128,256]{1,0:T(8,128)}, f32[256,256]{1,0:T(8,128)}, f32[256,256]{1,0:T(8,128)}), (f32[128,256]{1,0:T(8,128)}, f32[128,256]{1,0:T(8,128)}, f32[256,256]{1,0:T(8,128)}, ...) | async-done | bytes 786448 | tf_op jit(solution)/shard_map/psum | solution.py:125
  828.7 1.6 copy.44
  830.3 1.6 copy.45
  831.8 1.7 copy.46
  833.5 1.7 copy.47
  (27 shorter events, 0.1 us)
Async XLA Ops:
  7.2 49.6 %copy-start = (bf16[256,256]{1,0:T(8,128)(2,1)S(1)}, bf16[256,256]{1,0:T(8,128)(2,1)}, u32[]{:S(2)}) copy-start(bf16[256,256]{1,0:T(8,128)(2,1)} %param.24) | copy-start | bytes 393220
  7.2 45.8 %copy-start.9 = (s32[1,4]{1,0:T(1,128)S(1)}, s32[1,4]{1,0:T(1,128)}, u32[]{:S(2)}) copy-start(s32[1,4]{1,0:T(1,128)} %param.21) | copy-start | bytes 52
  8.6 32.3 %all-to-all-start = ((s32[64,1,32]{2,1,0:T(1,128)}), s32[64,1,32]{2,1,0:T(1,128)S(1)}, u32[]{:S(2)}, u32[]{:S(2)}) async-start(s32[64,1,32]{2,1,0:T(1,128)} %bitcast.1), calls=%async_computation | async-start | bytes 65536 | tf_op jit(solution)/shard_map/all_to_all | solution.py:72
  35.7 17.4 %copy-start.1 = (bf16[4,512,128]{2,1,0:T(8,128)(2,1)}, bf16[4,512,128]{2,1,0:T(8,128)(2,1)S(1)}, u32[]{:S(2)}) copy-start(bf16[4,512,128]{2,1,0:T(8,128)(2,1)S(1)} %get-tuple-element.47) | copy-start | bytes 1572868
  41.0 61.8 %all-to-all-start.1 = ((bf16[64,32,256]{2,1,0:T(8,128)(2,1)}), bf16[64,32,256]{2,1,0:T(8,128)(2,1)S(1)}, u32[]{:S(2)}, u32[]{:S(2)}) async-start(bf16[64,32,256]{2,1,0:T(8,128)(2,1)} %bitcast.5), calls=%async_computation.1 | async-start | bytes 2097152 | tf_op jit(solution)/shard_map/all_to_all | solution.py:71
  53.1 3.7 copy-start.3
  102.8 11.2 %copy-start.10 = (s32[1,128]{1,0:T(1,128)S(1)}, s32[1,128]{1,0:T(1,128)}, u32[]{:S(2)}) copy-start(s32[1,128]{1,0:T(1,128)} %param.20) | copy-start | bytes 1540
  102.8 15.4 %copy-start.8 = (bf16[128,256]{1,0:T(8,128)(2,1)S(1)}, bf16[128,256]{1,0:T(8,128)(2,1)}, u32[]{:S(2)}) copy-start(bf16[128,256]{1,0:T(8,128)(2,1)} %param.15) | copy-start | bytes 196612
  102.8 403.3 %all-to-all-start.2 = ((f32[64,128,256]{2,1,0:T(8,128)}), f32[64,128,256]{2,1,0:T(8,128)}, u32[]{:S(2)}, u32[]{:S(2)}) async-start(f32[64,128,256]{2,1,0:T(8,128)} %bitcast.60), calls=%async_computation.2 | async-start | bytes 16777216 | tf_op jit(solution)/shard_map/all_to_all | solution.py:109
  113.9 81.9 %all-reduce.4.cloned.1.call-start = ((), (), s32[]{:S(2)}) async-start(), calls=%async_computation.4 | async-start | bytes 262144 | tf_op jit(solution)/shard_map/psum | solution.py:87
  119.0 402.1 %all-gather.2.cloned.1.call-start = ((), (), s32[]{:S(2)}) async-start(), calls=%async_computation.5 | async-start | bytes 4259840 | tf_op jit(solution)/shard_map/all_gather | solution.py:91
  197.4 312.5 %copy-start.4 = (f32[128,256]{1,0:T(8,128)S(1)}, f32[128,256]{1,0:T(8,128)}, u32[]{:S(2)}) copy-start(f32[128,256]{1,0:T(8,128)} %all-reduce.4.cloned.1.call-done) | copy-start | bytes 393220
  197.4 312.5 %copy-start.5 = (bf16[256,256]{1,0:T(8,128)(2,1)S(1)}, bf16[256,256]{1,0:T(8,128)(2,1)}, u32[]{:S(2)}) copy-start(bf16[256,256]{1,0:T(8,128)(2,1)} %param.23) | copy-start | bytes 393220
  197.4 322.8 %copy-start.2 = (bf16[128,256]{1,0:T(8,128)(2,1)S(1)}, bf16[128,256]{1,0:T(8,128)(2,1)}, u32[]{:S(2)}) copy-start(bf16[128,256]{1,0:T(8,128)(2,1)} %multiply_convert_fusion) | copy-start | bytes 196612
  510.2 1.5 copy-start.6
  511.7 57.8 %all-to-all-start.3 = ((bf16[64,32,256]{2,1,0:T(8,128)(2,1)}), bf16[64,32,256]{2,1,0:T(8,128)(2,1)S(1)}, u32[]{:S(2)}, u32[]{:S(2)}) async-start(bf16[64,32,256]{2,1,0:T(8,128)(2,1)} %bitcast.64), calls=%async_computation.3 | async-start | bytes 2097152 | tf_op jit(solution)/shard_map/all_to_all | solution.py:120
  520.1 308.5 %all-reduce.6.cloned.1.call-start = ((), (), s32[]{:S(2)}) async-start(), calls=%async_computation.6 | async-start | bytes 1572864 | tf_op jit(solution)/shard_map/psum | solution.py:125
  521.1 4.1 copy-start.7
Sparse Core Ops, SparseCore 0:
  119.1 76.6 all-reduce.3
  199.7 249.5 all-gather.1
  571.6 257.0 all-reduce.5
where the time goes:
time: 852 us; the launch traced here: 842 us
  waiting for transfers between devices  728 us (85%)
  starting transfers between devices  50.8 us (6%)
  matrix products  30.8 us (4%)
  between operations  14 us (2%)
  local copies, waits for them, and re-layouts  11.6 us (1%)
    all_to_all x1, waiting for transfers between devices, shards(): lax.all_to_all(owner_terms, 'node', split_axis=0, concat_axis=0, tiled=True)  309 us
    psum x1, waiting for transfers between devices, shards(): lax.psum((upper_self, upper_others, lower_self, lower_others), 'node')  255 us
    psum x1, waiting for transfers between devices, shards(): pre_one = lax.psum(local_sum, 'feat')  76.8 us
    all_to_all x1, waiting for transfers between devices, shards(): lax.all_to_all(slot_back, 'node', split_axis=0, concat_axis=0, tiled=True)  43.3 us
    all_to_all x1, waiting for transfers between devices, shards(): lax.all_to_all(partials, 'node', split_axis=0, concat_axis=0, tiled=True)  41.3 us
    all_to_all x1, starting transfers between devices, shards(): lax.all_to_all(targets_of, 'node', split_axis=0, concat_axis=0, tiled=True)  19.1 us
  transfers between devices with their start and end apart: 7, of which 6 were waited for; matrix products, arithmetic and copies ran while one was open for 5% of the time, Pallas kernels for 0%

commit v1 on v0

v1 whole, which is shorter than its diff:
```python
import jax
import jax.numpy as jnp
from jax import lax
from jax.sharding import PartitionSpec as P

bf16 = jnp.bfloat16
f32 = jnp.float32


def dot(a, b, dims):
    return lax.dot_general(a, b, (dims, ((), ())), preferred_element_type=f32)


def exchange(values, axis, groups=None):
    return lax.all_to_all(
        values, axis, split_axis=0, concat_axis=0, tiled=True, axis_index_groups=groups
    )


def to_all(values, count):
    return jnp.broadcast_to(values[None], (count,) + values.shape)


def pick(table, row_ids):
    local_ids = jnp.arange(table.shape[0], dtype=jnp.int32)
    chosen = (row_ids[:, None] == local_ids[None, :]).astype(table.dtype)
    return dot(chosen, table, ((1,), (0,))).astype(table.dtype)


def shards(
    features,
    self_one,
    neighbour_one,
    sample_ids,
    dest_slots,
    send_counts,
    self_ids,
    tile_blocks,
    tile_weights,
    self_two,
    neighbour_two,
    out_grad,
):
    feats = lax.axis_size("feat")
    nodes = lax.axis_size("node")
    nx = 4
    nz = nodes // nx
    along_x = [[x * nz + z for x in range(nx)] for z in range(nz)]
    along_z = [[x * nz + z for z in range(nz)] for x in range(nx)]
    device = lax.axis_index("node")
    feat = lax.axis_index("feat")
    x_at, z_at = device // nz, device % nz
    capacity = sample_ids.shape[2]
    targets = self_ids.shape[1]
    width = features.shape[1]
    hidden = neighbour_one.shape[1]
    part = hidden // feats
    block_ids = tile_blocks[0]
    tiles = tile_weights[0]

    sent_counts = lax.dynamic_index_in_dim(send_counts, device, 0, keepdims=False)
    used = jnp.arange(capacity, dtype=jnp.int32)[None, :] < sent_counts[:, None]
    slots = jnp.where(used, dest_slots[0], targets).astype(bf16)
    slot_rows = jnp.pad(slots[:, None, :], ((0, 0), (0, 7), (0, width - capacity)))
    rows = pick(features, sample_ids[0].reshape(-1)).reshape(nodes, capacity, width)
    came = exchange(jnp.concatenate([rows, slot_rows], axis=1), "node")
    came_rows = came[:, :capacity].reshape(-1, width)
    came_slots = came[:, capacity, :capacity].reshape(-1).astype(jnp.int32)

    grad_t = lax.dynamic_slice_in_dim(out_grad.T, feat * part, part, 0)
    terms = jnp.einsum("kt,ntb->nkb", grad_t, tiles, preferred_element_type=f32)
    here = block_ids[None, :] == jnp.arange(nodes, dtype=jnp.int32)[:, None]
    placed = sum(
        jnp.where(here[:, n, None, None], terms[n][None], 0.0) for n in range(tiles.shape[0])
    ).astype(bf16)
    placed = exchange(placed, "node", along_x).reshape((nx, nz) + placed.shape[1:])
    placed = exchange(jnp.sum(placed.astype(f32), axis=0).astype(bf16), "node", along_z)
    back_part = jnp.sum(placed.astype(f32), axis=0).astype(bf16)
    back_t = exchange(to_all(back_part, feats), "feat").reshape(hidden, targets)

    self_rows = pick(features, self_ids[0])
    chosen = came_slots[None, :] == jnp.arange(targets, dtype=jnp.int32)[:, None]
    degree = jnp.sum(chosen.astype(f32), axis=1)
    summed = dot(chosen.astype(bf16), came_rows, ((1,), (0,)))
    mean = summed / (degree + 1.0)[:, None]
    mean_high = mean.astype(bf16)
    mean_low = (mean - mean_high.astype(f32)).astype(bf16)
    terms_one = (
        dot(self_one, self_rows, ((0,), (1,)))
        + dot(neighbour_one, mean_high, ((0,), (1,)))
        + dot(neighbour_one, mean_low, ((0,), (1,)))
    )
    pre_one = jnp.sum(exchange(terms_one.reshape(feats, part, targets), "feat"), axis=0)
    sigma = jax.nn.sigmoid(pre_one)
    hidden_part = (pre_one * sigma).astype(bf16)
    slope = sigma * (1.0 + pre_one * (1.0 - sigma))

    self_two_part = lax.dynamic_slice_in_dim(self_two, feat * part, part, 0)
    neighbour_two_part = lax.dynamic_slice_in_dim(neighbour_two, feat * part, part, 0)
    pre_grad = (
        dot(self_two_part, out_grad, ((1,), (1,))) + dot(neighbour_two_part, back_t, ((1,), (0,)))
    ) * slope
    full = exchange(
        to_all(jnp.concatenate([pre_grad.astype(bf16), hidden_part], axis=0), feats), "feat"
    )
    pre_round = full[:, :part].reshape(hidden, targets)
    hidden_t = full[:, part:].reshape(hidden, targets)

    upper_self = dot(hidden_part, out_grad, ((1,), (0,)))
    upper_others = dot(hidden_part, back_t, ((1,), (1,)))
    half = hidden // 2
    upper = jnp.concatenate(
        [upper_self[:, :half], upper_self[:, half:], upper_others[:, :half], upper_others[:, half:]],
        axis=0,
    ).astype(bf16)
    share = upper.shape[0] // nz
    sent = jnp.concatenate([to_all(hidden_part, nz), upper.reshape(nz, share, half)], axis=1)
    got = exchange(sent, "node", along_z)
    upper_sum = jnp.sum(got[:, part:].astype(f32), axis=0).astype(bf16)
    column = jnp.concatenate([got[:, :part].reshape(nz * part, targets), upper_sum], axis=0)
    got = exchange(to_all(column, nx), "node", along_x)
    upper_sum = jnp.sum(got[:, nz * part :].astype(f32), axis=0).astype(bf16)
    all_hidden = got[:, : nz * part].reshape(nodes, part, targets)
    agg_part = sum(
        dot(lax.dynamic_index_in_dim(all_hidden, block_ids[n], 0, keepdims=False), tiles[n], ((1,), (1,)))
        for n in range(tiles.shape[0])
    ).astype(bf16)
    got = exchange(to_all(jnp.concatenate([agg_part, upper_sum], axis=0), feats), "feat")
    agg_t = got[:, :part].reshape(hidden, targets)
    upper_parts = got[:, part:]
    layer_output = (
        dot(hidden_t, self_two, ((0,), (0,))) + dot(agg_t, neighbour_two, ((0,), (0,)))
    ).astype(bf16)

    lower_self = dot(self_rows, pre_round, ((0,), (1,)))
    lower_others = dot(mean_high, pre_round, ((0,), (1,)))
    lower = jnp.concatenate(
        [lower_self[:, :half], lower_self[:, half:], lower_others[:, :half], lower_others[:, half:]],
        axis=0,
    ).astype(bf16)
    rows_each = lower.shape[0] // nodes
    got = exchange(lower.reshape(nodes, rows_each, half), "node")
    lower_sum = jnp.sum(got.astype(f32), axis=0).astype(bf16)
    each = feats // nx
    mine = lax.dynamic_slice_in_dim(upper_parts, x_at * each, each, 0).reshape(each * share, half)
    got = exchange(to_all(jnp.concatenate([lower_sum, mine], axis=0), nodes), "node")
    lower = got[:, :rows_each].reshape(4, width, half).astype(f32)
    upper = got[:, rows_each:].reshape(nx, nz, each, share, half)
    upper = upper.transpose(0, 2, 1, 3, 4).reshape(feats, 4, part, half).astype(f32)
    upper = upper.transpose(1, 0, 2, 3).reshape(4, hidden, half)

    def halves(stack, which):
        return jnp.concatenate([stack[2 * which], stack[2 * which + 1]], axis=1)

    return (layer_output, halves(lower, 0), halves(lower, 1), halves(upper, 0), halves(upper, 1))


def solution(mesh):
    placed = (
        P("node", "feat"),
        P("feat", None),
        P("feat", None),
        P("node", None, None),
        P("node", None, None),
        P(),
        P("node", None),
        P("node", None),
        P("node", None, None, None),
        P(),
        P(),
        P("node", None),
    )
    return jax.shard_map(
        shards,
        mesh=mesh,
        in_specs=placed,
        out_specs=(P("node", None), P("feat", None), P("feat", None), P(), P()),
        check_vma=False,
    )
```

time: 852 us -> 221 us (0.26)
  waiting for transfers between devices: 728 us -> 111 us
  starting transfers between devices: 50.8 us -> 76.8 us
  matrix products: 30.8 us -> 5.73 us
    psum x2 -> x0, waiting for transfers between devices: 332 us -> none  [the longest x1 255 us: shards(): lax.psum((upper_self, upper_others, lower_self, lower_others), 'node')]
    all_to_all x4 -> x11, waiting for transfers between devices: 396 us -> 111 us  [exchange(): lax.all_to_all(values, axis, split_axis=0, concat_axis=0, tiled=True, axi...]
    all_to_all x4 -> x11, starting transfers between devices: 50.7 us -> 76.8 us  [exchange(): lax.all_to_all(values, axis, split_axis=0, concat_axis=0, tiled=True, axi...]
    dot_general x19, matrix products: 30.8 us -> 5.73 us  [the longest x18 4.53 us: dot(): return lax.dot_general(a, b, (dims, ((), ())), preferred_element_type=f32)]
  transfers between devices with their start and end apart: 7 -> 11, of which waited for: 6 -> 11; matrix products, arithmetic and copies ran while one was open for 5% -> 5% of each run, Pallas kernels for 0% -> 0%
where the time goes in v1:
time: 221 us; the launch traced here: 218 us
  waiting for transfers between devices  111 us (50%)
  starting transfers between devices  76.8 us (35%)
  between operations  8.74 us (4%)
  other arithmetic  8.48 us (4%)
  local copies, waits for them, and re-layouts  6.88 us (3%)
  matrix products  5.73 us (3%)
    all_to_all x11, waiting for transfers between devices, exchange(): lax.all_to_all(values, axis, split_axis=0, concat_axis=0, tiled=True, axi...  111 us
    all_to_all x11, starting transfers between devices, exchange(): lax.all_to_all(values, axis, split_axis=0, concat_axis=0, tiled=True, axi...  76.8 us
    dot_general x18, matrix products, dot(): return lax.dot_general(a, b, (dims, ((), ())), preferred_element_type=f32)  4.53 us
  transfers between devices with their start and end apart: 11, of which 11 were waited for; matrix products, arithmetic and copies ran while one was open for 5% of the time, Pallas kernels for 0%

profile of v1, /device:TPU:1, one launch (start us, length us, event | category | flops | bytes accessed | tf_op | source)
XLA Modules:
  0.0 217.7 jit_solution(12637080601864495851)
XLA Ops:
  0.7 1.2 convolution_bitcast_fusion
  1.9 0.7 iota_compare_fusion.9
  2.6 1.3 add_convert_fusion
  3.9 5.0 %all-to-all-start = ((bf16[64,32,128]{2,1,0:T(8,128)(2,1)}), bf16[64,32,128]{2,1,0:T(8,128)(2,1)S(1)}, u32[]{:S(2)}, u32[]{:S(2)}) async-start(bf16[64,32,128]{2,1,0:T(8,128)(2,1)} %add_convert_fusion), calls=%async_computation | async-start | bytes 1048576 | tf_op jit(solution)/shard_map/all_to_all | solution.py:15
  8.9 0.7 fusion.44
  9.6 0.1 fusion.13
  9.8 0.1 copy.30
  10.0 1.0 fusion.1
  11.0 0.9 fusion.9
  11.9 3.9 %all-to-all-done = bf16[64,32,128]{2,1,0:T(8,128)(2,1)S(1)} async-done(((bf16[64,32,128]{2,1,0:T(8,128)(2,1)}), bf16[64,32,128]{2,1,0:T(8,128)(2,1)S(1)}, u32[]{:S(2)}, u32[]{:S(2)}) %all-to-all-start) | async-done | bytes 524320 | tf_op jit(solution)/shard_map/all_to_all | solution.py:15
  15.8 17.8 %all-to-all-start.3 = ((bf16[64,40,128]{2,1,0:T(8,128)(2,1)}), bf16[64,40,128]{2,1,0:T(8,128)(2,1)S(1)}, u32[]{:S(2)}, u32[]{:S(2)}) async-start(bf16[64,40,128]{2,1,0:T(8,128)(2,1)} %fusion.9), calls=%async_computation.3 | async-start | bytes 1310720 | tf_op jit(solution)/shard_map/all_to_all | solution.py:15
  33.6 0.2 convolution_convert_fusion.2
  33.8 0.1 fusion.55
  34.0 0.8 reduce_sum.78
  34.7 32.2 %all-to-all-done.3 = bf16[64,40,128]{2,1,0:T(8,128)(2,1)S(1)} async-done(((bf16[64,40,128]{2,1,0:T(8,128)(2,1)}), bf16[64,40,128]{2,1,0:T(8,128)(2,1)S(1)}, u32[]{:S(2)}, u32[]{:S(2)}) %all-to-all-start.3) | async-done | bytes 655392 | tf_op jit(solution)/shard_map/all_to_all | solution.py:15
  66.9 6.6 %all-to-all-start.1 = ((bf16[16,32,128]{2,1,0:T(8,128)(2,1)}), bf16[16,32,128]{2,1,0:T(8,128)(2,1)S(1)}, u32[]{:S(2)}, u32[]{:S(2)}) async-start(bf16[16,32,128]{2,1,0:T(8,128)(2,1)} %reduce_sum.78), calls=%async_computation.1 | async-start | bytes 262144 | tf_op jit(solution)/shard_map/all_to_all | solution.py:15
  73.5 0.1 fusion.14
  73.7 0.2 convert_reduce_fusion
  73.9 0.3 convolution_divide_fusion
  74.2 0.5 copy-done.3
  74.7 0.1 convolution_add_fusion.2
  74.9 0.2 fusion.4
  75.1 0.8 copy.32
  75.8 9.6 %all-to-all-done.1 = bf16[16,32,128]{2,1,0:T(8,128)(2,1)S(1)} async-done(((bf16[16,32,128]{2,1,0:T(8,128)(2,1)}), bf16[16,32,128]{2,1,0:T(8,128)(2,1)S(1)}, u32[]{:S(2)}, u32[]{:S(2)}) %all-to-all-start.1) | async-done | bytes 131104 | tf_op jit(solution)/shard_map/all_to_all | solution.py:15
  85.4 9.4 %all-to-all-start.4 = ((f32[8,32,128]{2,1,0:T(8,128)}), f32[8,32,128]{2,1,0:T(8,128)S(1)}, u32[]{:S(2)}, u32[]{:S(2)}) async-start(f32[8,32,128]{2,1,0:T(8,128)} %bitcast.20), calls=%async_computation.4 | async-start | bytes 262144 | tf_op jit(solution)/shard_map/all_to_all | solution.py:15
  94.9 0.1 fusion.27
  95.0 5.1 %all-to-all-done.4 = f32[8,32,128]{2,1,0:T(8,128)S(1)} async-done(((f32[8,32,128]{2,1,0:T(8,128)}), f32[8,32,128]{2,1,0:T(8,128)S(1)}, u32[]{:S(2)}, u32[]{:S(2)}) %all-to-all-start.4) | async-done | bytes 131104 | tf_op jit(solution)/shard_map/all_to_all | solution.py:15
  100.1 0.6 broadcast_in_dim.135
  100.8 4.1 %all-to-all-start.2 = ((bf16[8,32,128]{2,1,0:T(8,128)(2,1)}), bf16[8,32,128]{2,1,0:T(8,128)(2,1)S(1)}, u32[]{:S(2)}, u32[]{:S(2)}) async-start(bf16[8,32,128]{2,1,0:T(8,128)(2,1)} %broadcast_in_dim.135), calls=%async_computation.2 | async-start | bytes 131072 | tf_op jit(solution)/shard_map/all_to_all | solution.py:15
  104.9 0.1 convolution_convert_fusion.4
  105.0 4.7 %all-to-all-done.2 = bf16[8,32,128]{2,1,0:T(8,128)(2,1)S(1)} async-done(((bf16[8,32,128]{2,1,0:T(8,128)(2,1)}), bf16[8,32,128]{2,1,0:T(8,128)(2,1)S(1)}, u32[]{:S(2)}, u32[]{:S(2)}) %all-to-all-start.2) | async-done | bytes 65568 | tf_op jit(solution)/shard_map/all_to_all | solution.py:15
  109.8 0.1 convolution_convert_fusion.3
  109.9 0.2 fusion.7
  110.0 0.7 broadcast_in_dim.137
  110.7 4.1 %all-to-all-start.5 = ((bf16[8,64,128]{2,1,0:T(8,128)(2,1)}), bf16[8,64,128]{2,1,0:T(8,128)(2,1)S(1)}, u32[]{:S(2)}, u32[]{:S(2)}) async-start(bf16[8,64,128]{2,1,0:T(8,128)(2,1)} %broadcast_in_dim.137), calls=%async_computation.5 | async-start | bytes 262144 | tf_op jit(solution)/shard_map/all_to_all | solution.py:15
  114.8 0.7 pad_maximum_fusion.2
  115.5 4.6 %all-to-all-done.5 = bf16[8,64,128]{2,1,0:T(8,128)(2,1)S(1)} async-done(((bf16[8,64,128]{2,1,0:T(8,128)(2,1)}), bf16[8,64,128]{2,1,0:T(8,128)(2,1)S(1)}, u32[]{:S(2)}, u32[]{:S(2)}) %all-to-all-start.5) | async-done | bytes 131104 | tf_op jit(solution)/shard_map/all_to_all | solution.py:15
  120.1 3.7 %all-to-all-start.6 = ((bf16[16,40,128]{2,1,0:T(8,128)(2,1)}), bf16[16,40,128]{2,1,0:T(8,128)(2,1)S(1)}, u32[]{:S(2)}, u32[]{:S(2)}) async-start(bf16[16,40,128]{2,1,0:T(8,128)(2,1)} %pad_maximum_fusion.2), calls=%async_computation.6 | async-start | bytes 327680 | tf_op jit(solution)/shard_map/all_to_all | solution.py:15
  123.8 0.6 fusion.54
  132.1 0.2 convolution_convert_fusion
  132.3 3.6 %all-to-all-done.6 = bf16[16,40,128]{2,1,0:T(8,128)(2,1)S(1)} async-done(((bf16[16,40,128]{2,1,0:T(8,128)(2,1)}), bf16[16,40,128]{2,1,0:T(8,128)(2,1)S(1)}, u32[]{:S(2)}, u32[]{:S(2)}) %all-to-all-start.6) | async-done | bytes 163872 | tf_op jit(solution)/shard_map/all_to_all | solution.py:15
  136.0 0.9 broadcast_in_dim.139
  136.9 3.5 %all-to-all-start.7 = ((bf16[4,520,128]{2,1,0:T(8,128)(2,1)}), bf16[4,520,128]{2,1,0:T(8,128)(2,1)S(1)}, u32[]{:S(2)}, u32[]{:S(2)}) async-start(bf16[4,520,128]{2,1,0:T(8,128)(2,1)} %broadcast_in_dim.139), calls=%async_computation.7 | async-start | bytes 1064960 | tf_op jit(solution)/shard_map/all_to_all | solution.py:15
  140.4 0.2 convolution_convert_fusion.1
  140.6 0.7 maximum_bitcast_fusion
  141.3 6.0 %all-to-all-done.7 = bf16[4,520,128]{2,1,0:T(8,128)(2,1)S(1)} async-done(((bf16[4,520,128]{2,1,0:T(8,128)(2,1)}), bf16[4,520,128]{2,1,0:T(8,128)(2,1)S(1)}, u32[]{:S(2)}, u32[]{:S(2)}) %all-to-all-start.7) | async-done | bytes 532512 | tf_op jit(solution)/shard_map/all_to_all | solution.py:15
  147.3 10.8 %all-to-all-start.9 = ((bf16[64,8,128]{2,1,0:T(8,128)(2,1)}), bf16[64,8,128]{2,1,0:T(8,128)(2,1)S(1)}, u32[]{:S(2)}, u32[]{:S(2)}) async-start(bf16[64,8,128]{2,1,0:T(8,128)(2,1)} %maximum_bitcast_fusion), calls=%async_computation.9 | async-start | bytes 262144 | tf_op jit(solution)/shard_map/all_to_all | solution.py:15
  158.2 0.1 fusion.19
  158.3 0.1 convolution_add_fusion.5
  158.5 0.2 convolution_add_fusion.4
  158.6 0.2 fusion.8
  158.8 13.3 %all-to-all-done.9 = bf16[64,8,128]{2,1,0:T(8,128)(2,1)S(1)} async-done(((bf16[64,8,128]{2,1,0:T(8,128)(2,1)}), bf16[64,8,128]{2,1,0:T(8,128)(2,1)S(1)}, u32[]{:S(2)}, u32[]{:S(2)}) %all-to-all-start.9) | async-done | bytes 131104 | tf_op jit(solution)/shard_map/all_to_all | solution.py:15
  172.1 0.6 broadcast_in_dim.140
  172.7 6.9 %all-to-all-start.8 = ((bf16[8,40,128]{2,1,0:T(8,128)(2,1)}), bf16[8,40,128]{2,1,0:T(8,128)(2,1)S(1)}, u32[]{:S(2)}, u32[]{:S(2)}) async-start(bf16[8,40,128]{2,1,0:T(8,128)(2,1)} %broadcast_in_dim.140), calls=%async_computation.8 | async-start | bytes 163840 | tf_op jit(solution)/shard_map/all_to_all | solution.py:15
  179.7 4.9 %all-to-all-done.8 = bf16[8,40,128]{2,1,0:T(8,128)(2,1)S(1)} async-done(((bf16[8,40,128]{2,1,0:T(8,128)(2,1)}), bf16[8,40,128]{2,1,0:T(8,128)(2,1)S(1)}, u32[]{:S(2)}, u32[]{:S(2)}) %all-to-all-start.8) | async-done | bytes 81952 | tf_op jit(solution)/shard_map/all_to_all | solution.py:15
  184.6 0.8 broadcast_in_dim.141
  185.4 5.1 %all-to-all-start.10 = ((bf16[64,24,128]{2,1,0:T(8,128)(2,1)}), bf16[64,24,128]{2,1,0:T(8,128)(2,1)S(1)}, u32[]{:S(2)}, u32[]{:S(2)}) async-start(bf16[64,24,128]{2,1,0:T(8,128)(2,1)} %broadcast_in_dim.141), calls=%async_computation.10 | async-start | bytes 786432 | tf_op jit(solution)/shard_map/all_to_all | solution.py:15
  190.5 0.2 fusion.56
  190.7 0.8 fusion.5
  191.5 23.2 %all-to-all-done.10 = bf16[64,24,128]{2,1,0:T(8,128)(2,1)S(1)} async-done(((bf16[64,24,128]{2,1,0:T(8,128)(2,1)}), bf16[64,24,128]{2,1,0:T(8,128)(2,1)S(1)}, u32[]{:S(2)}, u32[]{:S(2)}) %all-to-all-start.10) | async-done | bytes 393248 | tf_op jit(solution)/shard_map/all_to_all | solution.py:15
  215.0 0.7 pad_maximum_fusion.4
  215.6 0.7 pad_maximum_fusion.5
  216.3 0.7 pad_maximum_fusion
  217.0 0.7 pad_maximum_fusion.1
  (54 shorter events, 0.8 us)
Async XLA Ops:
  0.6 9.3 %copy-start = (bf16[512,128]{1,0:T(8,128)(2,1)S(1)}, bf16[512,128]{1,0:T(8,128)(2,1)}, u32[]{:S(2)}) copy-start(bf16[512,128]{1,0:T(8,128)(2,1)} %param.12) | copy-start | bytes 393220
  3.9 5.0 %copy-start.7 = (s32[1,64,32]{1,2,0:T(8,128)S(1)}, s32[1,64,32]{1,2,0:T(8,128)}, u32[]{:S(2)}) copy-start(s32[1,64,32]{1,2,0:T(8,128)} %param.16) | copy-start | bytes 24580
  3.9 5.9 %copy-start.8 = (s32[1,64,32]{1,2,0:T(8,128)S(1)}, s32[1,64,32]{1,2,0:T(8,128)}, u32[]{:S(2)}) copy-start(s32[1,64,32]{1,2,0:T(8,128)} %param.15) | copy-start | bytes 24580
  3.9 11.9 %all-to-all-start = ((bf16[64,32,128]{2,1,0:T(8,128)(2,1)}), bf16[64,32,128]{2,1,0:T(8,128)(2,1)S(1)}, u32[]{:S(2)}, u32[]{:S(2)}) async-start(bf16[64,32,128]{2,1,0:T(8,128)(2,1)} %add_convert_fusion), calls=%async_computation | async-start | bytes 1048576 | tf_op jit(solution)/shard_map/all_to_all | solution.py:15
  11.9 21.7 %copy-start.10 = (s32[1,128]{1,0:T(1,128)S(1)}, s32[1,128]{1,0:T(1,128)}, u32[]{:S(2)}) copy-start(s32[1,128]{1,0:T(1,128)} %param.18) | copy-start | bytes 1540
  11.9 21.9 %copy-start.6 = (bf16[128,256]{1,0:T(8,128)(2,1)S(1)}, bf16[128,256]{1,0:T(8,128)(2,1)}, u32[]{:S(2)}) copy-start(bf16[128,256]{1,0:T(8,128)(2,1)} %param.13) | copy-start | bytes 196612
  15.8 51.1 %all-to-all-start.3 = ((bf16[64,40,128]{2,1,0:T(8,128)(2,1)}), bf16[64,40,128]{2,1,0:T(8,128)(2,1)S(1)}, u32[]{:S(2)}, u32[]{:S(2)}) async-start(bf16[64,40,128]{2,1,0:T(8,128)(2,1)} %fusion.9), calls=%async_computation.3 | async-start | bytes 1310720 | tf_op jit(solution)/shard_map/all_to_all | solution.py:15
  66.9 18.5 %all-to-all-start.1 = ((bf16[16,32,128]{2,1,0:T(8,128)(2,1)}), bf16[16,32,128]{2,1,0:T(8,128)(2,1)S(1)}, u32[]{:S(2)}, u32[]{:S(2)}) async-start(bf16[16,32,128]{2,1,0:T(8,128)(2,1)} %reduce_sum.78), calls=%async_computation.1 | async-start | bytes 262144 | tf_op jit(solution)/shard_map/all_to_all | solution.py:15
  73.9 0.8 copy-start.3
  74.7 20.1 %copy-start.2 = (bf16[128,256]{1,0:T(8,128)(2,1)S(1)}, bf16[128,256]{1,0:T(8,128)(2,1)}, u32[]{:S(2)}) copy-start(bf16[128,256]{1,0:T(8,128)(2,1)} %param.23) | copy-start | bytes 196612
  74.7 20.1 %copy-start.4 = (bf16[256,256]{1,0:T(8,128)(2,1)S(1)}, bf16[256,256]{1,0:T(8,128)(2,1)}, u32[]{:S(2)}) copy-start(bf16[256,256]{1,0:T(8,128)(2,1)} %param.21) | copy-start | bytes 393220
  75.1 34.8 %copy-start.5 = (bf16[256,256]{1,0:T(8,128)(2,1)S(1)}, bf16[256,256]{1,0:T(8,128)(2,1)}, u32[]{:S(2)}) copy-start(bf16[256,256]{1,0:T(8,128)(2,1)} %param.22) | copy-start | bytes 393220
  85.4 14.7 %all-to-all-start.4 = ((f32[8,32,128]{2,1,0:T(8,128)}), f32[8,32,128]{2,1,0:T(8,128)S(1)}, u32[]{:S(2)}, u32[]{:S(2)}) async-start(f32[8,32,128]{2,1,0:T(8,128)} %bitcast.20), calls=%async_computation.4 | async-start | bytes 262144 | tf_op jit(solution)/shard_map/all_to_all | solution.py:15
  100.8 9.0 %all-to-all-start.2 = ((bf16[8,32,128]{2,1,0:T(8,128)(2,1)}), bf16[8,32,128]{2,1,0:T(8,128)(2,1)S(1)}, u32[]{:S(2)}, u32[]{:S(2)}) async-start(bf16[8,32,128]{2,1,0:T(8,128)(2,1)} %broadcast_in_dim.135), calls=%async_computation.2 | async-start | bytes 131072 | tf_op jit(solution)/shard_map/all_to_all | solution.py:15
  110.0 13.7 %copy-start.9 = (s32[1,4]{1,0:T(1,128)S(1)}, s32[1,4]{1,0:T(1,128)}, u32[]{:S(2)}) copy-start(s32[1,4]{1,0:T(1,128)} %param.19) | copy-start | bytes 52
  110.7 9.3 %all-to-all-start.5 = ((bf16[8,64,128]{2,1,0:T(8,128)(2,1)}), bf16[8,64,128]{2,1,0:T(8,128)(2,1)S(1)}, u32[]{:S(2)}, u32[]{:S(2)}) async-start(bf16[8,64,128]{2,1,0:T(8,128)(2,1)} %broadcast_in_dim.137), calls=%async_computation.5 | async-start | bytes 262144 | tf_op jit(solution)/shard_map/all_to_all | solution.py:15
  120.1 15.9 %all-to-all-start.6 = ((bf16[16,40,128]{2,1,0:T(8,128)(2,1)}), bf16[16,40,128]{2,1,0:T(8,128)(2,1)S(1)}, u32[]{:S(2)}, u32[]{:S(2)}) async-start(bf16[16,40,128]{2,1,0:T(8,128)(2,1)} %pad_maximum_fusion.2), calls=%async_computation.6 | async-start | bytes 327680 | tf_op jit(solution)/shard_map/all_to_all | solution.py:15
  136.9 10.4 %all-to-all-start.7 = ((bf16[4,520,128]{2,1,0:T(8,128)(2,1)}), bf16[4,520,128]{2,1,0:T(8,128)(2,1)S(1)}, u32[]{:S(2)}, u32[]{:S(2)}) async-start(bf16[4,520,128]{2,1,0:T(8,128)(2,1)} %broadcast_in_dim.139), calls=%async_computation.7 | async-start | bytes 1064960 | tf_op jit(solution)/shard_map/all_to_all | solution.py:15
  141.3 16.9 %copy-start.1 = (bf16[1,4,128,128]{3,2,1,0:T(8,128)(2,1)S(1)}, bf16[1,4,128,128]{3,2,1,0:T(8,128)(2,1)}, u32[]{:S(2)}) copy-start(bf16[1,4,128,128]{3,2,1,0:T(8,128)(2,1)} %param.20) | copy-start | bytes 393220
  147.3 24.8 %all-to-all-start.9 = ((bf16[64,8,128]{2,1,0:T(8,128)(2,1)}), bf16[64,8,128]{2,1,0:T(8,128)(2,1)S(1)}, u32[]{:S(2)}, u32[]{:S(2)}) async-start(bf16[64,8,128]{2,1,0:T(8,128)(2,1)} %maximum_bitcast_fusion), calls=%async_computation.9 | async-start | bytes 262144 | tf_op jit(solution)/shard_map/all_to_all | solution.py:15
  172.7 11.8 %all-to-all-start.8 = ((bf16[8,40,128]{2,1,0:T(8,128)(2,1)}), bf16[8,40,128]{2,1,0:T(8,128)(2,1)S(1)}, u32[]{:S(2)}, u32[]{:S(2)}) async-start(bf16[8,40,128]{2,1,0:T(8,128)(2,1)} %broadcast_in_dim.140), calls=%async_computation.8 | async-start | bytes 163840 | tf_op jit(solution)/shard_map/all_to_all | solution.py:15
  185.4 29.4 %all-to-all-start.10 = ((bf16[64,24,128]{2,1,0:T(8,128)(2,1)}), bf16[64,24,128]{2,1,0:T(8,128)(2,1)S(1)}, u32[]{:S(2)}, u32[]{:S(2)}) async-start(bf16[64,24,128]{2,1,0:T(8,128)(2,1)} %broadcast_in_dim.141), calls=%async_computation.10 | async-start | bytes 786432 | tf_op jit(solution)/shard_map/all_to_all | solution.py:15

commit v2 on v1

v2 whole, which is shorter than its diff:
```python
import jax
import jax.numpy as jnp
from jax import lax
from jax.sharding import PartitionSpec as P

bf16 = jnp.bfloat16
f32 = jnp.float32


def dot(a, b, dims):
    return lax.dot_general(a, b, (dims, ((), ())), preferred_element_type=f32)


def exchange(values, axis, groups=None):
    return lax.all_to_all(
        values, axis, split_axis=0, concat_axis=0, tiled=True, axis_index_groups=groups
    )


def to_all(values, count):
    return jnp.broadcast_to(values[None], (count,) + values.shape)


def pick(table, row_ids):
    local_ids = jnp.arange(table.shape[0], dtype=jnp.int32)
    chosen = (row_ids[:, None] == local_ids[None, :]).astype(table.dtype)
    return dot(chosen, table, ((1,), (0,))).astype(table.dtype)


def split(values):
    high = values.astype(bf16)
    return high, (values - high.astype(f32)).astype(bf16)


def quarters(first, second):
    half = first.shape[1] // 2
    parts = [first[:, :half], first[:, half:], second[:, :half], second[:, half:]]
    return jnp.concatenate(parts, axis=0).astype(bf16)


def shards(
    features,
    self_one,
    neighbour_one,
    sample_ids,
    dest_slots,
    send_counts,
    self_ids,
    tile_blocks,
    tile_weights,
    self_two,
    neighbour_two,
    out_grad,
):
    feats = lax.axis_size("feat")
    nodes = lax.axis_size("node")
    nx = 4
    nz = nodes // nx
    along_x = [[x * nz + z for x in range(nx)] for z in range(nz)]
    along_z = [[x * nz + z for z in range(nz)] for x in range(nx)]
    device = lax.axis_index("node")
    feat = lax.axis_index("feat")
    capacity = sample_ids.shape[2]
    targets = self_ids.shape[1]
    width = features.shape[1]
    hidden = neighbour_one.shape[1]
    part = hidden // feats
    block_ids = tile_blocks[0]
    tiles = tile_weights[0]

    sent_counts = lax.dynamic_index_in_dim(send_counts, device, 0, keepdims=False)
    used = jnp.arange(capacity, dtype=jnp.int32)[None, :] < sent_counts[:, None]
    slots = jnp.where(used, dest_slots[0], targets).astype(bf16)
    slot_rows = jnp.pad(slots[:, None, :], ((0, 0), (0, 7), (0, width - capacity)))
    rows = pick(features, sample_ids[0].reshape(-1)).reshape(nodes, capacity, width)

    grad_t = lax.dynamic_slice_in_dim(out_grad.T, feat * part, part, 0)
    terms = jnp.einsum("kt,ntb->nkb", grad_t, tiles, preferred_element_type=f32)
    here = block_ids[None, :] == jnp.arange(nodes, dtype=jnp.int32)[:, None]
    placed = sum(
        jnp.where(here[:, n, None, None], terms[n][None], 0.0) for n in range(tiles.shape[0])
    ).astype(bf16)
    came = exchange(jnp.concatenate([rows, placed, slot_rows], axis=1), "node")
    came_rows = came[:, :capacity].reshape(-1, width)
    came_slots = came[:, capacity + part, :capacity].reshape(-1).astype(jnp.int32)
    back_part = jnp.sum(came[:, capacity : capacity + part].astype(f32), axis=0).astype(bf16)

    self_rows = pick(features, self_ids[0])
    chosen = came_slots[None, :] == jnp.arange(targets, dtype=jnp.int32)[:, None]
    degree = jnp.sum(chosen.astype(f32), axis=1)
    summed = dot(chosen.astype(bf16), came_rows, ((1,), (0,)))
    mean = summed / (degree + 1.0)[:, None]
    mean_high, mean_low = split(mean)
    terms_one = (
        dot(self_one, self_rows, ((0,), (1,)))
        + dot(neighbour_one, mean_high, ((0,), (1,)))
        + dot(neighbour_one, mean_low, ((0,), (1,)))
    )
    high, low = split(terms_one.reshape(feats, part, targets))
    got = exchange(jnp.concatenate([high, low, to_all(back_part, feats)], axis=1), "feat")
    pre_one = jnp.sum(got[:, :part].astype(f32) + got[:, part : 2 * part].astype(f32), axis=0)
    back_t = got[:, 2 * part :].reshape(hidden, targets)
    sigma = jax.nn.sigmoid(pre_one)
    hidden_part = (pre_one * sigma).astype(bf16)
    slope = sigma * (1.0 + pre_one * (1.0 - sigma))

    self_two_part = lax.dynamic_slice_in_dim(self_two, feat * part, part, 0)
    neighbour_two_part = lax.dynamic_slice_in_dim(neighbour_two, feat * part, part, 0)
    pre_grad = (
        dot(self_two_part, out_grad, ((1,), (1,))) + dot(neighbour_two_part, back_t, ((1,), (0,)))
    ) * slope
    full = exchange(
        to_all(jnp.concatenate([pre_grad.astype(bf16), hidden_part], axis=0), feats), "feat"
    )
    pre_round = full[:, :part].reshape(hidden, targets)
    hidden_t = full[:, part:].reshape(hidden, targets)

    half = hidden // 2
    upper = quarters(
        dot(hidden_part, out_grad, ((1,), (0,))), dot(hidden_part, back_t, ((1,), (1,)))
    )
    lower = quarters(
        dot(self_rows, pre_round, ((0,), (1,))), dot(mean_high, pre_round, ((0,), (1,)))
    )
    share = upper.shape[0] // nz
    rows_each = lower.shape[0] // nz
    sent = [to_all(hidden_part, nz), lower.reshape(nz, rows_each, half), upper.reshape(nz, share, half)]
    got = exchange(jnp.concatenate(sent, axis=1), "node", along_z)
    sums = split(jnp.sum(got[:, part:].astype(f32), axis=0))
    column = jnp.concatenate([got[:, :part].reshape(nz * part, targets), *sums], axis=0)
    got = exchange(to_all(column, nx), "node", along_x)
    all_hidden = got[:, : nz * part].reshape(nodes, part, targets)
    sums = got[:, nz * part :].reshape(2 * nx, rows_each + share, half).astype(f32)
    got = exchange(to_all(jnp.sum(sums, axis=0).astype(bf16), nz), "node", along_z)
    lower = got[:, :rows_each].reshape(4, width, half).astype(f32)

    agg_part = sum(
        dot(lax.dynamic_index_in_dim(all_hidden, block_ids[n], 0, keepdims=False), tiles[n], ((1,), (1,)))
        for n in range(tiles.shape[0])
    ).astype(bf16)
    upper = got[:, rows_each:].reshape(nz * share, half)
    got = exchange(to_all(jnp.concatenate([agg_part, upper], axis=0), feats), "feat")
    agg_t = got[:, :part].reshape(hidden, targets)
    layer_output = (
        dot(hidden_t, self_two, ((0,), (0,))) + dot(agg_t, neighbour_two, ((0,), (0,)))
    ).astype(bf16)
    upper = got[:, part:].reshape(feats, 4, part, half).astype(f32)
    upper = upper.transpose(1, 0, 2, 3).reshape(4, hidden, half)

    def halves(stack, which):
        return jnp.concatenate([stack[2 * which], stack[2 * which + 1]], axis=1)

    return (layer_output, halves(lower, 0), halves(lower, 1), halves(upper, 0), halves(upper, 1))


def solution(mesh):
    placed = (
        P("node", "feat"),
        P("feat", None),
        P("feat", None),
        P("node", None, None),
        P("node", None, None),
        P(),
        P("node", None),
        P("node", None),
        P("node", None, None, None),
        P(),
        P(),
        P("node", None),
    )
    return jax.shard_map(
        shards,
        mesh=mesh,
        in_specs=placed,
        out_specs=(P("node", None), P("feat", None), P("feat", None), P(), P()),
        check_vma=False,
    )
```

time: 221 us -> 188 us (0.85); the launches traced: 218 us -> 187 us
  waiting for transfers between devices: 111 us -> 83.5 us
  starting transfers between devices: 76.8 us -> 57.3 us
  blocking collectives: 0 us -> 18.5 us
    all_to_all x11 -> x6, waiting for transfers between devices: 111 us -> 83.5 us  [exchange(): lax.all_to_all(values, axis, split_axis=0, concat_axis=0, tiled=True, axi...]
    all_to_all x11 -> x6, starting transfers between devices: 76.8 us -> 57.3 us  [exchange(): lax.all_to_all(values, axis, split_axis=0, concat_axis=0, tiled=True, axi...]
    all_to_all x0 -> x1, blocking collectives: none -> 18.5 us  [exchange(): lax.all_to_all(values, axis, split_axis=0, concat_axis=0, tiled=True, axi...]
  transfers between devices with their start and end apart: 11 -> 6, of which waited for: 11 -> 5; matrix products, arithmetic and copies ran while one was open for 5% -> 2% of each run, Pallas kernels for 0% -> 0%
where the time goes in v2:
time: 188 us; the launch traced here: 187 us
  waiting for transfers between devices  83.5 us (44%)
  starting transfers between devices  57.3 us (30%)
  blocking collectives  18.5 us (10%)
  between operations  8.76 us (5%)
  local copies, waits for them, and re-layouts  6.82 us (4%)
  other arithmetic  6.76 us (4%)
  matrix products  5.76 us (3%)
    all_to_all x6, waiting for transfers between devices, exchange(): lax.all_to_all(values, axis, split_axis=0, concat_axis=0, tiled=True, axi...  83.5 us
    all_to_all x6, starting transfers between devices, exchange(): lax.all_to_all(values, axis, split_axis=0, concat_axis=0, tiled=True, axi...  57.3 us
    all_to_all x1, blocking collectives, exchange(): lax.all_to_all(values, axis, split_axis=0, concat_axis=0, tiled=True, axi...  18.5 us
    dot_general x18, matrix products, dot(): return lax.dot_general(a, b, (dims, ((), ())), preferred_element_type=f32)  4.55 us
  transfers between devices with their start and end apart: 6, of which 5 were waited for; matrix products, arithmetic and copies ran while one was open for 2% of the time, Pallas kernels for 0%

profile of v2, /device:TPU:1, one launch (start us, length us, event | category | flops | bytes accessed | tf_op | source)
XLA Modules:
  0.0 187.4 jit_solution(13152262940733435711)
XLA Ops:
  0.6 0.0 copy-start
  0.7 1.2 convolution_bitcast_fusion
  1.9 0.7 iota_compare_fusion.9
  2.6 0.8 copy.30
  3.4 0.8 copy.28
  4.2 0.1 eq.62
  4.3 0.7 fusion.44
  5.0 0.1 fusion.13
  5.1 0.0 copy-done
  5.1 1.1 fusion.1
  6.2 0.6 add_convert_fusion
  6.8 1.1 fusion.4
  7.9 19.2 %all-to-all-start = ((bf16[64,72,128]{2,1,0:T(8,128)(2,1)}), bf16[64,72,128]{2,1,0:T(8,128)(2,1)S(1)}, u32[]{:S(2)}, u32[]{:S(2)}) async-start(bf16[64,72,128]{2,1,0:T(8,128)(2,1)} %fusion.4), calls=%async_computation | async-start | bytes 2359296 | tf_op jit(solution)/shard_map/all_to_all | solution.py:15
  27.2 0.2 convolution_convert_fusion.2
  27.4 0.1 fusion.57
  27.6 55.2 %all-to-all-done = bf16[64,72,128]{2,1,0:T(8,128)(2,1)S(1)} async-done(((bf16[64,72,128]{2,1,0:T(8,128)(2,1)}), bf16[64,72,128]{2,1,0:T(8,128)(2,1)S(1)}, u32[]{:S(2)}, u32[]{:S(2)}) %all-to-all-start) | async-done | bytes 1179680 | tf_op jit(solution)/shard_map/all_to_all | solution.py:15
  82.7 0.1 fusion.14
  82.9 0.1 reshape.179
  82.9 0.2 convert_reduce_fusion
  83.1 0.0 copy-start.3
  83.1 0.2 fusion.48
  83.3 0.3 convolution_divide_fusion
  83.6 0.4 copy-done.3
  84.0 0.1 convolution_add_fusion.2
  84.1 0.0 copy-start.5
  84.1 0.1 fusion.5
  84.3 0.1 copy.31
  84.4 0.7 pad_maximum_fusion.3
  85.1 9.5 %all-to-all-start.1 = ((bf16[8,96,128]{2,1,0:T(8,128)(2,1)}), bf16[8,96,128]{2,1,0:T(8,128)(2,1)S(1)}, u32[]{:S(2)}, u32[]{:S(2)}) async-start(bf16[8,96,128]{2,1,0:T(8,128)(2,1)} %pad_maximum_fusion.3), calls=%async_computation.1 | async-start | bytes 393216 | tf_op jit(solution)/shard_map/all_to_all | solution.py:15
  94.6 0.0 copy-done.4
  94.6 0.1 fusion.27
  94.8 5.8 %all-to-all-done.1 = bf16[8,96,128]{2,1,0:T(8,128)(2,1)S(1)} async-done(((bf16[8,96,128]{2,1,0:T(8,128)(2,1)}), bf16[8,96,128]{2,1,0:T(8,128)(2,1)S(1)}, u32[]{:S(2)}, u32[]{:S(2)}) %all-to-all-start.1) | async-done | bytes 196640 | tf_op jit(solution)/shard_map/all_to_all | solution.py:15
  100.6 0.1 convolution_convert_fusion.4
  100.7 0.1 convolution_convert_fusion.3
  100.8 0.2 fusion.8
  101.0 0.7 broadcast_in_dim.137
  101.7 4.2 %all-to-all-start.2 = ((bf16[8,64,128]{2,1,0:T(8,128)(2,1)}), bf16[8,64,128]{2,1,0:T(8,128)(2,1)S(1)}, u32[]{:S(2)}, u32[]{:S(2)}) async-start(bf16[8,64,128]{2,1,0:T(8,128)(2,1)} %broadcast_in_dim.137), calls=%async_computation.2 | async-start | bytes 262144 | tf_op jit(solution)/shard_map/all_to_all | solution.py:15
  105.9 5.3 %all-to-all-done.2 = bf16[8,64,128]{2,1,0:T(8,128)(2,1)S(1)} async-done(((bf16[8,64,128]{2,1,0:T(8,128)(2,1)}), bf16[8,64,128]{2,1,0:T(8,128)(2,1)S(1)}, u32[]{:S(2)}, u32[]{:S(2)}) %all-to-all-start.2) | async-done | bytes 131104 | tf_op jit(solution)/shard_map/all_to_all | solution.py:15
  111.2 0.2 convolution_convert_fusion
  111.4 0.2 convolution_convert_fusion.1
  111.7 18.5 %all_to_all.35 = bf16[16,72,128]{2,1,0:T(8,128)(2,1)S(1)} all-to-all(bf16[16,72,128]{2,1,0:T(8,128)(2,1)S(1)} %pad_maximum_fusion), channel_id=1, replica_groups={{0,1,2,3,4,5,6,7,8,9,10,11,12,13,14,15},{16,17,18,19,20,21,22,23,24,25,..., dimensions={0} | all-to-all | bytes 589824 | tf_op jit(solution)/shard_map/all_to_all | solution.py:15
  130.3 0.0 copy-start.7
  130.3 0.9 broadcast_in_dim.139
  131.2 3.5 %all-to-all-start.4 = ((bf16[4,592,128]{2,1,0:T(8,128)(2,1)}), bf16[4,592,128]{2,1,0:T(8,128)(2,1)S(1)}, u32[]{:S(2)}, u32[]{:S(2)}) async-start(bf16[4,592,128]{2,1,0:T(8,128)(2,1)} %broadcast_in_dim.139), calls=%async_computation.4 | async-start | bytes 1212416 | tf_op jit(solution)/shard_map/all_to_all | solution.py:15
  134.7 0.0 copy-start.1
  134.8 0.6 fusion.56
  143.1 0.2 fusion.58
  143.3 0.0 all-to-all-done.4
  143.4 0.7 broadcast_in_dim.140
  144.0 13.0 %all-to-all-start.5 = ((bf16[16,40,128]{2,1,0:T(8,128)(2,1)}), bf16[16,40,128]{2,1,0:T(8,128)(2,1)S(1)}, u32[]{:S(2)}, u32[]{:S(2)}) async-start(bf16[16,40,128]{2,1,0:T(8,128)(2,1)} %broadcast_in_dim.140), calls=%async_computation.5 | async-start | bytes 327680 | tf_op jit(solution)/shard_map/all_to_all | solution.py:15
  157.1 0.1 fusion.19
  157.2 0.1 convolution_add_fusion.5
  157.4 0.2 convolution_add_fusion.4
  157.5 0.2 fusion.9
  157.7 11.5 %all-to-all-done.5 = bf16[16,40,128]{2,1,0:T(8,128)(2,1)S(1)} async-done(((bf16[16,40,128]{2,1,0:T(8,128)(2,1)}), bf16[16,40,128]{2,1,0:T(8,128)(2,1)S(1)}, u32[]{:S(2)}, u32[]{:S(2)}) %all-to-all-start.5) | async-done | bytes 163872 | tf_op jit(solution)/shard_map/all_to_all | solution.py:15
  169.2 0.8 broadcast_in_dim.141
  170.0 7.8 %all-to-all-start.6 = ((bf16[8,160,128]{2,1,0:T(8,128)(2,1)}), bf16[8,160,128]{2,1,0:T(8,128)(2,1)S(1)}, u32[]{:S(2)}, u32[]{:S(2)}) async-start(bf16[8,160,128]{2,1,0:T(8,128)(2,1)} %broadcast_in_dim.141), calls=%async_computation.6 | async-start | bytes 655360 | tf_op jit(solution)/shard_map/all_to_all | solution.py:15
  177.9 0.7 pad_maximum_fusion.7
  178.5 0.7 pad_maximum_fusion.6
  179.2 5.8 %all-to-all-done.6 = bf16[8,160,128]{2,1,0:T(8,128)(2,1)S(1)} async-done(((bf16[8,160,128]{2,1,0:T(8,128)(2,1)}), bf16[8,160,128]{2,1,0:T(8,128)(2,1)S(1)}, u32[]{:S(2)}, u32[]{:S(2)}) %all-to-all-start.6) | async-done | bytes 327712 | tf_op jit(solution)/shard_map/all_to_all | solution.py:15
  185.0 0.1 convert_bitcast_fusion
  185.1 0.7 pad_maximum_fusion.2
  185.8 0.7 pad_maximum_fusion.1
  186.5 0.8 fusion.6
  (40 shorter events, 0.5 us)
Async XLA Ops:
  0.6 4.5 %copy-start = (bf16[512,128]{1,0:T(8,128)(2,1)S(1)}, bf16[512,128]{1,0:T(8,128)(2,1)}, u32[]{:S(2)}) copy-start(bf16[512,128]{1,0:T(8,128)(2,1)} %param.12) | copy-start | bytes 393220
  7.9 19.3 %copy-start.8 = (s32[1,128]{1,0:T(1,128)S(1)}, s32[1,128]{1,0:T(1,128)}, u32[]{:S(2)}) copy-start(s32[1,128]{1,0:T(1,128)} %param.18) | copy-start | bytes 1540
  7.9 19.5 %copy-start.6 = (bf16[128,256]{1,0:T(8,128)(2,1)S(1)}, bf16[128,256]{1,0:T(8,128)(2,1)}, u32[]{:S(2)}) copy-start(bf16[128,256]{1,0:T(8,128)(2,1)} %param.13) | copy-start | bytes 196612
  7.9 74.8 %all-to-all-start = ((bf16[64,72,128]{2,1,0:T(8,128)(2,1)}), bf16[64,72,128]{2,1,0:T(8,128)(2,1)S(1)}, u32[]{:S(2)}, u32[]{:S(2)}) async-start(bf16[64,72,128]{2,1,0:T(8,128)(2,1)} %fusion.4), calls=%async_computation | async-start | bytes 2359296 | tf_op jit(solution)/shard_map/all_to_all | solution.py:15
  83.1 0.8 copy-start.3
  84.0 10.7 %copy-start.2 = (bf16[128,256]{1,0:T(8,128)(2,1)S(1)}, bf16[128,256]{1,0:T(8,128)(2,1)}, u32[]{:S(2)}) copy-start(bf16[128,256]{1,0:T(8,128)(2,1)} %param.23) | copy-start | bytes 196612
  84.0 10.7 %copy-start.4 = (bf16[256,256]{1,0:T(8,128)(2,1)S(1)}, bf16[256,256]{1,0:T(8,128)(2,1)}, u32[]{:S(2)}) copy-start(bf16[256,256]{1,0:T(8,128)(2,1)} %param.21) | copy-start | bytes 393220
  84.1 16.7 %copy-start.5 = (bf16[256,256]{1,0:T(8,128)(2,1)S(1)}, bf16[256,256]{1,0:T(8,128)(2,1)}, u32[]{:S(2)}) copy-start(bf16[256,256]{1,0:T(8,128)(2,1)} %param.22) | copy-start | bytes 393220
  85.1 15.4 %all-to-all-start.1 = ((bf16[8,96,128]{2,1,0:T(8,128)(2,1)}), bf16[8,96,128]{2,1,0:T(8,128)(2,1)S(1)}, u32[]{:S(2)}, u32[]{:S(2)}) async-start(bf16[8,96,128]{2,1,0:T(8,128)(2,1)} %pad_maximum_fusion.3), calls=%async_computation.1 | async-start | bytes 393216 | tf_op jit(solution)/shard_map/all_to_all | solution.py:15
  101.7 9.5 %all-to-all-start.2 = ((bf16[8,64,128]{2,1,0:T(8,128)(2,1)}), bf16[8,64,128]{2,1,0:T(8,128)(2,1)S(1)}, u32[]{:S(2)}, u32[]{:S(2)}) async-start(bf16[8,64,128]{2,1,0:T(8,128)(2,1)} %broadcast_in_dim.137), calls=%async_computation.2 | async-start | bytes 262144 | tf_op jit(solution)/shard_map/all_to_all | solution.py:15
  130.3 4.4 %copy-start.7 = (s32[1,4]{1,0:T(1,128)S(1)}, s32[1,4]{1,0:T(1,128)}, u32[]{:S(2)}) copy-start(s32[1,4]{1,0:T(1,128)} %param.19) | copy-start | bytes 52
  131.2 12.1 %all-to-all-start.4 = ((bf16[4,592,128]{2,1,0:T(8,128)(2,1)}), bf16[4,592,128]{2,1,0:T(8,128)(2,1)S(1)}, u32[]{:S(2)}, u32[]{:S(2)}) async-start(bf16[4,592,128]{2,1,0:T(8,128)(2,1)} %broadcast_in_dim.139), calls=%async_computation.4 | async-start | bytes 1212416 | tf_op jit(solution)/shard_map/all_to_all | solution.py:15
  134.7 22.4 %copy-start.1 = (bf16[1,4,128,128]{3,2,1,0:T(8,128)(2,1)S(1)}, bf16[1,4,128,128]{3,2,1,0:T(8,128)(2,1)}, u32[]{:S(2)}) copy-start(bf16[1,4,128,128]{3,2,1,0:T(8,128)(2,1)} %param.20) | copy-start | bytes 393220
  144.0 25.2 %all-to-all-start.5 = ((bf16[16,40,128]{2,1,0:T(8,128)(2,1)}), bf16[16,40,128]{2,1,0:T(8,128)(2,1)S(1)}, u32[]{:S(2)}, u32[]{:S(2)}) async-start(bf16[16,40,128]{2,1,0:T(8,128)(2,1)} %broadcast_in_dim.140), calls=%async_computation.5 | async-start | bytes 327680 | tf_op jit(solution)/shard_map/all_to_all | solution.py:15
  170.0 14.9 %all-to-all-start.6 = ((bf16[8,160,128]{2,1,0:T(8,128)(2,1)}), bf16[8,160,128]{2,1,0:T(8,128)(2,1)S(1)}, u32[]{:S(2)}, u32[]{:S(2)}) async-start(bf16[8,160,128]{2,1,0:T(8,128)(2,1)} %broadcast_in_dim.141), calls=%async_computation.6 | async-start | bytes 655360 | tf_op jit(solution)/shard_map/all_to_all | solution.py:15

commit v3 on v2

--- a/solution.py
+++ b/solution.py
@@ -28,8 +28,8 @@
 
 
 def split(values):
-    high = values.astype(bf16)
-    return high, (values - high.astype(f32)).astype(bf16)
+    high = lax.reduce_precision(values, 8, 7)
+    return high.astype(bf16), (values - high).astype(bf16)
 
 
 def quarters(first, second):
@@ -59,6 +59,7 @@
     along_x = [[x * nz + z for x in range(nx)] for z in range(nz)]
     along_z = [[x * nz + z for z in range(nz)] for x in range(nx)]
     device = lax.axis_index("node")
+    x_at = device // nz
     feat = lax.axis_index("feat")
     capacity = sample_ids.shape[2]
     targets = self_ids.shape[1]
@@ -70,25 +71,50 @@
 
     sent_counts = lax.dynamic_index_in_dim(send_counts, device, 0, keepdims=False)
     used = jnp.arange(capacity, dtype=jnp.int32)[None, :] < sent_counts[:, None]
-    slots = jnp.where(used, dest_slots[0], targets).astype(bf16)
-    slot_rows = jnp.pad(slots[:, None, :], ((0, 0), (0, 7), (0, width - capacity)))
-    rows = pick(features, sample_ids[0].reshape(-1)).reshape(nodes, capacity, width)
-
+    slots = jnp.tile(jnp.where(used, dest_slots[0], targets), (1, nx))
+    own_lanes = jnp.arange(nx * capacity, dtype=jnp.int32) // capacity == x_at
+    slots = jnp.where(own_lanes[None, :], slots, 0).astype(bf16)
+    rows = pick(features, sample_ids[0].reshape(-1))
     grad_t = lax.dynamic_slice_in_dim(out_grad.T, feat * part, part, 0)
-    terms = jnp.einsum("kt,ntb->nkb", grad_t, tiles, preferred_element_type=f32)
-    here = block_ids[None, :] == jnp.arange(nodes, dtype=jnp.int32)[:, None]
-    placed = sum(
-        jnp.where(here[:, n, None, None], terms[n][None], 0.0) for n in range(tiles.shape[0])
+    terms = jnp.einsum("kt,ntb->nkb", grad_t, tiles, preferred_element_type=f32).astype(bf16)
+    count = tiles.shape[0]
+    in_x = (block_ids // nz)[None, :] == jnp.arange(nx, dtype=jnp.int32)[:, None]
+    terms = jnp.where(in_x[:, :, None, None], terms[None], jnp.zeros((), bf16))
+    block_z = jnp.broadcast_to((block_ids % nz)[:, None], (count, targets)).astype(bf16)
+    sent = [
+        rows.reshape(nx, nz * capacity, width),
+        slots.reshape(nx, nz, width),
+        terms.reshape(nx, count * part, targets),
+        to_all(jnp.pad(block_z, ((0, 8 - count), (0, 0))), nx),
+    ]
+    got = exchange(jnp.concatenate(sent, axis=1), "node", along_x)
+
+    ends = [nz * capacity, nz * capacity + nz, nz * capacity + nz + count * part]
+    rows = got[:, : ends[0]].reshape(nx, nz, capacity, width).transpose(1, 0, 2, 3)
+    slots = jnp.sum(got[:, ends[0] : ends[1]].astype(f32), axis=0).astype(bf16)
+    terms = got[:, ends[1] : ends[2]].reshape(nx * count, part, targets).astype(f32)
+    block_z = got[:, ends[2] : ends[2] + count].reshape(nx * count, 1, targets).astype(jnp.int32)
+    z_ids = jnp.arange(nz, dtype=jnp.int32)[:, None, None]
+    terms = sum(
+        jnp.where(block_z[n][None] == z_ids, terms[n][None], 0.0) for n in range(nx * count)
     ).astype(bf16)
-    came = exchange(jnp.concatenate([rows, placed, slot_rows], axis=1), "node")
-    came_rows = came[:, :capacity].reshape(-1, width)
-    came_slots = came[:, capacity + part, :capacity].reshape(-1).astype(jnp.int32)
-    back_part = jnp.sum(came[:, capacity : capacity + part].astype(f32), axis=0).astype(bf16)
+    per_z = nx * capacity
+    sent = [
+        rows.reshape(nz, per_z, width),
+        terms,
+        jnp.pad(slots[:, None, :], ((0, 0), (0, 7), (0, 0))),
+    ]
+    came = exchange(jnp.concatenate(sent, axis=1), "node", along_z)
+    back_part = jnp.sum(came[:, per_z : per_z + part].astype(f32), axis=0).astype(bf16)
 
     self_rows = pick(features, self_ids[0])
-    chosen = came_slots[None, :] == jnp.arange(targets, dtype=jnp.int32)[:, None]
-    degree = jnp.sum(chosen.astype(f32), axis=1)
-    summed = dot(chosen.astype(bf16), came_rows, ((1,), (0,)))
+    came_slots = came[:, per_z + part].astype(jnp.int32)
+    target_ids = jnp.arange(targets, dtype=jnp.int32)
+    chosen = came_slots[:, None, :] == target_ids[None, :, None]
+    degree = jnp.sum(chosen.astype(f32), axis=(0, 2))
+    summed = jnp.einsum(
+        "ztr,zrs->ts", chosen.astype(bf16), came[:, :per_z], preferred_element_type=f32
+    )
     mean = summed / (degree + 1.0)[:, None]
     mean_high, mean_low = split(mean)
     terms_one = (

time: 188 us -> 177 us (0.941)
  waiting for transfers between devices: 83.5 us -> 56.2 us
  blocking collectives: 18.5 us -> 33.2 us
    all_to_all x6, waiting for transfers between devices: 83.5 us -> 56.2 us  [exchange(): lax.all_to_all(values, axis, split_axis=0, concat_axis=0, tiled=True, axi...]
    all_to_all x1 -> x2, blocking collectives: 18.5 us -> 33.2 us  [exchange(): lax.all_to_all(values, axis, split_axis=0, concat_axis=0, tiled=True, axi...]
    dot_general x18 -> x17, matrix products: 4.55 us -> 4.26 us  [dot(): return lax.dot_general(a, b, (dims, ((), ())), preferred_element_type=f32)]
where the time goes in v3:
time: 177 us; the launch traced here: 176 us
  starting transfers between devices  58 us (33%)
  waiting for transfers between devices  56.2 us (32%)
  blocking collectives  33.2 us (19%)
  between operations  8.94 us (5%)
  other arithmetic  8.08 us (5%)
  local copies, waits for them, and re-layouts  6.06 us (3%)
  matrix products  5.72 us (3%)
    all_to_all x6, starting transfers between devices, exchange(): lax.all_to_all(values, axis, split_axis=0, concat_axis=0, tiled=True, axi...  58 us
    all_to_all x6, waiting for transfers between devices, exchange(): lax.all_to_all(values, axis, split_axis=0, concat_axis=0, tiled=True, axi...  56.2 us
    all_to_all x2, blocking collectives, exchange(): lax.all_to_all(values, axis, split_axis=0, concat_axis=0, tiled=True, axi...  33.2 us
    dot_general x17, matrix products, dot(): return lax.dot_general(a, b, (dims, ((), ())), preferred_element_type=f32)  4.26 us
  transfers between devices with their start and end apart: 6, of which 5 were waited for; matrix products, arithmetic and copies ran while one was open for 2% of the time, Pallas kernels for 0%

profile of v3, /device:TPU:1, one launch (start us, length us, event | category | flops | bytes accessed | tf_op | source)
XLA Modules:
  0.0 176.2 jit_solution(13687055005407488241)
XLA Ops:
  0.6 0.0 copy-start
  0.7 0.7 fusion.53
  1.4 0.7 fusion.50
  2.0 0.1 broadcast_in_dim.324
  2.1 0.1 broadcast_in_dim.325
  2.2 0.7 fusion.51
  2.9 0.7 bitcast_select_fusion
  3.6 0.1 copy.27
  3.7 0.1 tile.10
  3.9 0.8 copy.26
  4.7 0.1 eq.403
  4.7 0.1 fusion.41
  4.8 1.2 convolution_convert_fusion.2
  6.0 0.1 broadcast_select_fusion
  6.2 1.1 fusion.1
  7.2 0.2 maximum_maximum_fusion
  7.4 12.4 %all_to_all.40 = bf16[4,664,128]{2,1,0:T(8,128)(2,1)S(1)} all-to-all(bf16[4,664,128]{2,1,0:T(8,128)(2,1)S(1)} %maximum_maximum_fusion), channel_id=1, replica_groups={{0,16,32,48},{1,17,33,49},{2,18,34,50},{3,19,35,51},{4,20,36,52},{5,21,..., dimensions={0} | all-to-all | bytes 1359872 | tf_op jit(solution)/shard_map/all_to_all | solution.py:15
  20.2 0.6 add_convert_fusion
  20.8 0.9 fusion.10
  21.7 17.4 %all-to-all-start.1 = ((bf16[16,168,128]{2,1,0:T(8,128)(2,1)}), bf16[16,168,128]{2,1,0:T(8,128)(2,1)S(1)}, u32[]{:S(2)}, u32[]{:S(2)}) async-start(bf16[16,168,128]{2,1,0:T(8,128)(2,1)} %fusion.10), calls=%async_computation.1 | async-start | bytes 1376256 | tf_op jit(solution)/shard_map/all_to_all | solution.py:15
  39.1 0.2 convolution_convert_fusion.3
  39.3 0.0 copy-start.3
  39.4 0.1 fusion.62
  39.5 27.9 %all-to-all-done.1 = bf16[16,168,128]{2,1,0:T(8,128)(2,1)S(1)} async-done(((bf16[16,168,128]{2,1,0:T(8,128)(2,1)}), bf16[16,168,128]{2,1,0:T(8,128)(2,1)S(1)}, u32[]{:S(2)}, u32[]{:S(2)}) %all-to-all-start.1) | async-done | bytes 688160 | tf_op jit(solution)/shard_map/all_to_all | solution.py:15
  67.4 0.2 convert_reduce_fusion
  67.6 0.3 fusion.6
  67.9 0.1 convolution_add_fusion.2
  68.0 0.1 fusion.4
  68.2 0.1 copy.31
  68.3 0.0 copy-start.2
  68.4 0.0 copy-start.5
  68.4 0.7 pad_maximum_fusion.3
  69.1 11.8 %all-to-all-start.2 = ((bf16[8,96,128]{2,1,0:T(8,128)(2,1)}), bf16[8,96,128]{2,1,0:T(8,128)(2,1)S(1)}, u32[]{:S(2)}, u32[]{:S(2)}) async-start(bf16[8,96,128]{2,1,0:T(8,128)(2,1)} %pad_maximum_fusion.3), calls=%async_computation.2 | async-start | bytes 393216 | tf_op jit(solution)/shard_map/all_to_all | solution.py:15
  80.9 0.1 fusion.31
  81.0 5.8 %all-to-all-done.2 = bf16[8,96,128]{2,1,0:T(8,128)(2,1)S(1)} async-done(((bf16[8,96,128]{2,1,0:T(8,128)(2,1)}), bf16[8,96,128]{2,1,0:T(8,128)(2,1)S(1)}, u32[]{:S(2)}, u32[]{:S(2)}) %all-to-all-start.2) | async-done | bytes 196640 | tf_op jit(solution)/shard_map/all_to_all | solution.py:15
  86.8 0.1 convolution_convert_fusion.5
  87.0 0.1 convolution_convert_fusion.4
  87.1 0.2 fusion.8
  87.3 0.7 broadcast_in_dim.382
  87.9 4.2 %all-to-all-start.3 = ((bf16[8,64,128]{2,1,0:T(8,128)(2,1)}), bf16[8,64,128]{2,1,0:T(8,128)(2,1)S(1)}, u32[]{:S(2)}, u32[]{:S(2)}) async-start(bf16[8,64,128]{2,1,0:T(8,128)(2,1)} %broadcast_in_dim.382), calls=%async_computation.3 | async-start | bytes 262144 | tf_op jit(solution)/shard_map/all_to_all | solution.py:15
  92.2 5.3 %all-to-all-done.3 = bf16[8,64,128]{2,1,0:T(8,128)(2,1)S(1)} async-done(((bf16[8,64,128]{2,1,0:T(8,128)(2,1)}), bf16[8,64,128]{2,1,0:T(8,128)(2,1)S(1)}, u32[]{:S(2)}, u32[]{:S(2)}) %all-to-all-start.3) | async-done | bytes 131104 | tf_op jit(solution)/shard_map/all_to_all | solution.py:15
  97.5 0.2 convolution_convert_fusion
  97.7 0.2 convolution_convert_fusion.1
  98.0 20.8 %all_to_all.41 = bf16[16,72,128]{2,1,0:T(8,128)(2,1)S(1)} all-to-all(bf16[16,72,128]{2,1,0:T(8,128)(2,1)S(1)} %pad_maximum_fusion), channel_id=1, replica_groups={{0,1,2,3,4,5,6,7,8,9,10,11,12,13,14,15},{16,17,18,19,20,21,22,23,24,25,..., dimensions={0} | all-to-all | bytes 589824 | tf_op jit(solution)/shard_map/all_to_all | solution.py:15
  118.9 0.9 broadcast_in_dim.384
  119.8 3.6 %all-to-all-start.5 = ((bf16[4,592,128]{2,1,0:T(8,128)(2,1)}), bf16[4,592,128]{2,1,0:T(8,128)(2,1)S(1)}, u32[]{:S(2)}, u32[]{:S(2)}) async-start(bf16[4,592,128]{2,1,0:T(8,128)(2,1)} %broadcast_in_dim.384), calls=%async_computation.5 | async-start | bytes 1212416 | tf_op jit(solution)/shard_map/all_to_all | solution.py:15
  123.4 0.6 fusion.61
  131.8 0.2 fusion.63
  132.0 0.7 broadcast_in_dim.385
  132.7 13.2 %all-to-all-start.6 = ((bf16[16,40,128]{2,1,0:T(8,128)(2,1)}), bf16[16,40,128]{2,1,0:T(8,128)(2,1)S(1)}, u32[]{:S(2)}, u32[]{:S(2)}) async-start(bf16[16,40,128]{2,1,0:T(8,128)(2,1)} %broadcast_in_dim.385), calls=%async_computation.6 | async-start | bytes 327680 | tf_op jit(solution)/shard_map/all_to_all | solution.py:15
  145.9 0.1 fusion.22
  146.1 0.1 convolution_add_fusion.5
  146.2 0.2 convolution_add_fusion.4
  146.4 0.2 fusion.9
  146.5 11.5 %all-to-all-done.6 = bf16[16,40,128]{2,1,0:T(8,128)(2,1)S(1)} async-done(((bf16[16,40,128]{2,1,0:T(8,128)(2,1)}), bf16[16,40,128]{2,1,0:T(8,128)(2,1)S(1)}, u32[]{:S(2)}, u32[]{:S(2)}) %all-to-all-start.6) | async-done | bytes 163872 | tf_op jit(solution)/shard_map/all_to_all | solution.py:15
  158.1 0.8 broadcast_in_dim.386
  158.8 7.8 %all-to-all-start.7 = ((bf16[8,160,128]{2,1,0:T(8,128)(2,1)}), bf16[8,160,128]{2,1,0:T(8,128)(2,1)S(1)}, u32[]{:S(2)}, u32[]{:S(2)}) async-start(bf16[8,160,128]{2,1,0:T(8,128)(2,1)} %broadcast_in_dim.386), calls=%async_computation.7 | async-start | bytes 655360 | tf_op jit(solution)/shard_map/all_to_all | solution.py:15
  166.7 0.7 pad_maximum_fusion.6
  167.3 0.7 pad_maximum_fusion.7
  168.0 5.8 %all-to-all-done.7 = bf16[8,160,128]{2,1,0:T(8,128)(2,1)S(1)} async-done(((bf16[8,160,128]{2,1,0:T(8,128)(2,1)}), bf16[8,160,128]{2,1,0:T(8,128)(2,1)S(1)}, u32[]{:S(2)}, u32[]{:S(2)}) %all-to-all-start.7) | async-done | bytes 327712 | tf_op jit(solution)/shard_map/all_to_all | solution.py:15
  173.8 0.1 convert_bitcast_fusion
  173.9 0.8 fusion.5
  174.7 0.7 pad_maximum_fusion.1
  175.5 0.7 pad_maximum_fusion.2
  (68 shorter events, 0.8 us)
Async XLA Ops:
  0.6 5.5 %copy-start = (bf16[512,128]{1,0:T(8,128)(2,1)S(1)}, bf16[512,128]{1,0:T(8,128)(2,1)}, u32[]{:S(2)}) copy-start(bf16[512,128]{1,0:T(8,128)(2,1)} %param.12) | copy-start | bytes 393220
  21.7 17.4 %copy-start.8 = (s32[1,128]{1,0:T(1,128)S(1)}, s32[1,128]{1,0:T(1,128)}, u32[]{:S(2)}) copy-start(s32[1,128]{1,0:T(1,128)} %param.18) | copy-start | bytes 1540
  21.7 17.6 %copy-start.6 = (bf16[128,256]{1,0:T(8,128)(2,1)S(1)}, bf16[128,256]{1,0:T(8,128)(2,1)}, u32[]{:S(2)}) copy-start(bf16[128,256]{1,0:T(8,128)(2,1)} %param.13) | copy-start | bytes 196612
  21.7 45.7 %all-to-all-start.1 = ((bf16[16,168,128]{2,1,0:T(8,128)(2,1)}), bf16[16,168,128]{2,1,0:T(8,128)(2,1)S(1)}, u32[]{:S(2)}, u32[]{:S(2)}) async-start(bf16[16,168,128]{2,1,0:T(8,128)(2,1)} %fusion.10), calls=%async_computation.1 | async-start | bytes 1376256 | tf_op jit(solution)/shard_map/all_to_all | solution.py:15
  39.3 28.5 %copy-start.3 = (bf16[128,256]{1,0:T(8,128)(2,1)S(1)}, bf16[128,256]{1,0:T(8,128)(2,1)}, u32[]{:S(2)}) copy-start(bf16[128,256]{1,0:T(8,128)(2,1)} %param.14) | copy-start | bytes 196612
  68.3 12.6 %copy-start.2 = (bf16[128,256]{1,0:T(8,128)(2,1)S(1)}, bf16[128,256]{1,0:T(8,128)(2,1)}, u32[]{:S(2)}) copy-start(bf16[128,256]{1,0:T(8,128)(2,1)} %param.23) | copy-start | bytes 196612
  68.3 12.6 %copy-start.4 = (bf16[256,256]{1,0:T(8,128)(2,1)S(1)}, bf16[256,256]{1,0:T(8,128)(2,1)}, u32[]{:S(2)}) copy-start(bf16[256,256]{1,0:T(8,128)(2,1)} %param.21) | copy-start | bytes 393220
  68.4 18.7 %copy-start.5 = (bf16[256,256]{1,0:T(8,128)(2,1)S(1)}, bf16[256,256]{1,0:T(8,128)(2,1)}, u32[]{:S(2)}) copy-start(bf16[256,256]{1,0:T(8,128)(2,1)} %param.22) | copy-start | bytes 393220
  69.1 17.7 %all-to-all-start.2 = ((bf16[8,96,128]{2,1,0:T(8,128)(2,1)}), bf16[8,96,128]{2,1,0:T(8,128)(2,1)S(1)}, u32[]{:S(2)}, u32[]{:S(2)}) async-start(bf16[8,96,128]{2,1,0:T(8,128)(2,1)} %pad_maximum_fusion.3), calls=%async_computation.2 | async-start | bytes 393216 | tf_op jit(solution)/shard_map/all_to_all | solution.py:15
  87.9 9.5 %all-to-all-start.3 = ((bf16[8,64,128]{2,1,0:T(8,128)(2,1)}), bf16[8,64,128]{2,1,0:T(8,128)(2,1)S(1)}, u32[]{:S(2)}, u32[]{:S(2)}) async-start(bf16[8,64,128]{2,1,0:T(8,128)(2,1)} %broadcast_in_dim.382), calls=%async_computation.3 | async-start | bytes 262144 | tf_op jit(solution)/shard_map/all_to_all | solution.py:15
  119.8 3.6 %copy-start.7 = (s32[1,4]{1,0:T(1,128)S(1)}, s32[1,4]{1,0:T(1,128)}, u32[]{:S(2)}) copy-start(s32[1,4]{1,0:T(1,128)} %param.19) | copy-start | bytes 52
  119.8 12.2 %all-to-all-start.5 = ((bf16[4,592,128]{2,1,0:T(8,128)(2,1)}), bf16[4,592,128]{2,1,0:T(8,128)(2,1)S(1)}, u32[]{:S(2)}, u32[]{:S(2)}) async-start(bf16[4,592,128]{2,1,0:T(8,128)(2,1)} %broadcast_in_dim.384), calls=%async_computation.5 | async-start | bytes 1212416 | tf_op jit(solution)/shard_map/all_to_all | solution.py:15
  132.7 13.2 %copy-start.1 = (bf16[1,4,128,128]{3,2,1,0:T(8,128)(2,1)S(1)}, bf16[1,4,128,128]{3,2,1,0:T(8,128)(2,1)}, u32[]{:S(2)}) copy-start(bf16[1,4,128,128]{3,2,1,0:T(8,128)(2,1)} %param.20) | copy-start | bytes 393220
  132.7 25.3 %all-to-all-start.6 = ((bf16[16,40,128]{2,1,0:T(8,128)(2,1)}), bf16[16,40,128]{2,1,0:T(8,128)(2,1)S(1)}, u32[]{:S(2)}, u32[]{:S(2)}) async-start(bf16[16,40,128]{2,1,0:T(8,128)(2,1)} %broadcast_in_dim.385), calls=%async_computation.6 | async-start | bytes 327680 | tf_op jit(solution)/shard_map/all_to_all | solution.py:15
  158.8 14.9 %all-to-all-start.7 = ((bf16[8,160,128]{2,1,0:T(8,128)(2,1)}), bf16[8,160,128]{2,1,0:T(8,128)(2,1)S(1)}, u32[]{:S(2)}, u32[]{:S(2)}) async-start(bf16[8,160,128]{2,1,0:T(8,128)(2,1)} %broadcast_in_dim.386), calls=%async_computation.7 | async-start | bytes 655360 | tf_op jit(solution)/shard_map/all_to_all | solution.py:15

commit v4 on v2

v4 whole, which is shorter than its diff:
```python
import jax
import jax.numpy as jnp
from jax import lax
from jax.sharding import PartitionSpec as P

bf16 = jnp.bfloat16
f32 = jnp.float32


def dot(a, b, dims):
    return lax.dot_general(a, b, (dims, ((), ())), preferred_element_type=f32)


def exchange(values, axis, groups=None):
    return lax.all_to_all(
        values, axis, split_axis=0, concat_axis=0, tiled=True, axis_index_groups=groups
    )


def to_all(values, count):
    return jnp.broadcast_to(values[None], (count,) + values.shape)


def pick(table, row_ids):
    local_ids = jnp.arange(table.shape[0], dtype=jnp.int32)
    chosen = (row_ids[:, None] == local_ids[None, :]).astype(table.dtype)
    return dot(chosen, table, ((1,), (0,))).astype(table.dtype)


def split(values):
    high = lax.reduce_precision(values, 8, 7)
    return high.astype(bf16), (values - high).astype(bf16)


def quarters(first, second):
    half = first.shape[1] // 2
    parts = [first[:, :half], first[:, half:], second[:, :half], second[:, half:]]
    return jnp.concatenate(parts, axis=0).astype(bf16)


def shards(
    features,
    self_one,
    neighbour_one,
    sample_ids,
    dest_slots,
    send_counts,
    self_ids,
    tile_blocks,
    tile_weights,
    self_two,
    neighbour_two,
    out_grad,
):
    feats = lax.axis_size("feat")
    nodes = lax.axis_size("node")
    nx, nb = 4, 2
    na = nodes // (nx * nb)
    near = nx * nb
    near_ids = [(x * na + a) * nb + b for a in range(na) for x in range(nx) for b in range(nb)]
    near_groups = [near_ids[a * near : (a + 1) * near] for a in range(na)]
    far_groups = [list(group) for group in zip(*near_groups)]
    device = lax.axis_index("node")
    feat = lax.axis_index("feat")
    near_at = device // (na * nb) * nb + device % nb
    capacity = sample_ids.shape[2]
    targets = self_ids.shape[1]
    width = features.shape[1]
    hidden = neighbour_one.shape[1]
    part = hidden // feats
    block_ids = tile_blocks[0]
    block_near = block_ids // (na * nb) * nb + block_ids % nb
    block_far = block_ids % (na * nb) // nb
    tiles = tile_weights[0]
    count = tiles.shape[0]
    lanes = targets // capacity

    def by_near(values):
        values = values.reshape((nx, na, nb) + values.shape[1:])
        return jnp.swapaxes(values, 1, 2).reshape((near, na) + values.shape[3:])

    sent_counts = lax.dynamic_index_in_dim(send_counts, device, 0, keepdims=False)
    used = jnp.arange(capacity, dtype=jnp.int32)[None, :] < sent_counts[:, None]
    slots = jnp.tile(by_near(jnp.where(used, dest_slots[0], targets)), (1, 1, lanes))
    own_lanes = jnp.arange(targets, dtype=jnp.int32) // capacity == near_at % lanes
    slots = jnp.where(own_lanes, slots, 0).astype(bf16)
    rows = pick(features, by_near(sample_ids[0]).reshape(-1))
    grad_t = lax.dynamic_slice_in_dim(out_grad.T, feat * part, part, 0)
    terms = jnp.einsum("kt,ntb->nkb", grad_t, tiles, preferred_element_type=f32).astype(bf16)
    there = block_near[None, :] == jnp.arange(near, dtype=jnp.int32)[:, None]
    terms = jnp.where(there[:, :, None, None], terms[None], jnp.zeros((), bf16))
    term_far = jnp.broadcast_to(block_far[:, None], (count, targets)).astype(bf16)
    sent = [
        rows.reshape(near, na * capacity, width),
        slots,
        terms.reshape(near, count * part, targets),
        to_all(jnp.pad(term_far, ((0, 8 - count), (0, 0))), near),
    ]
    got = exchange(jnp.concatenate(sent, axis=1), "node", near_groups)

    ends = [na * capacity, na * capacity + na, na * capacity + na + count * part]
    rows = got[:, : ends[0]].reshape(near, na, capacity, width).transpose(1, 0, 2, 3)
    rows = rows.reshape(na, near * capacity, width)
    slots = got[:, ends[0] : ends[1]].astype(f32).reshape(near // lanes, lanes, na, targets)
    slots = jnp.sum(slots, axis=1).astype(jnp.int32).transpose(1, 0, 2)
    target_ids = jnp.arange(targets, dtype=jnp.int32)
    chosen = slots.reshape(na, 1, near * capacity) == target_ids[None, :, None]
    degree = jnp.sum(chosen.astype(f32), axis=2).astype(bf16)
    summed = jnp.einsum("atr,ars->ats", chosen.astype(bf16), rows, preferred_element_type=f32)
    terms = got[:, ends[1] : ends[2]].reshape(near * count, part, targets).astype(f32)
    term_far = got[:, ends[2] : ends[2] + count].reshape(near * count, 1, targets).astype(jnp.int32)
    far_ids = jnp.arange(na, dtype=jnp.int32)[:, None, None]
    terms = sum(
        jnp.where(term_far[n][None] == far_ids, terms[n][None], 0.0) for n in range(near * count)
    ).astype(bf16)
    sent = [summed.astype(bf16), terms, jnp.pad(degree[:, None, :], ((0, 0), (0, 7), (0, 0)))]
    came = exchange(jnp.concatenate(sent, axis=1), "node", far_groups).astype(f32)
    summed = jnp.sum(came[:, :targets], axis=0)
    back_high, back_low = split(jnp.sum(came[:, targets : targets + part], axis=0))
    degree = jnp.sum(came[:, targets + part], axis=0)

    self_rows = pick(features, self_ids[0])
    mean = summed / (degree + 1.0)[:, None]
    mean_high, mean_low = split(mean)
    terms_one = (
        dot(self_one, self_rows, ((0,), (1,)))
        + dot(neighbour_one, mean_high, ((0,), (1,)))
        + dot(neighbour_one, mean_low, ((0,), (1,)))
    )
    high, low = split(terms_one.reshape(feats, part, targets))
    sent = [high, low, to_all(back_high, feats), to_all(back_low, feats)]
    got = exchange(jnp.concatenate(sent, axis=1), "feat")
    pre_one = jnp.sum(got[:, :part].astype(f32) + got[:, part : 2 * part].astype(f32), axis=0)
    back_high = got[:, 2 * part : 3 * part].reshape(hidden, targets)
    back_low = got[:, 3 * part :].reshape(hidden, targets)
    sigma = jax.nn.sigmoid(pre_one)
    hidden_part = (pre_one * sigma).astype(bf16)
    slope = sigma * (1.0 + pre_one * (1.0 - sigma))

    self_two_part = lax.dynamic_slice_in_dim(self_two, feat * part, part, 0)
    neighbour_two_part = lax.dynamic_slice_in_dim(neighbour_two, feat * part, part, 0)
    pre_grad = (
        dot(self_two_part, out_grad, ((1,), (1,)))
        + dot(neighbour_two_part, back_high, ((1,), (0,)))
        + dot(neighbour_two_part, back_low, ((1,), (0,)))
    ) * slope
    full = exchange(
        to_all(jnp.concatenate([pre_grad.astype(bf16), hidden_part], axis=0), feats), "feat"
    )
    pre_round = full[:, :part].reshape(hidden, targets)
    hidden_t = full[:, part:].reshape(hidden, targets)

    half = hidden // 2
    upper = quarters(
        dot(hidden_part, out_grad, ((1,), (0,))),
        dot(hidden_part, back_high, ((1,), (1,))) + dot(hidden_part, back_low, ((1,), (1,))),
    )
    lower = quarters(
        dot(self_rows, pre_round, ((0,), (1,))), dot(mean_high, pre_round, ((0,), (1,)))
    )
    share = upper.shape[0] // near
    rows_each = lower.shape[0] // near
    sent = [lower.reshape(near, rows_each, half), upper.reshape(near, share, half)]
    got = exchange(jnp.concatenate(sent, axis=1), "node", near_groups).astype(f32)
    sent = [jnp.sum(got, axis=0).astype(bf16), hidden_part]
    got = exchange(to_all(jnp.concatenate(sent, axis=0), na), "node", far_groups)
    sums = jnp.sum(got[:, : rows_each + share].astype(f32), axis=0).astype(bf16)
    sent = [sums, got[:, rows_each + share :].reshape(na * part, targets)]
    got = exchange(to_all(jnp.concatenate(sent, axis=0), near), "node", near_groups)
    lower = got[:, :rows_each].reshape(4, width, half).astype(f32)
    upper = got[:, rows_each : rows_each + share].reshape(near * share, half)
    all_hidden = got[:, rows_each + share :].reshape(near * na, part, targets)

    places = block_near * na + block_far
    agg_part = sum(
        dot(lax.dynamic_index_in_dim(all_hidden, places[n], 0, keepdims=False), tiles[n], ((1,), (1,)))
        for n in range(tiles.shape[0])
    ).astype(bf16)
    got = exchange(to_all(jnp.concatenate([agg_part, upper], axis=0), feats), "feat")
    agg_t = got[:, :part].reshape(hidden, targets)
    layer_output = (
        dot(hidden_t, self_two, ((0,), (0,))) + dot(agg_t, neighbour_two, ((0,), (0,)))
    ).astype(bf16)
    upper = got[:, part:].reshape(feats, 4, part, half).astype(f32)
    upper = upper.transpose(1, 0, 2, 3).reshape(4, hidden, half)

    def halves(stack, which):
        return jnp.concatenate([stack[2 * which], stack[2 * which + 1]], axis=1)

    return (layer_output, halves(lower, 0), halves(lower, 1), halves(upper, 0), halves(upper, 1))


def solution(mesh):
    placed = (
        P("node", "feat"),
        P("feat", None),
        P("feat", None),
        P("node", None, None),
        P("node", None, None),
        P(),
        P("node", None),
        P("node", None),
        P("node", None, None, None),
        P(),
        P(),
        P("node", None),
    )
    return jax.shard_map(
        shards,
        mesh=mesh,
        in_specs=placed,
        out_specs=(P("node", None), P("feat", None), P("feat", None), P(), P()),
        check_vma=False,
    )
```

time: 188 us -> 152 us (0.81)
  waiting for transfers between devices: 83.5 us -> 37 us
  blocking collectives: 18.5 us -> 43.5 us
  starting transfers between devices: 57.3 us -> 42.2 us
    all_to_all x6 -> x5, waiting for transfers between devices: 83.5 us -> 37 us  [exchange(): lax.all_to_all(values, axis, split_axis=0, concat_axis=0, tiled=True, axi...]
    all_to_all x1 -> x3, blocking collectives: 18.5 us -> 43.5 us  [exchange(): lax.all_to_all(values, axis, split_axis=0, concat_axis=0, tiled=True, axi...]
    all_to_all x6 -> x5, starting transfers between devices: 57.3 us -> 42.2 us  [exchange(): lax.all_to_all(values, axis, split_axis=0, concat_axis=0, tiled=True, axi...]
    dot_general x18 -> x19, matrix products: 4.55 us -> 4.73 us  [dot(): return lax.dot_general(a, b, (dims, ((), ())), preferred_element_type=f32)]
  transfers between devices with their start and end apart: 6 -> 5, of which waited for: 5 -> 4; matrix products, arithmetic and copies ran while one was open for 2% -> 2% of each run, Pallas kernels for 0% -> 0%
where the time goes in v4:
time: 152 us; the launch traced here: 151 us
  blocking collectives  43.5 us (29%)
  starting transfers between devices  42.2 us (28%)
  waiting for transfers between devices  37 us (24%)
  between operations  9.11 us (6%)
  other arithmetic  7.75 us (5%)
  local copies, waits for them, and re-layouts  6.32 us (4%)
  matrix products  5.27 us (3%)
    all_to_all x3, blocking collectives, exchange(): lax.all_to_all(values, axis, split_axis=0, concat_axis=0, tiled=True, axi...  43.5 us
    all_to_all x5, starting transfers between devices, exchange(): lax.all_to_all(values, axis, split_axis=0, concat_axis=0, tiled=True, axi...  42.2 us
    all_to_all x5, waiting for transfers between devices, exchange(): lax.all_to_all(values, axis, split_axis=0, concat_axis=0, tiled=True, axi...  37 us
    dot_general x19, matrix products, dot(): return lax.dot_general(a, b, (dims, ((), ())), preferred_element_type=f32)  4.73 us
  transfers between devices with their start and end apart: 5, of which 4 were waited for; matrix products, arithmetic and copies ran while one was open for 2% of the time, Pallas kernels for 0%

profile of v4, /device:TPU:1, one launch (start us, length us, event | category | flops | bytes accessed | tf_op | source)
XLA Modules:
  0.0 151.1 jit_solution(13251078582047634731)
XLA Ops:
  0.6 0.0 copy-start
  0.7 0.7 fusion.55
  1.4 0.7 multiply_add_fusion
  2.2 0.1 fusion.50
  2.2 0.1 broadcast_in_dim.524
  2.3 0.1 broadcast_in_dim.525
  2.4 0.7 fusion.54
  3.1 0.1 lt.62
  3.2 0.8 copy.19
  4.0 0.1 eq.720
  4.1 0.8 copy.21
  4.9 0.1 fusion.16
  5.1 0.1 tile.12
  5.2 0.2 convolution_convert_fusion.3
  5.5 0.2 broadcast_select_fusion
  5.7 1.1 fusion.1
  6.8 0.2 maximum_maximum_fusion
  7.0 16.1 %all_to_all.40 = bf16[8,400,128]{2,1,0:T(8,128)(2,1)S(1)} all-to-all(bf16[8,400,128]{2,1,0:T(8,128)(2,1)S(1)} %maximum_maximum_fusion), channel_id=1, replica_groups={{0,1,16,17,32,33,48,49},{2,3,18,19,34,35,50,51},{4,5,20,21,36,37,52,53}..., dimensions={0} | all-to-all | bytes 1638400 | tf_op jit(solution)/shard_map/all_to_all | solution.py:15
  23.2 0.1 convert.35
  23.3 0.2 convert_reduce_fusion
  23.7 0.3 convolution_convert_fusion
  24.2 0.7 add_convert_fusion
  24.9 0.8 fusion.11
  25.6 16.0 %all-to-all-start.1 = ((bf16[8,168,128]{2,1,0:T(8,128)(2,1)}), bf16[8,168,128]{2,1,0:T(8,128)(2,1)S(1)}, u32[]{:S(2)}, u32[]{:S(2)}) async-start(bf16[8,168,128]{2,1,0:T(8,128)(2,1)} %fusion.11), calls=%async_computation.1 | async-start | bytes 688128 | tf_op jit(solution)/shard_map/all_to_all | solution.py:15
  41.6 0.2 convolution_convert_fusion.4
  41.8 0.1 fusion.65
  42.0 0.0 copy-start.3
  42.0 19.6 %all-to-all-done.1 = bf16[8,168,128]{2,1,0:T(8,128)(2,1)S(1)} async-done(((bf16[8,168,128]{2,1,0:T(8,128)(2,1)}), bf16[8,168,128]{2,1,0:T(8,128)(2,1)S(1)}, u32[]{:S(2)}, u32[]{:S(2)}) %all-to-all-start.1) | async-done | bytes 344096 | tf_op jit(solution)/shard_map/all_to_all | solution.py:15
  61.8 0.2 convolution_add_fusion.2
  62.0 0.2 fusion.3
  62.2 0.1 copy.26
  62.4 0.7 pad_maximum_fusion
  63.1 9.9 %all-to-all-start.2 = ((bf16[8,128,128]{2,1,0:T(8,128)(2,1)}), bf16[8,128,128]{2,1,0:T(8,128)(2,1)S(1)}, u32[]{:S(2)}, u32[]{:S(2)}) async-start(bf16[8,128,128]{2,1,0:T(8,128)(2,1)} %pad_maximum_fusion), calls=%async_computation.2 | async-start | bytes 524288 | tf_op jit(solution)/shard_map/all_to_all | solution.py:15
  73.0 0.1 fusion.30
  73.1 6.4 %all-to-all-done.2 = bf16[8,128,128]{2,1,0:T(8,128)(2,1)S(1)} async-done(((bf16[8,128,128]{2,1,0:T(8,128)(2,1)}), bf16[8,128,128]{2,1,0:T(8,128)(2,1)S(1)}, u32[]{:S(2)}, u32[]{:S(2)}) %all-to-all-start.2) | async-done | bytes 262176 | tf_op jit(solution)/shard_map/all_to_all | solution.py:15
  79.6 0.1 convolution_convert_fusion.5
  79.7 0.1 fusion.67
  79.8 0.1 convolution_add_fusion.8
  80.0 0.1 fusion.7
  80.1 0.1 fusion.5
  80.3 0.7 broadcast_in_dim.630
  81.0 4.3 %all-to-all-start.3 = ((bf16[8,64,128]{2,1,0:T(8,128)(2,1)}), bf16[8,64,128]{2,1,0:T(8,128)(2,1)S(1)}, u32[]{:S(2)}, u32[]{:S(2)}) async-start(bf16[8,64,128]{2,1,0:T(8,128)(2,1)} %broadcast_in_dim.630), calls=%async_computation.3 | async-start | bytes 262144 | tf_op jit(solution)/shard_map/all_to_all | solution.py:15
  85.3 5.3 %all-to-all-done.3 = bf16[8,64,128]{2,1,0:T(8,128)(2,1)S(1)} async-done(((bf16[8,64,128]{2,1,0:T(8,128)(2,1)}), bf16[8,64,128]{2,1,0:T(8,128)(2,1)S(1)}, u32[]{:S(2)}, u32[]{:S(2)}) %all-to-all-start.3) | async-done | bytes 131104 | tf_op jit(solution)/shard_map/all_to_all | solution.py:15
  90.6 0.3 convolution_convert_fusion.1
  90.9 0.2 convolution_convert_fusion.2
  91.1 8.2 %all_to_all.41 = bf16[8,80,128]{2,1,0:T(8,128)(2,1)S(1)} all-to-all(bf16[8,80,128]{2,1,0:T(8,128)(2,1)S(1)} %pad_maximum_fusion.3), channel_id=1, replica_groups={{0,1,16,17,32,33,48,49},{2,3,18,19,34,35,50,51},{4,5,20,21,36,37,52,53}..., dimensions={0} | all-to-all | bytes 327680 | tf_op jit(solution)/shard_map/all_to_all | solution.py:15
  99.4 19.2 %all_to_all.42 = bf16[8,112,128]{2,1,0:T(8,128)(2,1)S(1)} all-to-all(bf16[8,112,128]{2,1,0:T(8,128)(2,1)S(1)} %broadcast_in_dim.631), channel_id=1, replica_groups={{0,2,4,6,8,10,12,14},{1,3,5,7,9,11,13,15},{16,18,20,22,24,26,28,30},{17..., dimensions={0} | all-to-all | bytes 458752 | tf_op jit(solution)/shard_map/all_to_all | solution.py:15
  118.7 1.0 broadcast_in_dim.632
  119.6 3.5 %all-to-all-start.6 = ((bf16[8,336,128]{2,1,0:T(8,128)(2,1)}), bf16[8,336,128]{2,1,0:T(8,128)(2,1)S(1)}, u32[]{:S(2)}, u32[]{:S(2)}) async-start(bf16[8,336,128]{2,1,0:T(8,128)(2,1)} %broadcast_in_dim.632), calls=%async_computation.6 | async-start | bytes 1376256 | tf_op jit(solution)/shard_map/all_to_all | solution.py:15
  123.2 0.6 fusion.64
  131.5 0.2 fusion.66
  131.8 0.1 fusion.22
  131.9 0.1 convolution_add_fusion.6
  132.1 0.2 convolution_add_fusion.5
  132.2 0.2 fusion.8
  132.4 0.8 broadcast_in_dim.633
  133.2 8.4 %all-to-all-start.7 = ((bf16[8,160,128]{2,1,0:T(8,128)(2,1)}), bf16[8,160,128]{2,1,0:T(8,128)(2,1)S(1)}, u32[]{:S(2)}, u32[]{:S(2)}) async-start(bf16[8,160,128]{2,1,0:T(8,128)(2,1)} %broadcast_in_dim.633), calls=%async_computation.7 | async-start | bytes 655360 | tf_op jit(solution)/shard_map/all_to_all | solution.py:15
  141.6 0.7 pad_maximum_fusion.6
  142.3 0.7 pad_maximum_fusion.5
  143.0 5.8 %all-to-all-done.7 = bf16[8,160,128]{2,1,0:T(8,128)(2,1)S(1)} async-done(((bf16[8,160,128]{2,1,0:T(8,128)(2,1)}), bf16[8,160,128]{2,1,0:T(8,128)(2,1)S(1)}, u32[]{:S(2)}, u32[]{:S(2)}) %all-to-all-start.7) | async-done | bytes 327712 | tf_op jit(solution)/shard_map/all_to_all | solution.py:15
  148.8 0.1 convert_bitcast_fusion
  148.9 0.8 fusion.4
  149.7 0.7 pad_maximum_fusion.2
  150.4 0.7 pad_maximum_fusion.1
  (84 shorter events, 1.0 us)
Async XLA Ops:
  0.6 5.1 %copy-start = (bf16[512,128]{1,0:T(8,128)(2,1)S(1)}, bf16[512,128]{1,0:T(8,128)(2,1)}, u32[]{:S(2)}) copy-start(bf16[512,128]{1,0:T(8,128)(2,1)} %param.12) | copy-start | bytes 393220
  0.6 4.6 %copy-start.1 = (bf16[1,4,128,128]{3,2,1,0:T(8,128)(2,1)S(1)}, bf16[1,4,128,128]{3,2,1,0:T(8,128)(2,1)}, u32[]{:S(2)}) copy-start(bf16[1,4,128,128]{3,2,1,0:T(8,128)(2,1)} %param.20) | copy-start | bytes 393220
  0.7 4.6 %copy-start.2 = (bf16[128,256]{1,0:T(8,128)(2,1)S(1)}, bf16[128,256]{1,0:T(8,128)(2,1)}, u32[]{:S(2)}) copy-start(bf16[128,256]{1,0:T(8,128)(2,1)} %param.23) | copy-start | bytes 196612
  24.8 16.8 %copy-start.7 = (s32[1,128]{1,0:T(1,128)S(1)}, s32[1,128]{1,0:T(1,128)}, u32[]{:S(2)}) copy-start(s32[1,128]{1,0:T(1,128)} %param.18) | copy-start | bytes 1540
  24.8 17.0 %copy-start.6 = (bf16[128,256]{1,0:T(8,128)(2,1)S(1)}, bf16[128,256]{1,0:T(8,128)(2,1)}, u32[]{:S(2)}) copy-start(bf16[128,256]{1,0:T(8,128)(2,1)} %param.13) | copy-start | bytes 196612
  25.6 36.0 %all-to-all-start.1 = ((bf16[8,168,128]{2,1,0:T(8,128)(2,1)}), bf16[8,168,128]{2,1,0:T(8,128)(2,1)S(1)}, u32[]{:S(2)}, u32[]{:S(2)}) async-start(bf16[8,168,128]{2,1,0:T(8,128)(2,1)} %fusion.11), calls=%async_computation.1 | async-start | bytes 688128 | tf_op jit(solution)/shard_map/all_to_all | solution.py:15
  42.0 19.8 %copy-start.3 = (bf16[128,256]{1,0:T(8,128)(2,1)S(1)}, bf16[128,256]{1,0:T(8,128)(2,1)}, u32[]{:S(2)}) copy-start(bf16[128,256]{1,0:T(8,128)(2,1)} %param.14) | copy-start | bytes 196612
  62.2 10.8 %copy-start.5 = (bf16[256,256]{1,0:T(8,128)(2,1)S(1)}, bf16[256,256]{1,0:T(8,128)(2,1)}, u32[]{:S(2)}) copy-start(bf16[256,256]{1,0:T(8,128)(2,1)} %param.21) | copy-start | bytes 393220
  62.4 17.5 %copy-start.4 = (bf16[256,256]{1,0:T(8,128)(2,1)S(1)}, bf16[256,256]{1,0:T(8,128)(2,1)}, u32[]{:S(2)}) copy-start(bf16[256,256]{1,0:T(8,128)(2,1)} %param.22) | copy-start | bytes 393220
  63.1 16.4 %all-to-all-start.2 = ((bf16[8,128,128]{2,1,0:T(8,128)(2,1)}), bf16[8,128,128]{2,1,0:T(8,128)(2,1)S(1)}, u32[]{:S(2)}, u32[]{:S(2)}) async-start(bf16[8,128,128]{2,1,0:T(8,128)(2,1)} %pad_maximum_fusion), calls=%async_computation.2 | async-start | bytes 524288 | tf_op jit(solution)/shard_map/all_to_all | solution.py:15
  81.0 9.6 %all-to-all-start.3 = ((bf16[8,64,128]{2,1,0:T(8,128)(2,1)}), bf16[8,64,128]{2,1,0:T(8,128)(2,1)S(1)}, u32[]{:S(2)}, u32[]{:S(2)}) async-start(bf16[8,64,128]{2,1,0:T(8,128)(2,1)} %broadcast_in_dim.630), calls=%async_computation.3 | async-start | bytes 262144 | tf_op jit(solution)/shard_map/all_to_all | solution.py:15
  119.6 12.1 %all-to-all-start.6 = ((bf16[8,336,128]{2,1,0:T(8,128)(2,1)}), bf16[8,336,128]{2,1,0:T(8,128)(2,1)S(1)}, u32[]{:S(2)}, u32[]{:S(2)}) async-start(bf16[8,336,128]{2,1,0:T(8,128)(2,1)} %broadcast_in_dim.632), calls=%async_computation.6 | async-start | bytes 1376256 | tf_op jit(solution)/shard_map/all_to_all | solution.py:15
  133.2 15.6 %all-to-all-start.7 = ((bf16[8,160,128]{2,1,0:T(8,128)(2,1)}), bf16[8,160,128]{2,1,0:T(8,128)(2,1)S(1)}, u32[]{:S(2)}, u32[]{:S(2)}) async-start(bf16[8,160,128]{2,1,0:T(8,128)(2,1)} %broadcast_in_dim.633), calls=%async_computation.7 | async-start | bytes 655360 | tf_op jit(solution)/shard_map/all_to_all | solution.py:15

commit v5 on v4

--- a/solution.py
+++ b/solution.py
@@ -1,6 +1,10 @@
+import functools
+
 import jax
 import jax.numpy as jnp
 from jax import lax
+from jax.experimental import pallas as pl
+from jax.experimental.pallas import tpu as pltpu
 from jax.sharding import PartitionSpec as P
 
 bf16 = jnp.bfloat16
@@ -36,6 +40,92 @@
     half = first.shape[1] // 2
     parts = [first[:, :half], first[:, half:], second[:, :half], second[:, half:]]
     return jnp.concatenate(parts, axis=0).astype(bf16)
+
+
+def where_am_i():
+    return lax.axis_index("node"), lax.axis_index("feat")
+
+
+def pack_kernel(
+    ids_ref,
+    slots_ref,
+    counts_ref,
+    blocks_ref,
+    features_ref,
+    tiles_ref,
+    grad_ref,
+    sent_ref,
+    slots_scratch,
+    grad_scratch,
+    *,
+    nx,
+    na,
+    nb,
+    place,
+):
+    device, feat = place()
+    near = nx * nb
+    capacity, nodes = ids_ref.shape
+    locals_, width = features_ref.shape
+    count, targets, _ = tiles_ref.shape
+    part = sent_ref.shape[1] - na * capacity - na - 8
+    part = part // count
+    lanes = targets // capacity
+    near_at = (device // (na * nb)) * nb + device % nb
+
+    used = lax.broadcasted_iota(jnp.int32, (capacity, nodes), 0) < counts_ref[pl.ds(device, 1), :]
+    slots = jnp.where(used, slots_ref[...], targets).astype(f32)
+    slots = jnp.concatenate([slots] * lanes, axis=0)
+    slots = jnp.concatenate([slots, jnp.zeros((targets, targets - nodes), f32)], axis=1).T
+    group = lax.broadcasted_iota(jnp.int32, (targets, targets), 1) // capacity
+    slots_scratch[...] = jnp.where(group == near_at % lanes, slots, 0.0)
+    grad_scratch[...] = grad_ref[...].astype(f32).T
+    grad_t = grad_scratch[pl.ds(pl.multiple_of(feat * part, part), part), :].astype(bf16)
+    terms = [dot(grad_t, tiles_ref[k], ((1,), (0,))) for k in range(count)]
+    blocks = [blocks_ref[0, k] for k in range(count)]
+    row = lax.broadcasted_iota(jnp.int32, (8, targets), 0)
+    far_rows = jnp.zeros((8, targets), jnp.int32)
+    for k in range(count):
+        far_rows = jnp.where(row == k, blocks[k] % (na * nb) // nb, far_rows)
+    far_rows = far_rows.astype(f32)
+    local_ids = lax.broadcasted_iota(jnp.int32, (capacity, locals_), 1)
+    for x in range(nx):
+        for b in range(nb):
+            to = x * nb + b
+            owners = [(x * na + a) * nb + b for a in range(na)]
+            chosen = jnp.concatenate(
+                [jnp.where(ids_ref[:, o : o + 1] == local_ids, 1.0, 0.0).astype(bf16) for o in owners],
+                axis=0,
+            )
+            rows = dot(chosen, features_ref[...], ((1,), (0,)))
+            sent_ref[to, : na * capacity, :] = rows.astype(bf16)
+            at = na * capacity
+            for k in range(count):
+                there = blocks[k] // (na * nb) * nb + blocks[k] % nb == to
+                term = jnp.where(there, terms[k], 0.0)
+                sent_ref[to, at : at + part, :] = term.astype(bf16)
+                at += part
+            slot_rows = slots_scratch[pl.ds(owners[0], na, stride=nb), :]
+            sent_ref[to, at : at + na + 8, :] = jnp.concatenate([slot_rows, far_rows], 0).astype(bf16)
+
+
+def pack(sample_ids, dest_slots, counts, blocks, features, tiles, grad, nx, na, nb, part, place):
+    count, targets, _ = tiles.shape
+    capacity, nodes = sample_ids.shape
+    total = na * capacity + count * part + na + 8
+    kernel = functools.partial(pack_kernel, nx=nx, na=na, nb=nb, place=place)
+    vmem = pl.BlockSpec(memory_space=pltpu.VMEM)
+    return pl.pallas_call(
+        kernel,
+        out_shape=jax.ShapeDtypeStruct((nx * nb, total, features.shape[1]), bf16),
+        in_specs=[vmem] * 3 + [pl.BlockSpec(memory_space=pltpu.SMEM)] + [vmem] * 3,
+        out_specs=vmem,
+        scratch_shapes=[
+            pltpu.VMEM((targets, targets), f32),
+            pltpu.VMEM((grad.shape[1], targets), f32),
+        ],
+        compiler_params=pltpu.CompilerParams(vmem_limit_bytes=24 * 1024 * 1024),
+    )(sample_ids, dest_slots, counts, blocks, features, tiles, grad)
 
 
 def shards(
@@ -60,9 +150,7 @@
     near_ids = [(x * na + a) * nb + b for a in range(na) for x in range(nx) for b in range(nb)]
     near_groups = [near_ids[a * near : (a + 1) * near] for a in range(na)]
     far_groups = [list(group) for group in zip(*near_groups)]
-    device = lax.axis_index("node")
     feat = lax.axis_index("feat")
-    near_at = device // (na * nb) * nb + device % nb
     capacity = sample_ids.shape[2]
     targets = self_ids.shape[1]
     width = features.shape[1]
@@ -75,39 +163,32 @@
     count = tiles.shape[0]
     lanes = targets // capacity
 
-    def by_near(values):
-        values = values.reshape((nx, na, nb) + values.shape[1:])
-        return jnp.swapaxes(values, 1, 2).reshape((near, na) + values.shape[3:])
-
-    sent_counts = lax.dynamic_index_in_dim(send_counts, device, 0, keepdims=False)
-    used = jnp.arange(capacity, dtype=jnp.int32)[None, :] < sent_counts[:, None]
-    slots = jnp.tile(by_near(jnp.where(used, dest_slots[0], targets)), (1, 1, lanes))
-    own_lanes = jnp.arange(targets, dtype=jnp.int32) // capacity == near_at % lanes
-    slots = jnp.where(own_lanes, slots, 0).astype(bf16)
-    rows = pick(features, by_near(sample_ids[0]).reshape(-1))
-    grad_t = lax.dynamic_slice_in_dim(out_grad.T, feat * part, part, 0)
-    terms = jnp.einsum("kt,ntb->nkb", grad_t, tiles, preferred_element_type=f32).astype(bf16)
-    there = block_near[None, :] == jnp.arange(near, dtype=jnp.int32)[:, None]
-    terms = jnp.where(there[:, :, None, None], terms[None], jnp.zeros((), bf16))
-    term_far = jnp.broadcast_to(block_far[:, None], (count, targets)).astype(bf16)
-    sent = [
-        rows.reshape(near, na * capacity, width),
-        slots,
-        terms.reshape(near, count * part, targets),
-        to_all(jnp.pad(term_far, ((0, 8 - count), (0, 0))), near),
-    ]
-    got = exchange(jnp.concatenate(sent, axis=1), "node", near_groups)
-
-    ends = [na * capacity, na * capacity + na, na * capacity + na + count * part]
+    sent = pack(
+        sample_ids[0].T,
+        dest_slots[0].T,
+        send_counts,
+        tile_blocks,
+        features,
+        tiles,
+        out_grad,
+        nx,
+        na,
+        nb,
+        part,
+        where_am_i,
+    )
+    got = exchange(sent, "node", near_groups)
+
+    ends = [na * capacity, na * capacity + count * part, na * capacity + count * part + na]
     rows = got[:, : ends[0]].reshape(near, na, capacity, width).transpose(1, 0, 2, 3)
     rows = rows.reshape(na, near * capacity, width)
-    slots = got[:, ends[0] : ends[1]].astype(f32).reshape(near // lanes, lanes, na, targets)
+    slots = got[:, ends[1] : ends[2]].astype(f32).reshape(near // lanes, lanes, na, targets)
     slots = jnp.sum(slots, axis=1).astype(jnp.int32).transpose(1, 0, 2)
     target_ids = jnp.arange(targets, dtype=jnp.int32)
     chosen = slots.reshape(na, 1, near * capacity) == target_ids[None, :, None]
     degree = jnp.sum(chosen.astype(f32), axis=2).astype(bf16)
     summed = jnp.einsum("atr,ars->ats", chosen.astype(bf16), rows, preferred_element_type=f32)
-    terms = got[:, ends[1] : ends[2]].reshape(near * count, part, targets).astype(f32)
+    terms = got[:, ends[0] : ends[1]].reshape(near * count, part, targets).astype(f32)
     term_far = got[:, ends[2] : ends[2] + count].reshape(near * count, 1, targets).astype(jnp.int32)
     far_ids = jnp.arange(na, dtype=jnp.int32)[:, None, None]
     terms = sum(

time: 152 us -> 154 us (1.013)
  local copies, waits for them, and re-layouts: 6.32 us -> 11.9 us
  other arithmetic: 7.75 us -> 5.71 us
    unnamed x18 -> x30, local copies, waits for them, and re-layouts: 1.65 us -> 8.43 us
    dot_general x19 -> x18, matrix products: 4.73 us -> 3.67 us  [dot(): return lax.dot_general(a, b, (dims, ((), ())), preferred_element_type=f32)]
where the time goes in v5:
time: 154 us; the launch traced here: 153 us
  blocking collectives  43.5 us (28%)
  starting transfers between devices  41.6 us (27%)
  waiting for transfers between devices  35.8 us (23%)
  local copies, waits for them, and re-layouts  11.9 us (8%)
  between operations  8.94 us (6%)
  other arithmetic  5.71 us (4%)
  matrix products  3.97 us (3%)
    all_to_all x3, blocking collectives, exchange(): lax.all_to_all(values, axis, split_axis=0, concat_axis=0, tiled=True, axi...  43.5 us
    all_to_all x5, starting transfers between devices, exchange(): lax.all_to_all(values, axis, split_axis=0, concat_axis=0, tiled=True, axi...  41.6 us
    all_to_all x5, waiting for transfers between devices, exchange(): lax.all_to_all(values, axis, split_axis=0, concat_axis=0, tiled=True, axi...  35.8 us
    unnamed x30, local copies, waits for them, and re-layouts  8.43 us
    dot_general x18, matrix products, dot(): return lax.dot_general(a, b, (dims, ((), ())), preferred_element_type=f32)  3.67 us
  transfers between devices with their start and end apart: 5, of which 4 were waited for; matrix products, arithmetic and copies ran while one was open for 2% of the time, Pallas kernels for 0%

profile of v5, /device:TPU:1, one launch (start us, length us, event | category | flops | bytes accessed | tf_op | source)
XLA Modules:
  0.0 152.8 jit_solution(11470488309971092244)
XLA Ops:
  0.6 0.0 copy-start
  0.6 0.0 copy-start.10
  0.7 0.7 copy-done.10
  1.3 0.8 copy-done.1
  2.2 0.9 copy-done.3
  3.1 0.9 copy-done.5
  4.0 0.8 copy-done.7
  4.8 0.7 copy-done.8
  5.5 0.7 copy-done.9
  6.2 1.4 shard_map.155
  7.6 16.1 %all_to_all.40 = bf16[8,400,128]{2,1,0:T(8,128)(2,1)S(1)} all-to-all(bf16[8,400,128]{2,1,0:T(8,128)(2,1)S(1)} %shard_map.155), channel_id=1, replica_groups={{0,1,16,17,32,33,48,49},{2,3,18,19,34,35,50,51},{4,5,20,21,36,37,52,53}..., dimensions={0} | all-to-all | bytes 1638400 | tf_op jit(solution)/shard_map/all_to_all | solution.py:19
  23.8 0.1 convert.36
  24.0 0.2 convert_reduce_fusion
  24.3 0.3 convolution_convert_fusion
  24.8 0.7 add_convert_fusion
  25.5 0.8 fusion.8
  26.2 16.1 %all-to-all-start.1 = ((bf16[8,168,128]{2,1,0:T(8,128)(2,1)}), bf16[8,168,128]{2,1,0:T(8,128)(2,1)S(1)}, u32[]{:S(2)}, u32[]{:S(2)}) async-start(bf16[8,168,128]{2,1,0:T(8,128)(2,1)} %fusion.8), calls=%async_computation.1 | async-start | bytes 688128 | tf_op jit(solution)/shard_map/all_to_all | solution.py:19
  42.3 0.6 copy-done.14
  43.0 0.2 convolution_convert_fusion.3
  43.2 0.6 copy-done.13
  43.8 0.1 fusion.53
  44.0 18.4 %all-to-all-done.1 = bf16[8,168,128]{2,1,0:T(8,128)(2,1)S(1)} async-done(((bf16[8,168,128]{2,1,0:T(8,128)(2,1)}), bf16[8,168,128]{2,1,0:T(8,128)(2,1)S(1)}, u32[]{:S(2)}, u32[]{:S(2)}) %all-to-all-start.1) | async-done | bytes 344096 | tf_op jit(solution)/shard_map/all_to_all | solution.py:19
  62.4 0.0 copy-start.11
  62.5 0.8 copy-done.11
  63.3 0.2 convolution_add_fusion.2
  63.5 0.2 fusion
  63.7 0.1 copy.84
  63.9 0.7 pad_maximum_fusion
  64.6 10.0 %all-to-all-start.2 = ((bf16[8,128,128]{2,1,0:T(8,128)(2,1)}), bf16[8,128,128]{2,1,0:T(8,128)(2,1)S(1)}, u32[]{:S(2)}, u32[]{:S(2)}) async-start(bf16[8,128,128]{2,1,0:T(8,128)(2,1)} %pad_maximum_fusion), calls=%async_computation.2 | async-start | bytes 524288 | tf_op jit(solution)/shard_map/all_to_all | solution.py:19
  74.7 0.1 fusion.23
  74.8 6.4 %all-to-all-done.2 = bf16[8,128,128]{2,1,0:T(8,128)(2,1)S(1)} async-done(((bf16[8,128,128]{2,1,0:T(8,128)(2,1)}), bf16[8,128,128]{2,1,0:T(8,128)(2,1)S(1)}, u32[]{:S(2)}, u32[]{:S(2)}) %all-to-all-start.2) | async-done | bytes 262176 | tf_op jit(solution)/shard_map/all_to_all | solution.py:19
  81.2 0.1 convolution_convert_fusion.4
  81.4 0.1 fusion.55
  81.5 0.0 copy-done
  81.5 0.1 convolution_add_fusion.8
  81.6 0.1 fusion.4
  81.8 0.1 fusion.2
  81.9 0.7 broadcast_in_dim.565
  82.6 4.3 %all-to-all-start.3 = ((bf16[8,64,128]{2,1,0:T(8,128)(2,1)}), bf16[8,64,128]{2,1,0:T(8,128)(2,1)S(1)}, u32[]{:S(2)}, u32[]{:S(2)}) async-start(bf16[8,64,128]{2,1,0:T(8,128)(2,1)} %broadcast_in_dim.565), calls=%async_computation.3 | async-start | bytes 262144 | tf_op jit(solution)/shard_map/all_to_all | solution.py:19
  86.9 5.3 %all-to-all-done.3 = bf16[8,64,128]{2,1,0:T(8,128)(2,1)S(1)} async-done(((bf16[8,64,128]{2,1,0:T(8,128)(2,1)}), bf16[8,64,128]{2,1,0:T(8,128)(2,1)S(1)}, u32[]{:S(2)}, u32[]{:S(2)}) %all-to-all-start.3) | async-done | bytes 131104 | tf_op jit(solution)/shard_map/all_to_all | solution.py:19
  92.2 0.3 convolution_convert_fusion.1
  92.5 0.2 convolution_convert_fusion.2
  92.8 8.2 %all_to_all.41 = bf16[8,80,128]{2,1,0:T(8,128)(2,1)S(1)} all-to-all(bf16[8,80,128]{2,1,0:T(8,128)(2,1)S(1)} %pad_maximum_fusion.3), channel_id=1, replica_groups={{0,1,16,17,32,33,48,49},{2,3,18,19,34,35,50,51},{4,5,20,21,36,37,52,53}..., dimensions={0} | all-to-all | bytes 327680 | tf_op jit(solution)/shard_map/all_to_all | solution.py:19
  101.0 19.2 %all_to_all.42 = bf16[8,112,128]{2,1,0:T(8,128)(2,1)S(1)} all-to-all(bf16[8,112,128]{2,1,0:T(8,128)(2,1)S(1)} %broadcast_in_dim.566), channel_id=1, replica_groups={{0,2,4,6,8,10,12,14},{1,3,5,7,9,11,13,15},{16,18,20,22,24,26,28,30},{17..., dimensions={0} | all-to-all | bytes 458752 | tf_op jit(solution)/shard_map/all_to_all | solution.py:19
  120.3 0.9 broadcast_in_dim.567
  121.2 3.5 %all-to-all-start.6 = ((bf16[8,336,128]{2,1,0:T(8,128)(2,1)}), bf16[8,336,128]{2,1,0:T(8,128)(2,1)S(1)}, u32[]{:S(2)}, u32[]{:S(2)}) async-start(bf16[8,336,128]{2,1,0:T(8,128)(2,1)} %broadcast_in_dim.567), calls=%async_computation.6 | async-start | bytes 1376256 | tf_op jit(solution)/shard_map/all_to_all | solution.py:19
  124.8 0.6 fusion.52
  133.2 0.2 fusion.54
  133.4 0.0 copy-start.4
  133.4 0.0 all-to-all-done.6
  133.4 0.8 copy-done.4
  134.3 0.1 fusion.16
  134.4 0.1 convolution_add_fusion.6
  134.6 0.2 convolution_add_fusion.5
  134.7 0.2 fusion.5
  134.9 0.8 broadcast_in_dim.568
  135.7 7.6 %all-to-all-start.7 = ((bf16[8,160,128]{2,1,0:T(8,128)(2,1)}), bf16[8,160,128]{2,1,0:T(8,128)(2,1)S(1)}, u32[]{:S(2)}, u32[]{:S(2)}) async-start(bf16[8,160,128]{2,1,0:T(8,128)(2,1)} %broadcast_in_dim.568), calls=%async_computation.7 | async-start | bytes 655360 | tf_op jit(solution)/shard_map/all_to_all | solution.py:19
  143.3 0.7 pad_maximum_fusion.6
  143.9 0.7 pad_maximum_fusion.5
  144.6 5.8 %all-to-all-done.7 = bf16[8,160,128]{2,1,0:T(8,128)(2,1)S(1)} async-done(((bf16[8,160,128]{2,1,0:T(8,128)(2,1)}), bf16[8,160,128]{2,1,0:T(8,128)(2,1)S(1)}, u32[]{:S(2)}, u32[]{:S(2)}) %all-to-all-start.7) | async-done | bytes 327712 | tf_op jit(solution)/shard_map/all_to_all | solution.py:19
  150.4 0.1 convert_bitcast_fusion
  150.5 0.8 fusion.1
  151.3 0.7 pad_maximum_fusion.2
  152.1 0.7 pad_maximum_fusion.1
  (78 shorter events, 0.9 us)
Async XLA Ops:
  0.6 80.8 %copy-start = (bf16[256,256]{1,0:T(8,128)(2,1)S(1)}, bf16[256,256]{1,0:T(8,128)(2,1)}, u32[]{:S(2)}) copy-start(bf16[256,256]{1,0:T(8,128)(2,1)} %param.22) | copy-start | bytes 393220
  0.6 0.7 copy-start.10
  1.3 0.8 copy-start.1
  2.2 0.9 copy-start.3
  3.1 0.9 copy-start.5
  4.0 0.8 copy-start.7
  4.7 0.7 copy-start.8
  5.5 0.7 copy-start.9
  26.2 16.1 %copy-start.6 = (bf16[512,128]{1,0:T(8,128)(2,1)S(1)}, bf16[512,128]{1,0:T(8,128)(2,1)}, u32[]{:S(2)}) copy-start(bf16[512,128]{1,0:T(8,128)(2,1)} %features_ref.1) | copy-start | bytes 393220
  26.2 36.1 %all-to-all-start.1 = ((bf16[8,168,128]{2,1,0:T(8,128)(2,1)}), bf16[8,168,128]{2,1,0:T(8,128)(2,1)S(1)}, u32[]{:S(2)}, u32[]{:S(2)}) async-start(bf16[8,168,128]{2,1,0:T(8,128)(2,1)} %fusion.8), calls=%async_computation.1 | async-start | bytes 688128 | tf_op jit(solution)/shard_map/all_to_all | solution.py:19
  42.3 0.7 copy-start.14
  43.0 0.8 copy-start.13
  62.4 0.8 copy-start.11
  64.6 10.0 %copy-start.2 = (bf16[128,256]{1,0:T(8,128)(2,1)S(1)}, bf16[128,256]{1,0:T(8,128)(2,1)}, u32[]{:S(2)}) copy-start(bf16[128,256]{1,0:T(8,128)(2,1)} %grad_ref.1) | copy-start | bytes 196612
  64.6 10.0 %copy-start.12 = (bf16[256,256]{1,0:T(8,128)(2,1)S(1)}, bf16[256,256]{1,0:T(8,128)(2,1)}, u32[]{:S(2)}) copy-start(bf16[256,256]{1,0:T(8,128)(2,1)} %param.21) | copy-start | bytes 393220
  64.6 16.5 %all-to-all-start.2 = ((bf16[8,128,128]{2,1,0:T(8,128)(2,1)}), bf16[8,128,128]{2,1,0:T(8,128)(2,1)S(1)}, u32[]{:S(2)}, u32[]{:S(2)}) async-start(bf16[8,128,128]{2,1,0:T(8,128)(2,1)} %pad_maximum_fusion), calls=%async_computation.2 | async-start | bytes 524288 | tf_op jit(solution)/shard_map/all_to_all | solution.py:19
  82.6 9.6 %all-to-all-start.3 = ((bf16[8,64,128]{2,1,0:T(8,128)(2,1)}), bf16[8,64,128]{2,1,0:T(8,128)(2,1)S(1)}, u32[]{:S(2)}, u32[]{:S(2)}) async-start(bf16[8,64,128]{2,1,0:T(8,128)(2,1)} %broadcast_in_dim.565), calls=%async_computation.3 | async-start | bytes 262144 | tf_op jit(solution)/shard_map/all_to_all | solution.py:19
  121.2 12.1 %all-to-all-start.6 = ((bf16[8,336,128]{2,1,0:T(8,128)(2,1)}), bf16[8,336,128]{2,1,0:T(8,128)(2,1)S(1)}, u32[]{:S(2)}, u32[]{:S(2)}) async-start(bf16[8,336,128]{2,1,0:T(8,128)(2,1)} %broadcast_in_dim.567), calls=%async_computation.6 | async-start | bytes 1376256 | tf_op jit(solution)/shard_map/all_to_all | solution.py:19
  133.4 0.9 copy-start.4
  135.7 14.7 %all-to-all-start.7 = ((bf16[8,160,128]{2,1,0:T(8,128)(2,1)}), bf16[8,160,128]{2,1,0:T(8,128)(2,1)S(1)}, u32[]{:S(2)}, u32[]{:S(2)}) async-start(bf16[8,160,128]{2,1,0:T(8,128)(2,1)} %broadcast_in_dim.568), calls=%async_computation.7 | async-start | bytes 655360 | tf_op jit(solution)/shard_map/all_to_all | solution.py:19

commit v6 on v5

v6 whole, which is shorter than its diff:
```python
import functools

import jax
import jax.numpy as jnp
from jax import lax
from jax.experimental import pallas as pl
from jax.experimental.pallas import tpu as pltpu
from jax.sharding import PartitionSpec as P

bf16 = jnp.bfloat16
f32 = jnp.float32
VMEM_LIMIT = 16 * 1024 * 1024


def dot(a, b, dims):
    return lax.dot_general(a, b, (dims, ((), ())), preferred_element_type=f32)


def exchange(values, axis, groups=None):
    return lax.all_to_all(
        values, axis, split_axis=0, concat_axis=0, tiled=True, axis_index_groups=groups
    )


def to_all(values, count):
    return jnp.broadcast_to(values[None], (count,) + values.shape)


def pick(table, row_ids):
    local_ids = jnp.arange(table.shape[0], dtype=jnp.int32)
    chosen = (row_ids[:, None] == local_ids[None, :]).astype(table.dtype)
    return dot(chosen, table, ((1,), (0,))).astype(table.dtype)


def quarters(first, second):
    half = first.shape[1] // 2
    parts = [first[:, :half], first[:, half:], second[:, :half], second[:, half:]]
    return jnp.concatenate(parts, axis=0).astype(bf16)


def near_index(device, na, nb):
    return device // (na * nb) * nb + device % nb


def where_am_i():
    return lax.axis_index("node"), lax.axis_index("feat")


def pack_kernel(
    ids_hbm,
    slots_hbm,
    counts_hbm,
    blocks_hbm,
    features_hbm,
    tiles_hbm,
    grad_hbm,
    sent_ref,
    ids_ref,
    slots_ref,
    counts_ref,
    blocks_ref,
    features_ref,
    tiles_ref,
    grad_ref,
    slots_scratch,
    grad_scratch,
    sems,
    *,
    nx,
    na,
    nb,
    place,
):
    copies = [
        pltpu.make_async_copy(source, target, sems.at[n])
        for n, (source, target) in enumerate(
            [
                (ids_hbm, ids_ref),
                (slots_hbm, slots_ref),
                (counts_hbm, counts_ref),
                (blocks_hbm, blocks_ref),
                (features_hbm, features_ref),
                (tiles_hbm, tiles_ref),
                (grad_hbm, grad_ref),
            ]
        )
    ]
    for copy in copies:
        copy.start()
    for copy in copies:
        copy.wait()
    device, feat = place()
    near = nx * nb
    capacity, nodes = ids_ref.shape
    locals_, width = features_ref.shape
    count, targets, _ = tiles_ref.shape
    part = sent_ref.shape[1] - na * capacity - na - 8
    part = part // count
    lanes = targets // capacity
    near_at = near_index(device, na, nb)

    used = lax.broadcasted_iota(jnp.int32, (capacity, nodes), 0) < counts_ref[pl.ds(device, 1), :]
    slots = jnp.where(used, slots_ref[...], targets).astype(f32)
    slots = jnp.concatenate([slots] * lanes, axis=0)
    slots = jnp.concatenate([slots, jnp.zeros((targets, targets - nodes), f32)], axis=1).T
    group = lax.broadcasted_iota(jnp.int32, (targets, targets), 1) // capacity
    slots_scratch[...] = jnp.where(group == near_at % lanes, slots, 0.0)
    grad_scratch[...] = grad_ref[...].astype(f32).T
    grad_t = grad_scratch[pl.ds(pl.multiple_of(feat * part, part), part), :].astype(bf16)
    terms = [dot(grad_t, tiles_ref[k], ((1,), (0,))) for k in range(count)]
    blocks = [blocks_ref[0, k] for k in range(count)]
    row = lax.broadcasted_iota(jnp.int32, (8, targets), 0)
    far_rows = jnp.zeros((8, targets), jnp.int32)
    for k in range(count):
        far_rows = jnp.where(row == k, blocks[k] % (na * nb) // nb, far_rows)
        far_rows = jnp.where(row == count + k, blocks[k] // (na * nb) * nb + blocks[k] % nb, far_rows)
    far_rows = far_rows.astype(f32)
    local_ids = lax.broadcasted_iota(jnp.int32, (capacity, locals_), 1)
    for x in range(nx):
        for b in range(nb):
            to = x * nb + b
            owners = [(x * na + a) * nb + b for a in range(na)]
            chosen = jnp.concatenate(
                [jnp.where(ids_ref[:, o : o + 1] == local_ids, 1.0, 0.0).astype(bf16) for o in owners],
                axis=0,
            )
            rows = dot(chosen, features_ref[...], ((1,), (0,)))
            sent_ref[to, : na * capacity, :] = rows.astype(bf16)
            at = na * capacity
            for k in range(count):
                there = blocks[k] // (na * nb) * nb + blocks[k] % nb == to
                term = jnp.where(there, terms[k], 0.0)
                sent_ref[to, at : at + part, :] = term.astype(bf16)
                at += part
            slot_rows = slots_scratch[pl.ds(owners[0], na, stride=nb), :]
            sent_ref[to, at : at + na + 8, :] = jnp.concatenate([slot_rows, far_rows], 0).astype(bf16)


def pack(sample_ids, dest_slots, counts, blocks, features, tiles, grad, nx, na, nb, part, place):
    count, targets, _ = tiles.shape
    capacity, nodes = sample_ids.shape
    total = na * capacity + count * part + na + 8
    kernel = functools.partial(pack_kernel, nx=nx, na=na, nb=nb, place=place)
    args = (sample_ids, dest_slots, counts, blocks, features, tiles, grad)
    held = [pltpu.VMEM(arg.shape, arg.dtype) for arg in args]
    held[3] = pltpu.SMEM(blocks.shape, blocks.dtype)
    return pl.pallas_call(
        kernel,
        out_shape=jax.ShapeDtypeStruct((nx * nb, total, features.shape[1]), bf16),
        in_specs=[pl.BlockSpec(memory_space=pltpu.HBM)] * len(args),
        out_specs=pl.BlockSpec(memory_space=pltpu.VMEM),
        scratch_shapes=held
        + [
            pltpu.VMEM((targets, targets), f32),
            pltpu.VMEM((grad.shape[1], targets), f32),
            pltpu.SemaphoreType.DMA((len(args),)),
        ],
        compiler_params=pltpu.CompilerParams(vmem_limit_bytes=VMEM_LIMIT),
    )(*args)


def in_vmem(kernel, out_shape, *args):
    vmem = pl.BlockSpec(memory_space=pltpu.VMEM)
    many = isinstance(out_shape, (list, tuple))
    return pl.pallas_call(
        kernel,
        out_shape=out_shape,
        in_specs=[vmem] * len(args),
        out_specs=[vmem] * len(out_shape) if many else vmem,
        compiler_params=pltpu.CompilerParams(vmem_limit_bytes=VMEM_LIMIT),
    )(*args)


def halve(values):
    high = values.astype(bf16)
    return high, (values - high.astype(f32)).astype(bf16)


def gather_kernel(got_ref, sent_ref, *, capacity, part, count):
    near = got_ref.shape[0]
    far, _, targets = sent_ref.shape
    lanes = targets // capacity
    at = far * capacity + count * part
    marks = [got_ref[n, at : at + far + 8, :].astype(f32) for n in range(near)]
    slots = [sum(marks[h : h + lanes])[:far] for h in range(0, near, lanes)]
    nodes = lax.broadcasted_iota(jnp.int32, (targets, targets), 0).astype(f32)
    ones = jnp.ones((8, targets), bf16)
    back = [jnp.zeros((part, targets), f32) for _ in range(far)]
    for n in range(near):
        for k in range(count):
            start = far * capacity + k * part
            term = got_ref[n, start : start + part, :].astype(f32)
            mark = jnp.broadcast_to(marks[n][far + k : far + k + 1, :], (part, targets))
            back = [back[a] + jnp.where(mark == float(a), term, 0.0) for a in range(far)]
    for a in range(far):
        total = jnp.zeros((targets, targets), f32)
        degree = jnp.zeros((8, targets), f32)
        for h in range(near // lanes):
            chosen = jnp.where(slots[h][a : a + 1, :] == nodes, 1.0, 0.0).astype(bf16)
            rows = [
                got_ref[h * lanes + n, a * capacity : (a + 1) * capacity, :] for n in range(lanes)
            ]
            total += dot(chosen, jnp.concatenate(rows, axis=0), ((1,), (0,)))
            degree += dot(ones, chosen, ((1,), (1,)))
        sent_ref[a] = jnp.concatenate([total, back[a], degree], axis=0).astype(bf16)


def first_kernel(came_ref, rows_ref, self_ref, other_ref, sent_ref, mean_ref, *, part):
    targets = rows_ref.shape[0]
    came = came_ref[0].astype(f32)
    for a in range(1, came_ref.shape[0]):
        came += came_ref[a].astype(f32)
    degree = jnp.broadcast_to(came[targets + part : targets + part + 1, :], (targets, targets)).T
    high, low = halve(came[:targets] / (degree + 1.0))
    mean_ref[...] = high
    pre = dot(rows_ref[...], self_ref[...], ((1,), (0,)))
    pre += dot(high, other_ref[...], ((1,), (0,)))
    pre += dot(low, other_ref[...], ((1,), (0,)))
    pre_high, pre_low = halve(pre.T)
    back = jnp.concatenate(halve(came[targets : targets + part]), axis=0)
    for f in range(sent_ref.shape[0]):
        mine = slice(f * part, (f + 1) * part)
        sent_ref[f] = jnp.concatenate([pre_high[mine], pre_low[mine], back], axis=0)


def hidden_kernel(got_ref, self_ref, other_ref, grad_ref, sent_ref, *, part):
    feats = got_ref.shape[0]
    pre = jnp.zeros((part, got_ref.shape[2]), f32)
    for f in range(feats):
        pre += got_ref[f, :part, :].astype(f32) + got_ref[f, part : 2 * part, :].astype(f32)
    sigma = 1.0 / (1.0 + jnp.exp(-pre))
    slope = sigma * (1.0 + pre * (1.0 - sigma))
    back_high = jnp.concatenate([got_ref[f, 2 * part : 3 * part, :] for f in range(feats)], axis=0)
    back_low = jnp.concatenate([got_ref[f, 3 * part :, :] for f in range(feats)], axis=0)
    grad = dot(self_ref[...], grad_ref[...], ((1,), (1,)))
    grad += dot(other_ref[...], back_high, ((1,), (0,)))
    grad += dot(other_ref[...], back_low, ((1,), (0,)))
    both = jnp.concatenate([grad * slope, pre * sigma], axis=0).astype(bf16)
    for f in range(feats):
        sent_ref[f] = both


def near_kernel(got_ref, marks_ref, sent_ref, *, sums, part, count, where):
    far = got_ref.shape[0]
    total = got_ref[0, :sums, :].astype(f32)
    for a in range(1, far):
        total += got_ref[a, :sums, :].astype(f32)
    total = total.astype(bf16)
    here = where().astype(f32)
    blocks = [got_ref[a, sums:, :].astype(f32) for a in range(far)]
    for n in range(sent_ref.shape[0]):
        sent_ref[n, :sums, :] = total
        marks = marks_ref[n].astype(f32)
        for k in range(count):
            mark = jnp.where(marks[far + count + k :][:1] == here, marks[far + k :][:1], -1.0)
            mark = jnp.broadcast_to(mark, blocks[0].shape)
            block = jnp.zeros_like(blocks[0])
            for a in range(far):
                block = jnp.where(mark == float(a), blocks[a], block)
            at = sums + k * part
            sent_ref[n, at : at + part, :] = block.astype(bf16)


def second_kernel(got_ref, tiles_ref, sent_ref, *, rows_each, share, part):
    near = got_ref.shape[0]
    agg = jnp.zeros((part, tiles_ref.shape[1]), f32)
    for k in range(tiles_ref.shape[0]):
        at = rows_each + share + k * part
        block = got_ref[0, at : at + part, :].astype(f32)
        for n in range(1, near):
            block += got_ref[n, at : at + part, :].astype(f32)
        agg += dot(block.astype(bf16), tiles_ref[k], ((1,), (1,)))
    rows = [got_ref[n, rows_each : rows_each + share, :] for n in range(near)]
    both = jnp.concatenate([agg.astype(bf16)] + rows, axis=0)
    for f in range(sent_ref.shape[0]):
        sent_ref[f] = both


def last_kernel(got_ref, hidden_ref, self_ref, other_ref, out_ref, first_ref, second_ref, *, part):
    feats = got_ref.shape[0]
    half = first_ref.shape[1] // 2
    agg = jnp.concatenate([got_ref[f, :part, :] for f in range(feats)], axis=0)
    out = dot(hidden_ref[...], self_ref[...], ((0,), (0,))) + dot(agg, other_ref[...], ((0,), (0,)))
    out_ref[...] = out.astype(bf16)
    for f in range(feats):
        at = f * part
        for n, ref in enumerate([first_ref, second_ref]):
            start = part * (1 + 2 * n)
            ref[at : at + part, :half] = got_ref[f, start : start + part, :].astype(f32)
            ref[at : at + part, half:] = got_ref[f, start + part : start + 2 * part, :].astype(f32)


def shards(
    features,
    self_one,
    neighbour_one,
    sample_ids,
    dest_slots,
    send_counts,
    self_ids,
    tile_blocks,
    tile_weights,
    self_two,
    neighbour_two,
    out_grad,
):
    feats = lax.axis_size("feat")
    nodes = lax.axis_size("node")
    nx, nb = 4, 2
    na = nodes // (nx * nb)
    near = nx * nb
    near_ids = [(x * na + a) * nb + b for a in range(na) for x in range(nx) for b in range(nb)]
    near_groups = [near_ids[a * near : (a + 1) * near] for a in range(na)]
    far_groups = [list(group) for group in zip(*near_groups)]
    feat = lax.axis_index("feat")
    capacity = sample_ids.shape[2]
    targets = self_ids.shape[1]
    width = features.shape[1]
    hidden = neighbour_one.shape[1]
    part = hidden // feats
    tiles = tile_weights[0]
    count = tiles.shape[0]

    sent = pack(
        sample_ids[0].T,
        dest_slots[0].T,
        send_counts,
        tile_blocks,
        features,
        tiles,
        out_grad,
        nx,
        na,
        nb,
        part,
        where_am_i,
    )
    got = exchange(sent, "node", near_groups)

    marks = got[:, na * capacity + count * part :]
    sent = in_vmem(
        functools.partial(gather_kernel, capacity=capacity, part=part, count=count),
        jax.ShapeDtypeStruct((na, targets + part + 8, width), bf16),
        got,
    )
    came = exchange(sent, "node", far_groups)

    self_rows = pick(features, self_ids[0])
    sent, mean_high = in_vmem(
        functools.partial(first_kernel, part=part),
        [
            jax.ShapeDtypeStruct((feats, 4 * part, targets), bf16),
            jax.ShapeDtypeStruct((targets, width), bf16),
        ],
        came,
        self_rows,
        self_one,
        neighbour_one,
    )
    got = exchange(sent, "feat")
    back_high = got[:, 2 * part : 3 * part].reshape(hidden, targets)
    back_low = got[:, 3 * part :].reshape(hidden, targets)

    self_two_part = lax.dynamic_slice_in_dim(self_two, feat * part, part, 0)
    neighbour_two_part = lax.dynamic_slice_in_dim(neighbour_two, feat * part, part, 0)
    sent = in_vmem(
        functools.partial(hidden_kernel, part=part),
        jax.ShapeDtypeStruct((feats, 2 * part, targets), bf16),
        got,
        self_two_part,
        neighbour_two_part,
        out_grad,
    )
    hidden_part = sent[0, part:]
    full = exchange(sent, "feat")
    pre_round = full[:, :part].reshape(hidden, targets)
    hidden_t = full[:, part:].reshape(hidden, targets)

    half = hidden // 2
    upper = quarters(
        dot(hidden_part, out_grad, ((1,), (0,))),
        dot(hidden_part, back_high, ((1,), (1,))) + dot(hidden_part, back_low, ((1,), (1,))),
    )
    lower = quarters(
        dot(self_rows, pre_round, ((0,), (1,))), dot(mean_high, pre_round, ((0,), (1,)))
    )
    share = upper.shape[0] // near
    rows_each = lower.shape[0] // near
    sent = [lower.reshape(near, rows_each, half), upper.reshape(near, share, half)]
    got = exchange(jnp.concatenate(sent, axis=1), "node", near_groups).astype(f32)
    sent = [jnp.sum(got, axis=0).astype(bf16), hidden_part]
    got = exchange(to_all(jnp.concatenate(sent, axis=0), na), "node", far_groups)
    sums = rows_each + share
    sent = in_vmem(
        functools.partial(
            near_kernel,
            sums=sums,
            part=part,
            count=count,
            where=lambda: near_index(lax.axis_index("node"), na, nb),
        ),
        jax.ShapeDtypeStruct((near, sums + count * part, half), bf16),
        got,
        marks,
    )
    got = exchange(sent, "node", near_groups)
    lower = got[:, :rows_each].reshape(4, width, half).astype(f32)

    sent = in_vmem(
        functools.partial(second_kernel, rows_each=rows_each, share=share, part=part),
        jax.ShapeDtypeStruct((feats, part + near * share, targets), bf16),
        got,
        tiles,
    )
    got = exchange(sent, "feat")
    layer_output, upper_self, upper_others = in_vmem(
        functools.partial(last_kernel, part=part),
        [
            jax.ShapeDtypeStruct((targets, hidden), bf16),
            jax.ShapeDtypeStruct((hidden, hidden), f32),
            jax.ShapeDtypeStruct((hidden, hidden), f32),
        ],
        got,
        hidden_t,
        self_two,
        neighbour_two,
    )

    def halves(which):
        return jnp.concatenate([lower[2 * which], lower[2 * which + 1]], axis=1)

    return (layer_output, halves(0), halves(1), upper_self, upper_others)


def solution(mesh):
    placed = (
        P("node", "feat"),
        P("feat", None),
        P("feat", None),
        P("node", None, None),
        P("node", None, None),
        P(),
        P("node", None),
        P("node", None),
        P("node", None, None, None),
        P(),
        P(),
        P("node", None),
    )
    return jax.shard_map(
        shards,
        mesh=mesh,
        in_specs=placed,
        out_specs=(P("node", None), P("feat", None), P("feat", None), P(), P()),
        check_vma=False,
    )
```

time: 154 us -> 150 us (0.974)
  waiting for transfers between devices: 35.8 us -> 56.9 us
  blocking collectives: 43.5 us -> 25.7 us
  between operations: 8.94 us -> 0.81 us
  Pallas kernels: 1.42 us -> 6.89 us
  local copies, waits for them, and re-layouts: 11.9 us -> 7.67 us
  starting transfers between devices: 41.6 us -> 45.4 us
  other arithmetic: 5.71 us -> 2.08 us
    all_to_all x5 -> x6, waiting for transfers between devices: 35.8 us -> 56.9 us  [exchange(): lax.all_to_all(values, axis, split_axis=0, concat_axis=0, tiled=True, axi...]
    all_to_all x3 -> x2, blocking collectives: 43.5 us -> 25.7 us  [exchange(): lax.all_to_all(values, axis, split_axis=0, concat_axis=0, tiled=True, axi...]
    pallas_call x0 -> x6, Pallas kernels: none -> 5.36 us  [in_vmem(): pl.pallas_call(kernel, out_shape=out_shape, in_specs=[vmem] * len(args),...]
    all_to_all x5 -> x6, starting transfers between devices: 41.6 us -> 45.4 us  [exchange(): lax.all_to_all(values, axis, split_axis=0, concat_axis=0, tiled=True, axi...]
    unnamed x30, local copies, waits for them, and re-layouts: 8.43 us -> 6.16 us
    concatenate x7 -> x2, other arithmetic: 3.52 us -> 1.33 us  [halves(): return jnp.concatenate([lower[2 * which], lower[2 * which + 1]], axis=1)]
    broadcast_in_dim x6 -> x1, local copies, waits for them, and re-layouts: 2.44 us -> 0.72 us  [to_all(): return jnp.broadcast_to(values[None], (count,) + values.shape)]
    dot_general x18 -> x6, matrix products: 3.67 us -> 3.12 us  [dot(): return lax.dot_general(a, b, (dims, ((), ())), preferred_element_type=f32)]
  transfers between devices with their start and end apart: 5 -> 6, of which waited for: 4 -> 6; matrix products, arithmetic and copies ran while one was open for 2% -> 3% of each run, Pallas kernels for 0% -> 0%
where the time goes in v6:
time: 150 us; the launch traced here: 149 us
  waiting for transfers between devices  56.9 us (38%)
  starting transfers between devices  45.4 us (30%)
  blocking collectives  25.7 us (17%)
  local copies, waits for them, and re-layouts  7.67 us (5%)
  Pallas kernels  6.89 us (5%)
  matrix products  3.12 us (2%)
  other arithmetic  2.08 us (1%)
    all_to_all x6, waiting for transfers between devices, exchange(): lax.all_to_all(values, axis, split_axis=0, concat_axis=0, tiled=True, axi...  56.9 us
    all_to_all x6, starting transfers between devices, exchange(): lax.all_to_all(values, axis, split_axis=0, concat_axis=0, tiled=True, axi...  45.4 us
    all_to_all x2, blocking collectives, exchange(): lax.all_to_all(values, axis, split_axis=0, concat_axis=0, tiled=True, axi...  25.7 us
    unnamed x30, local copies, waits for them, and re-layouts  6.16 us
    pallas_call x6, Pallas kernels, in_vmem(): pl.pallas_call(kernel, out_shape=out_shape, in_specs=[vmem] * len(args),...  5.36 us
    dot_general x6, matrix products, dot(): return lax.dot_general(a, b, (dims, ((), ())), preferred_element_type=f32)  3.12 us
  transfers between devices with their start and end apart: 6, of which 6 were waited for; matrix products, arithmetic and copies ran while one was open for 3% of the time, Pallas kernels for 0%

profile of v6, /device:TPU:1, one launch (start us, length us, event | category | flops | bytes accessed | tf_op | source)
XLA Modules:
  0.0 148.6 jit_solution(8410195588091054537)
XLA Ops:
  0.6 0.0 copy-start.13
  0.6 0.6 copy-done.13
  1.3 0.0 copy-start
  1.3 0.8 copy-done
  2.1 0.0 copy-start.2
  2.1 0.9 copy-done.2
  3.0 0.0 copy-start.6
  3.0 0.9 copy-done.6
  3.9 0.0 copy-start.10
  3.9 0.8 copy-done.10
  4.7 0.0 copy-start.11
  4.7 0.7 copy-done.11
  5.4 0.0 copy-start.12
  5.4 0.7 copy-done.12
  6.1 1.5 %shard_map.155 = bf16[8,400,128]{2,1,0:T(8,128)(2,1)S(1)} custom-call(s32[32,64]{1,0:T(8,128)S(1)} %bitcast.34, s32[32,64]{1,0:T(8,128)S(1)} %bitcast.35, s32[64,64]{1,0:T(8,128)S(1)} %copy-done.10, s32[1,4]{1,0:T(1,128)S(1)} %copy-done.13, bf16[512,128]{1,0:T(8,128)(2,1)S(1)} %copy-done.6, bf16[4,128,128]{2,1,0:T(8,128)(2,1)S(1)} %bitcast.31, ...), custom_call_target="tpu_custom_call" | custom-call | tf_op jit(solution)/shard_map/pallas_call | solution.py:147
  7.7 16.1 %all_to_all.40.got_ref = bf16[8,400,128]{2,1,0:T(8,128)(2,1)S(1)} all-to-all(bf16[8,400,128]{2,1,0:T(8,128)(2,1)S(1)} %shard_map.155), channel_id=1, replica_groups={{0,1,16,17,32,33,48,49},{2,3,18,19,34,35,50,51},{4,5,20,21,36,37,52,53}..., dimensions={0} | all-to-all | bytes 1638400 | tf_op jit(solution)/shard_map/all_to_all | solution.py:20
  23.8 1.4 shard_map.156
  25.2 0.0 copy-start.7
  25.2 16.1 %all-to-all-start.1 = ((bf16[8,168,128]{2,1,0:T(8,128)(2,1)}), bf16[8,168,128]{2,1,0:T(8,128)(2,1)S(1)}, u32[]{:S(2)}, u32[]{:S(2)}) async-start(bf16[8,168,128]{2,1,0:T(8,128)(2,1)} %shard_map.156), calls=%async_computation.1 | async-start | bytes 688128 | tf_op jit(solution)/shard_map/all_to_all | solution.py:20
  41.4 0.0 copy-start.14
  41.4 0.0 copy-done.7
  41.4 0.6 copy-done.14
  42.0 0.0 copy-start.8
  42.0 0.0 copy-start.9
  42.0 0.2 convolution_convert_fusion.2.rows_ref
  42.3 19.1 %all-to-all-done.1.came_ref = bf16[8,168,128]{2,1,0:T(8,128)(2,1)S(1)} async-done(((bf16[8,168,128]{2,1,0:T(8,128)(2,1)}), bf16[8,168,128]{2,1,0:T(8,128)(2,1)S(1)}, u32[]{:S(2)}, u32[]{:S(2)}) %all-to-all-start.1) | async-done | bytes 344096 | tf_op jit(solution)/shard_map/all_to_all | solution.py:20
  61.4 0.0 copy-done.8
  61.4 0.0 copy-done.9
  61.4 1.0 shard_map.157
  62.4 0.0 copy-start.4
  62.4 0.0 copy-start.5
  62.4 10.0 %all-to-all-start.2 = ((bf16[8,128,128]{2,1,0:T(8,128)(2,1)}), bf16[8,128,128]{2,1,0:T(8,128)(2,1)S(1)}, u32[]{:S(2)}, u32[]{:S(2)}) async-start(bf16[8,128,128]{2,1,0:T(8,128)(2,1)} %get-tuple-element.10), calls=%async_computation.2 | async-start | bytes 524288 | tf_op jit(solution)/shard_map/all_to_all | solution.py:20
  72.5 0.0 copy-start.1
  72.5 0.0 copy-done.4
  72.5 0.0 copy-done.5
  72.5 6.5 %all-to-all-done.2.got_ref = bf16[8,128,128]{2,1,0:T(8,128)(2,1)S(1)} async-done(((bf16[8,128,128]{2,1,0:T(8,128)(2,1)}), bf16[8,128,128]{2,1,0:T(8,128)(2,1)S(1)}, u32[]{:S(2)}, u32[]{:S(2)}) %all-to-all-start.2) | async-done | bytes 262176 | tf_op jit(solution)/shard_map/all_to_all | solution.py:20
  79.0 0.0 copy-done.1
  79.0 0.8 shard_map.158
  79.8 0.8 convolution_convert_fusion.3
  80.6 4.3 %all-to-all-start.3 = ((bf16[8,64,128]{2,1,0:T(8,128)(2,1)}), bf16[8,64,128]{2,1,0:T(8,128)(2,1)S(1)}, u32[]{:S(2)}, u32[]{:S(2)}) async-start(bf16[8,64,128]{2,1,0:T(8,128)(2,1)} %shard_map.158), calls=%async_computation.3 | async-start | bytes 262144 | tf_op jit(solution)/shard_map/all_to_all | solution.py:20
  84.9 0.8 fusion.2
  85.8 0.8 fusion
  86.7 3.6 %all-to-all-done.3 = bf16[8,64,128]{2,1,0:T(8,128)(2,1)S(1)} async-done(((bf16[8,64,128]{2,1,0:T(8,128)(2,1)}), bf16[8,64,128]{2,1,0:T(8,128)(2,1)S(1)}, u32[]{:S(2)}, u32[]{:S(2)}) %all-to-all-start.3) | async-done | bytes 131104 | tf_op jit(solution)/shard_map/all_to_all | solution.py:20
  90.2 0.2 convolution_convert_fusion.1
  90.4 0.2 convolution_convert_fusion
  90.7 0.7 pad_maximum_fusion
  91.4 3.4 %all-to-all-start.4 = ((bf16[8,80,128]{2,1,0:T(8,128)(2,1)}), bf16[8,80,128]{2,1,0:T(8,128)(2,1)S(1)}, u32[]{:S(2)}, u32[]{:S(2)}) async-start(bf16[8,80,128]{2,1,0:T(8,128)(2,1)} %pad_maximum_fusion), calls=%async_computation.4 | async-start | bytes 327680 | tf_op jit(solution)/shard_map/all_to_all | solution.py:20
  94.7 0.7 slice_bitcast_fusion
  95.4 5.0 %all-to-all-done.4 = bf16[8,80,128]{2,1,0:T(8,128)(2,1)S(1)} async-done(((bf16[8,80,128]{2,1,0:T(8,128)(2,1)}), bf16[8,80,128]{2,1,0:T(8,128)(2,1)S(1)}, u32[]{:S(2)}, u32[]{:S(2)}) %all-to-all-start.4) | async-done | bytes 163872 | tf_op jit(solution)/shard_map/all_to_all | solution.py:20
  100.5 0.7 broadcast_in_dim.2
  101.2 3.4 %all-to-all-start.5 = ((bf16[8,112,128]{2,1,0:T(8,128)(2,1)}), bf16[8,112,128]{2,1,0:T(8,128)(2,1)S(1)}, u32[]{:S(2)}, u32[]{:S(2)}) async-start(bf16[8,112,128]{2,1,0:T(8,128)(2,1)} %broadcast_in_dim.2), calls=%async_computation.5 | async-start | bytes 458752 | tf_op jit(solution)/shard_map/all_to_all | solution.py:20
  104.6 17.0 %all-to-all-done.5.got_ref = bf16[8,112,128]{2,1,0:T(8,128)(2,1)S(1)} async-done(((bf16[8,112,128]{2,1,0:T(8,128)(2,1)}), bf16[8,112,128]{2,1,0:T(8,128)(2,1)S(1)}, u32[]{:S(2)}, u32[]{:S(2)}) %all-to-all-start.5) | async-done | bytes 229408 | tf_op jit(solution)/shard_map/all_to_all | solution.py:20
  121.6 0.2 shard_map.159
  121.8 0.0 copy-start.3
  121.8 9.6 %all_to_all.41.got_ref = bf16[8,208,128]{2,1,0:T(8,128)(2,1)S(1)} all-to-all(bf16[8,208,128]{2,1,0:T(8,128)(2,1)S(1)} %shard_map.159), channel_id=1, replica_groups={{0,1,16,17,32,33,48,49},{2,3,18,19,34,35,50,51},{4,5,20,21,36,37,52,53}..., dimensions={0} | all-to-all | bytes 851968 | tf_op jit(solution)/shard_map/all_to_all | solution.py:20
  131.5 0.0 copy-done.3
  131.5 0.9 shard_map.160
  132.4 8.2 %all-to-all-start.7 = ((bf16[8,160,128]{2,1,0:T(8,128)(2,1)}), bf16[8,160,128]{2,1,0:T(8,128)(2,1)S(1)}, u32[]{:S(2)}, u32[]{:S(2)}) async-start(bf16[8,160,128]{2,1,0:T(8,128)(2,1)} %shard_map.160), calls=%async_computation.7 | async-start | bytes 655360 | tf_op jit(solution)/shard_map/all_to_all | solution.py:20
  140.6 0.7 pad_maximum_fusion.2
  141.3 0.7 pad_maximum_fusion.3
  141.9 5.8 %all-to-all-done.7.got_ref = bf16[8,160,128]{2,1,0:T(8,128)(2,1)S(1)} async-done(((bf16[8,160,128]{2,1,0:T(8,128)(2,1)}), bf16[8,160,128]{2,1,0:T(8,128)(2,1)S(1)}, u32[]{:S(2)}, u32[]{:S(2)}) %all-to-all-start.7) | async-done | bytes 327712 | tf_op jit(solution)/shard_map/all_to_all | solution.py:20
  147.7 0.9 shard_map.161
  (14 shorter events, 0.2 us)
Async XLA Ops:
  0.6 0.7 copy-start.13
  1.3 0.8 copy-start
  2.1 0.9 copy-start.2
  3.0 0.9 copy-start.6
  3.9 0.8 copy-start.10
  4.7 0.7 copy-start.11
  5.4 0.7 copy-start.12
  25.2 16.1 %copy-start.7 = (bf16[512,128]{1,0:T(8,128)(2,1)S(1)}, bf16[512,128]{1,0:T(8,128)(2,1)}, u32[]{:S(2)}) copy-start(bf16[512,128]{1,0:T(8,128)(2,1)} %features_hbm.1) | copy-start | bytes 393220
  25.2 36.1 %all-to-all-start.1 = ((bf16[8,168,128]{2,1,0:T(8,128)(2,1)}), bf16[8,168,128]{2,1,0:T(8,128)(2,1)S(1)}, u32[]{:S(2)}, u32[]{:S(2)}) async-start(bf16[8,168,128]{2,1,0:T(8,128)(2,1)} %shard_map.156), calls=%async_computation.1 | async-start | bytes 688128 | tf_op jit(solution)/shard_map/all_to_all | solution.py:20
  41.4 0.7 copy-start.14
  42.0 19.4 %copy-start.8 = (bf16[128,256]{1,0:T(8,128)(2,1)S(1)}, bf16[128,256]{1,0:T(8,128)(2,1)}, u32[]{:S(2)}) copy-start(bf16[128,256]{1,0:T(8,128)(2,1)} %self_ref.2) | copy-start | bytes 196612
  42.0 19.4 %copy-start.9 = (bf16[128,256]{1,0:T(8,128)(2,1)S(1)}, bf16[128,256]{1,0:T(8,128)(2,1)}, u32[]{:S(2)}) copy-start(bf16[128,256]{1,0:T(8,128)(2,1)} %other_ref.2) | copy-start | bytes 196612
  62.4 10.0 %copy-start.4 = (bf16[256,256]{1,0:T(8,128)(2,1)S(1)}, bf16[256,256]{1,0:T(8,128)(2,1)}, u32[]{:S(2)}) copy-start(bf16[256,256]{1,0:T(8,128)(2,1)} %other_ref.3) | copy-start | bytes 393220
  62.4 10.0 %copy-start.5 = (bf16[256,256]{1,0:T(8,128)(2,1)S(1)}, bf16[256,256]{1,0:T(8,128)(2,1)}, u32[]{:S(2)}) copy-start(bf16[256,256]{1,0:T(8,128)(2,1)} %self_ref.3) | copy-start | bytes 393220
  62.4 16.5 %all-to-all-start.2 = ((bf16[8,128,128]{2,1,0:T(8,128)(2,1)}), bf16[8,128,128]{2,1,0:T(8,128)(2,1)S(1)}, u32[]{:S(2)}, u32[]{:S(2)}) async-start(bf16[8,128,128]{2,1,0:T(8,128)(2,1)} %get-tuple-element.10), calls=%async_computation.2 | async-start | bytes 524288 | tf_op jit(solution)/shard_map/all_to_all | solution.py:20
  72.5 6.5 %copy-start.1 = (bf16[128,256]{1,0:T(8,128)(2,1)S(1)}, bf16[128,256]{1,0:T(8,128)(2,1)}, u32[]{:S(2)}) copy-start(bf16[128,256]{1,0:T(8,128)(2,1)} %grad_ref.1) | copy-start | bytes 196612
  80.6 9.6 %all-to-all-start.3 = ((bf16[8,64,128]{2,1,0:T(8,128)(2,1)}), bf16[8,64,128]{2,1,0:T(8,128)(2,1)S(1)}, u32[]{:S(2)}, u32[]{:S(2)}) async-start(bf16[8,64,128]{2,1,0:T(8,128)(2,1)} %shard_map.158), calls=%async_computation.3 | async-start | bytes 262144 | tf_op jit(solution)/shard_map/all_to_all | solution.py:20
  91.4 9.1 %all-to-all-start.4 = ((bf16[8,80,128]{2,1,0:T(8,128)(2,1)}), bf16[8,80,128]{2,1,0:T(8,128)(2,1)S(1)}, u32[]{:S(2)}, u32[]{:S(2)}) async-start(bf16[8,80,128]{2,1,0:T(8,128)(2,1)} %pad_maximum_fusion), calls=%async_computation.4 | async-start | bytes 327680 | tf_op jit(solution)/shard_map/all_to_all | solution.py:20
  101.2 20.4 %all-to-all-start.5 = ((bf16[8,112,128]{2,1,0:T(8,128)(2,1)}), bf16[8,112,128]{2,1,0:T(8,128)(2,1)S(1)}, u32[]{:S(2)}, u32[]{:S(2)}) async-start(bf16[8,112,128]{2,1,0:T(8,128)(2,1)} %broadcast_in_dim.2), calls=%async_computation.5 | async-start | bytes 458752 | tf_op jit(solution)/shard_map/all_to_all | solution.py:20
  121.8 9.6 %copy-start.3 = (bf16[1,4,128,128]{3,2,1,0:T(8,128)(2,1)S(1)}, bf16[1,4,128,128]{3,2,1,0:T(8,128)(2,1)}, u32[]{:S(2)}) copy-start(bf16[1,4,128,128]{3,2,1,0:T(8,128)(2,1)} %param.20) | copy-start | bytes 393220
  132.4 15.3 %all-to-all-start.7 = ((bf16[8,160,128]{2,1,0:T(8,128)(2,1)}), bf16[8,160,128]{2,1,0:T(8,128)(2,1)S(1)}, u32[]{:S(2)}, u32[]{:S(2)}) async-start(bf16[8,160,128]{2,1,0:T(8,128)(2,1)} %shard_map.160), calls=%async_computation.7 | async-start | bytes 655360 | tf_op jit(solution)/shard_map/all_to_all | solution.py:20

commit v7 on v6

--- a/solution.py
+++ b/solution.py
@@ -10,6 +10,7 @@
 bf16 = jnp.bfloat16
 f32 = jnp.float32
 VMEM_LIMIT = 16 * 1024 * 1024
+PACK_LIMIT = 60 * 1024 * 1024
 
 
 def dot(a, b, dims):
@@ -20,10 +21,6 @@
     return lax.all_to_all(
         values, axis, split_axis=0, concat_axis=0, tiled=True, axis_index_groups=groups
     )
-
-
-def to_all(values, count):
-    return jnp.broadcast_to(values[None], (count,) + values.shape)
 
 
 def pick(table, row_ids):
@@ -155,7 +152,7 @@
             pltpu.VMEM((grad.shape[1], targets), f32),
             pltpu.SemaphoreType.DMA((len(args),)),
         ],
-        compiler_params=pltpu.CompilerParams(vmem_limit_bytes=VMEM_LIMIT),
+        compiler_params=pltpu.CompilerParams(vmem_limit_bytes=PACK_LIMIT),
     )(*args)
 
 
@@ -238,6 +235,41 @@
     both = jnp.concatenate([grad * slope, pre * sigma], axis=0).astype(bf16)
     for f in range(feats):
         sent_ref[f] = both
+
+
+def grads_kernel(
+    full_ref, rows_ref, mean_ref, hidden_ref, back_ref, grad_ref, sent_ref, *, part
+):
+    feats, near = full_ref.shape[0], sent_ref.shape[0]
+    half = sent_ref.shape[2]
+    pre = jnp.concatenate([full_ref[f, :part, :] for f in range(feats)], axis=0)
+    hidden = hidden_ref[0, part:, :]
+    back_high = jnp.concatenate(
+        [back_ref[f, 2 * part : 3 * part, :] for f in range(feats)], axis=0
+    )
+    back_low = jnp.concatenate([back_ref[f, 3 * part :, :] for f in range(feats)], axis=0)
+    rows_t = rows_ref[...].astype(f32).T.astype(bf16)
+    mean_t = mean_ref[...].astype(f32).T.astype(bf16)
+    lower = quarters(dot(rows_t, pre, ((1,), (1,))), dot(mean_t, pre, ((1,), (1,))))
+    upper = quarters(
+        dot(hidden, grad_ref[...], ((1,), (0,))),
+        dot(hidden, back_high, ((1,), (1,))) + dot(hidden, back_low, ((1,), (1,))),
+    )
+    rows_each, share = lower.shape[0] // near, upper.shape[0] // near
+    for n in range(near):
+        sent_ref[n, :rows_each, :] = lower[n * rows_each : (n + 1) * rows_each]
+        sent_ref[n, rows_each:, :] = upper[n * share : (n + 1) * share]
+
+
+def far_kernel(got_ref, hidden_ref, sent_ref, *, part):
+    total = got_ref[0].astype(f32)
+    for n in range(1, got_ref.shape[0]):
+        total += got_ref[n].astype(f32)
+    total = total.astype(bf16)
+    sums = total.shape[0]
+    for a in range(sent_ref.shape[0]):
+        sent_ref[a, :sums, :] = total
+        sent_ref[a, sums:, :] = hidden_ref[0, part:, :]
 
 
 def near_kernel(got_ref, marks_ref, sent_ref, *, sums, part, count, where):
@@ -357,39 +389,42 @@
         self_one,
         neighbour_one,
     )
-    got = exchange(sent, "feat")
-    back_high = got[:, 2 * part : 3 * part].reshape(hidden, targets)
-    back_low = got[:, 3 * part :].reshape(hidden, targets)
+    back = exchange(sent, "feat")
 
     self_two_part = lax.dynamic_slice_in_dim(self_two, feat * part, part, 0)
     neighbour_two_part = lax.dynamic_slice_in_dim(neighbour_two, feat * part, part, 0)
     sent = in_vmem(
         functools.partial(hidden_kernel, part=part),
         jax.ShapeDtypeStruct((feats, 2 * part, targets), bf16),
-        got,
+        back,
         self_two_part,
         neighbour_two_part,
         out_grad,
     )
-    hidden_part = sent[0, part:]
+    hidden_part = sent
     full = exchange(sent, "feat")
-    pre_round = full[:, :part].reshape(hidden, targets)
     hidden_t = full[:, part:].reshape(hidden, targets)
 
     half = hidden // 2
-    upper = quarters(
-        dot(hidden_part, out_grad, ((1,), (0,))),
-        dot(hidden_part, back_high, ((1,), (1,))) + dot(hidden_part, back_low, ((1,), (1,))),
-    )
-    lower = quarters(
-        dot(self_rows, pre_round, ((0,), (1,))), dot(mean_high, pre_round, ((0,), (1,)))
-    )
-    share = upper.shape[0] // near
-    rows_each = lower.shape[0] // near
-    sent = [lower.reshape(near, rows_each, half), upper.reshape(near, share, half)]
-    got = exchange(jnp.concatenate(sent, axis=1), "node", near_groups).astype(f32)
-    sent = [jnp.sum(got, axis=0).astype(bf16), hidden_part]
-    got = exchange(to_all(jnp.concatenate(sent, axis=0), na), "node", far_groups)
+    rows_each, share = 4 * width // near, 4 * part // near
+    sent = in_vmem(
+        functools.partial(grads_kernel, part=part),
+        jax.ShapeDtypeStruct((near, rows_each + share, half), bf16),
+        full,
+        self_rows,
+        mean_high,
+        hidden_part,
+        back,
+        out_grad,
+    )
+    got = exchange(sent, "node", near_groups)
+    sent = in_vmem(
+        functools.partial(far_kernel, part=part),
+        jax.ShapeDtypeStruct((na, rows_each + share + part, half), bf16),
+        got,
+        hidden_part,
+    )
+    got = exchange(sent, "node", far_groups)
     sums = rows_each + share
     sent = in_vmem(
         functools.partial(

time: 150 us -> 143 us (0.953)
  local copies, waits for them, and re-layouts: 7.67 us -> 0.71 us
  blocking collectives: 25.7 us -> 32.4 us
  matrix products: 3.12 us -> 0.23 us
  starting transfers between devices: 45.4 us -> 42.6 us
  Pallas kernels: 6.89 us -> 9.3 us
  waiting for transfers between devices: 56.9 us -> 54.5 us
    all_to_all x2 -> x3, blocking collectives: 25.7 us -> 32.4 us  [exchange(): lax.all_to_all(values, axis, split_axis=0, concat_axis=0, tiled=True, axi...]
    unnamed x30 -> x16, local copies, waits for them, and re-layouts: 6.16 us -> 0.67 us
    dot_general x6 -> x1, matrix products: 3.12 us -> 0.23 us  [dot(): return lax.dot_general(a, b, (dims, ((), ())), preferred_element_type=f32)]
    all_to_all x6 -> x5, starting transfers between devices: 45.4 us -> 42.6 us  [exchange(): lax.all_to_all(values, axis, split_axis=0, concat_axis=0, tiled=True, axi...]
    all_to_all x6 -> x5, waiting for transfers between devices: 56.9 us -> 54.5 us  [exchange(): lax.all_to_all(values, axis, split_axis=0, concat_axis=0, tiled=True, axi...]
    pallas_call x6 -> x8, Pallas kernels: 5.36 us -> 6.45 us  [in_vmem(): pl.pallas_call(kernel, out_shape=out_shape, in_specs=[vmem] * len(args),...]
  transfers between devices with their start and end apart: 6 -> 5, of which waited for: 6 -> 5; matrix products, arithmetic and copies ran while one was open for 3% -> 1% of each run, Pallas kernels for 0% -> 0%
where the time goes in v7:
time: 143 us; the launch traced here: 142 us
  waiting for transfers between devices  54.5 us (38%)
  starting transfers between devices  42.6 us (30%)
  blocking collectives  32.4 us (23%)
  Pallas kernels  9.3 us (7%)
    all_to_all x5, waiting for transfers between devices, exchange(): lax.all_to_all(values, axis, split_axis=0, concat_axis=0, tiled=True, axi...  54.5 us
    all_to_all x5, starting transfers between devices, exchange(): lax.all_to_all(values, axis, split_axis=0, concat_axis=0, tiled=True, axi...  42.6 us
    all_to_all x3, blocking collectives, exchange(): lax.all_to_all(values, axis, split_axis=0, concat_axis=0, tiled=True, axi...  32.4 us
    pallas_call x8, Pallas kernels, in_vmem(): pl.pallas_call(kernel, out_shape=out_shape, in_specs=[vmem] * len(args),...  6.45 us
  transfers between devices with their start and end apart: 5, of which 5 were waited for; matrix products, arithmetic and copies ran while one was open for 1% of the time, Pallas kernels for 0%

profile of v7, /device:TPU:1, one launch (start us, length us, event | category | flops | bytes accessed | tf_op | source)
XLA Modules:
  0.0 141.9 jit_solution(11949032071725404198)
XLA Ops:
  0.6 2.9 %shard_map.155 = bf16[8,400,128]{2,1,0:T(8,128)(2,1)} custom-call(s32[32,64]{1,0:T(8,128)} %bitcast.21, s32[32,64]{1,0:T(8,128)} %bitcast.22, s32[64,64]{1,0:T(8,128)} %counts_hbm.1, s32[1,4]{1,0:T(1,128)} %blocks_hbm.1, bf16[512,128]{1,0:T(8,128)(2,1)} %features_hbm.1, bf16[4,128,128]{2,1,0:T(8,128)(2,1)} %bitcast.14, bf16[128,256]{1,0:T(8,128)(2,1)} %grad_ref.3), custom_call_target="tpu_custom_call" | custom-call | tf_op jit(solution)/shard_map/pallas_call | solution.py:144
  3.5 15.5 %all_to_all.40.got_ref = bf16[8,400,128]{2,1,0:T(8,128)(2,1)S(1)} all-to-all(bf16[8,400,128]{2,1,0:T(8,128)(2,1)} %shard_map.155), channel_id=1, replica_groups={{0,1,16,17,32,33,48,49},{2,3,18,19,34,35,50,51},{4,5,20,21,36,37,52,53}..., dimensions={0} | all-to-all | bytes 1638400 | tf_op jit(solution)/shard_map/all_to_all | solution.py:21
  19.0 1.4 %shard_map.156 = bf16[8,168,128]{2,1,0:T(8,128)(2,1)} custom-call(bf16[8,400,128]{2,1,0:T(8,128)(2,1)S(1)} %all_to_all.40.got_ref), custom_call_target="tpu_custom_call" | custom-call | tf_op jit(solution)/shard_map/pallas_call | solution.py:162
  20.5 0.0 copy-start.6
  20.5 16.9 %all-to-all-start.1 = ((bf16[8,168,128]{2,1,0:T(8,128)(2,1)}), bf16[8,168,128]{2,1,0:T(8,128)(2,1)S(1)}, u32[]{:S(2)}, u32[]{:S(2)}) async-start(bf16[8,168,128]{2,1,0:T(8,128)(2,1)} %shard_map.156), calls=%async_computation.1 | async-start | bytes 688128 | tf_op jit(solution)/shard_map/all_to_all | solution.py:21
  37.4 0.0 copy-start.7
  37.4 0.0 copy-done.6
  37.4 0.6 copy-done.7
  38.1 0.0 copy-start.4
  38.1 0.0 copy-start.5
  38.1 0.2 convolution_convert_fusion.rows_ref
  38.3 19.1 %all-to-all-done.1.came_ref = bf16[8,168,128]{2,1,0:T(8,128)(2,1)S(1)} async-done(((bf16[8,168,128]{2,1,0:T(8,128)(2,1)}), bf16[8,168,128]{2,1,0:T(8,128)(2,1)S(1)}, u32[]{:S(2)}, u32[]{:S(2)}) %all-to-all-start.1) | async-done | bytes 344096 | tf_op jit(solution)/shard_map/all_to_all | solution.py:21
  57.4 0.0 copy-done.4
  57.4 0.0 copy-done.5
  57.4 1.0 shard_map.157
  58.5 0.0 copy-start.2
  58.5 0.0 copy-start.3
  58.5 10.0 %all-to-all-start.2 = ((bf16[8,128,128]{2,1,0:T(8,128)(2,1)}), bf16[8,128,128]{2,1,0:T(8,128)(2,1)S(1)}, u32[]{:S(2)}, u32[]{:S(2)}) async-start(bf16[8,128,128]{2,1,0:T(8,128)(2,1)} %get-tuple-element.10), calls=%async_computation.2 | async-start | bytes 524288 | tf_op jit(solution)/shard_map/all_to_all | solution.py:21
  68.5 0.0 copy-start
  68.5 0.0 copy-done.2
  68.5 0.0 copy-done.3
  68.5 6.5 %all-to-all-done.2.got_ref.back_ref = bf16[8,128,128]{2,1,0:T(8,128)(2,1)S(1)} async-done(((bf16[8,128,128]{2,1,0:T(8,128)(2,1)}), bf16[8,128,128]{2,1,0:T(8,128)(2,1)S(1)}, u32[]{:S(2)}, u32[]{:S(2)}) %all-to-all-start.2) | async-done | bytes 262176 | tf_op jit(solution)/shard_map/all_to_all | solution.py:21
  75.0 0.0 copy-done
  75.0 0.2 shard_map.158.hidden_ref
  75.2 8.7 %all_to_all.41.full_ref = bf16[8,64,128]{2,1,0:T(8,128)(2,1)S(1)} all-to-all(bf16[8,64,128]{2,1,0:T(8,128)(2,1)S(1)} %shard_map.158.hidden_ref), channel_id=1, replica_groups=mesh['feat'=8,'node'=64] {'feat'}, dimensions={0} | all-to-all | bytes 262144 | tf_op jit(solution)/shard_map/all_to_all | solution.py:21
  83.9 0.3 shard_map.159
  84.1 8.2 %all_to_all.42.got_ref = bf16[8,80,128]{2,1,0:T(8,128)(2,1)S(1)} all-to-all(bf16[8,80,128]{2,1,0:T(8,128)(2,1)S(1)} %shard_map.159), channel_id=1, replica_groups={{0,1,16,17,32,33,48,49},{2,3,18,19,34,35,50,51},{4,5,20,21,36,37,52,53}..., dimensions={0} | all-to-all | bytes 327680 | tf_op jit(solution)/shard_map/all_to_all | solution.py:21
  92.3 0.7 shard_map.160
  93.0 3.4 %all-to-all-start.5 = ((bf16[8,112,128]{2,1,0:T(8,128)(2,1)}), bf16[8,112,128]{2,1,0:T(8,128)(2,1)S(1)}, u32[]{:S(2)}, u32[]{:S(2)}) async-start(bf16[8,112,128]{2,1,0:T(8,128)(2,1)} %shard_map.160), calls=%async_computation.5 | async-start | bytes 458752 | tf_op jit(solution)/shard_map/all_to_all | solution.py:21
  96.4 16.2 %all-to-all-done.5.got_ref = bf16[8,112,128]{2,1,0:T(8,128)(2,1)S(1)} async-done(((bf16[8,112,128]{2,1,0:T(8,128)(2,1)}), bf16[8,112,128]{2,1,0:T(8,128)(2,1)S(1)}, u32[]{:S(2)}, u32[]{:S(2)}) %all-to-all-start.5) | async-done | bytes 229408 | tf_op jit(solution)/shard_map/all_to_all | solution.py:21
  112.7 1.0 shard_map.161
  113.6 3.5 %all-to-all-start.6 = ((bf16[8,208,128]{2,1,0:T(8,128)(2,1)}), bf16[8,208,128]{2,1,0:T(8,128)(2,1)S(1)}, u32[]{:S(2)}, u32[]{:S(2)}) async-start(bf16[8,208,128]{2,1,0:T(8,128)(2,1)} %shard_map.161), calls=%async_computation.6 | async-start | bytes 851968 | tf_op jit(solution)/shard_map/all_to_all | solution.py:21
  117.1 0.0 copy-start.1
  117.1 6.9 %all-to-all-done.6.got_ref = bf16[8,208,128]{2,1,0:T(8,128)(2,1)S(1)} async-done(((bf16[8,208,128]{2,1,0:T(8,128)(2,1)}), bf16[8,208,128]{2,1,0:T(8,128)(2,1)S(1)}, u32[]{:S(2)}, u32[]{:S(2)}) %all-to-all-start.6) | async-done | bytes 426016 | tf_op jit(solution)/shard_map/all_to_all | solution.py:21
  124.0 0.0 copy-done.1
  124.0 0.9 shard_map.162
  125.0 8.8 %all-to-all-start.7 = ((bf16[8,160,128]{2,1,0:T(8,128)(2,1)}), bf16[8,160,128]{2,1,0:T(8,128)(2,1)S(1)}, u32[]{:S(2)}, u32[]{:S(2)}) async-start(bf16[8,160,128]{2,1,0:T(8,128)(2,1)} %shard_map.162), calls=%async_computation.7 | async-start | bytes 655360 | tf_op jit(solution)/shard_map/all_to_all | solution.py:21
  133.9 0.7 pad_maximum_fusion
  134.5 0.7 pad_maximum_fusion.1
  135.2 5.8 %all-to-all-done.7.got_ref = bf16[8,160,128]{2,1,0:T(8,128)(2,1)S(1)} async-done(((bf16[8,160,128]{2,1,0:T(8,128)(2,1)}), bf16[8,160,128]{2,1,0:T(8,128)(2,1)S(1)}, u32[]{:S(2)}, u32[]{:S(2)}) %all-to-all-start.7) | async-done | bytes 327712 | tf_op jit(solution)/shard_map/all_to_all | solution.py:21
  140.9 0.9 shard_map.163
  (5 shorter events, 0.1 us)
Async XLA Ops:
  20.5 16.9 %copy-start.6 = (bf16[512,128]{1,0:T(8,128)(2,1)S(1)}, bf16[512,128]{1,0:T(8,128)(2,1)}, u32[]{:S(2)}) copy-start(bf16[512,128]{1,0:T(8,128)(2,1)} %features_hbm.1) | copy-start | bytes 393220
  20.5 36.9 %all-to-all-start.1 = ((bf16[8,168,128]{2,1,0:T(8,128)(2,1)}), bf16[8,168,128]{2,1,0:T(8,128)(2,1)S(1)}, u32[]{:S(2)}, u32[]{:S(2)}) async-start(bf16[8,168,128]{2,1,0:T(8,128)(2,1)} %shard_map.156), calls=%async_computation.1 | async-start | bytes 688128 | tf_op jit(solution)/shard_map/all_to_all | solution.py:21
  37.4 0.7 copy-start.7
  38.1 19.4 %copy-start.4 = (bf16[128,256]{1,0:T(8,128)(2,1)S(1)}, bf16[128,256]{1,0:T(8,128)(2,1)}, u32[]{:S(2)}) copy-start(bf16[128,256]{1,0:T(8,128)(2,1)} %self_ref.2) | copy-start | bytes 196612
  38.1 19.4 %copy-start.5 = (bf16[128,256]{1,0:T(8,128)(2,1)S(1)}, bf16[128,256]{1,0:T(8,128)(2,1)}, u32[]{:S(2)}) copy-start(bf16[128,256]{1,0:T(8,128)(2,1)} %other_ref.2) | copy-start | bytes 196612
  58.5 10.0 %copy-start.2 = (bf16[256,256]{1,0:T(8,128)(2,1)S(1)}, bf16[256,256]{1,0:T(8,128)(2,1)}, u32[]{:S(2)}) copy-start(bf16[256,256]{1,0:T(8,128)(2,1)} %other_ref.3) | copy-start | bytes 393220
  58.5 10.0 %copy-start.3 = (bf16[256,256]{1,0:T(8,128)(2,1)S(1)}, bf16[256,256]{1,0:T(8,128)(2,1)}, u32[]{:S(2)}) copy-start(bf16[256,256]{1,0:T(8,128)(2,1)} %self_ref.3) | copy-start | bytes 393220
  58.5 16.5 %all-to-all-start.2 = ((bf16[8,128,128]{2,1,0:T(8,128)(2,1)}), bf16[8,128,128]{2,1,0:T(8,128)(2,1)S(1)}, u32[]{:S(2)}, u32[]{:S(2)}) async-start(bf16[8,128,128]{2,1,0:T(8,128)(2,1)} %get-tuple-element.10), calls=%async_computation.2 | async-start | bytes 524288 | tf_op jit(solution)/shard_map/all_to_all | solution.py:21
  68.5 6.5 %copy-start = (bf16[128,256]{1,0:T(8,128)(2,1)S(1)}, bf16[128,256]{1,0:T(8,128)(2,1)}, u32[]{:S(2)}) copy-start(bf16[128,256]{1,0:T(8,128)(2,1)} %grad_ref.3) | copy-start | bytes 196612
  93.0 19.6 %all-to-all-start.5 = ((bf16[8,112,128]{2,1,0:T(8,128)(2,1)}), bf16[8,112,128]{2,1,0:T(8,128)(2,1)S(1)}, u32[]{:S(2)}, u32[]{:S(2)}) async-start(bf16[8,112,128]{2,1,0:T(8,128)(2,1)} %shard_map.160), calls=%async_computation.5 | async-start | bytes 458752 | tf_op jit(solution)/shard_map/all_to_all | solution.py:21
  113.6 10.4 %all-to-all-start.6 = ((bf16[8,208,128]{2,1,0:T(8,128)(2,1)}), bf16[8,208,128]{2,1,0:T(8,128)(2,1)S(1)}, u32[]{:S(2)}, u32[]{:S(2)}) async-start(bf16[8,208,128]{2,1,0:T(8,128)(2,1)} %shard_map.161), calls=%async_computation.6 | async-start | bytes 851968 | tf_op jit(solution)/shard_map/all_to_all | solution.py:21
  117.1 7.0 %copy-start.1 = (bf16[1,4,128,128]{3,2,1,0:T(8,128)(2,1)S(1)}, bf16[1,4,128,128]{3,2,1,0:T(8,128)(2,1)}, u32[]{:S(2)}) copy-start(bf16[1,4,128,128]{3,2,1,0:T(8,128)(2,1)} %param.20) | copy-start | bytes 393220
  125.0 16.0 %all-to-all-start.7 = ((bf16[8,160,128]{2,1,0:T(8,128)(2,1)}), bf16[8,160,128]{2,1,0:T(8,128)(2,1)S(1)}, u32[]{:S(2)}, u32[]{:S(2)}) async-start(bf16[8,160,128]{2,1,0:T(8,128)(2,1)} %shard_map.162), calls=%async_computation.7 | async-start | bytes 655360 | tf_op jit(solution)/shard_map/all_to_all | solution.py:21

commit v8 on v7

--- a/solution.py
+++ b/solution.py
@@ -156,7 +156,7 @@
     )(*args)
 
 
-def in_vmem(kernel, out_shape, *args):
+def in_vmem(kernel, out_shape, *args, scratch_shapes=()):
     vmem = pl.BlockSpec(memory_space=pltpu.VMEM)
     many = isinstance(out_shape, (list, tuple))
     return pl.pallas_call(
@@ -164,6 +164,7 @@
         out_shape=out_shape,
         in_specs=[vmem] * len(args),
         out_specs=[vmem] * len(out_shape) if many else vmem,
+        scratch_shapes=scratch_shapes,
         compiler_params=pltpu.CompilerParams(vmem_limit_bytes=VMEM_LIMIT),
     )(*args)
 
@@ -173,12 +174,14 @@
     return high, (values - high.astype(f32)).astype(bf16)
 
 
-def gather_kernel(got_ref, sent_ref, *, capacity, part, count):
+def gather_kernel(got_ref, sent_ref, marks_ref, *, capacity, part, count):
     near = got_ref.shape[0]
     far, _, targets = sent_ref.shape
     lanes = targets // capacity
     at = far * capacity + count * part
     marks = [got_ref[n, at : at + far + 8, :].astype(f32) for n in range(near)]
+    for n in range(near):
+        marks_ref[n] = got_ref[n, at : at + far + 8, :]
     slots = [sum(marks[h : h + lanes])[:far] for h in range(0, near, lanes)]
     nodes = lax.broadcasted_iota(jnp.int32, (targets, targets), 0).astype(f32)
     ones = jnp.ones((8, targets), bf16)
@@ -213,47 +216,52 @@
     pre = dot(rows_ref[...], self_ref[...], ((1,), (0,)))
     pre += dot(high, other_ref[...], ((1,), (0,)))
     pre += dot(low, other_ref[...], ((1,), (0,)))
-    pre_high, pre_low = halve(pre.T)
-    back = jnp.concatenate(halve(came[targets : targets + part]), axis=0)
+    back = halve(came[targets : targets + part])
+    all_rows = jnp.concatenate([pre.T.astype(bf16), *back], axis=0)
     for f in range(sent_ref.shape[0]):
-        mine = slice(f * part, (f + 1) * part)
-        sent_ref[f] = jnp.concatenate([pre_high[mine], pre_low[mine], back], axis=0)
-
-
-def hidden_kernel(got_ref, self_ref, other_ref, grad_ref, sent_ref, *, part):
-    feats = got_ref.shape[0]
-    pre = jnp.zeros((part, got_ref.shape[2]), f32)
-    for f in range(feats):
-        pre += got_ref[f, :part, :].astype(f32) + got_ref[f, part : 2 * part, :].astype(f32)
+        sent_ref[f] = all_rows
+
+
+def grads_kernel(
+    got_ref,
+    self_ref,
+    other_ref,
+    grad_ref,
+    rows_ref,
+    mean_ref,
+    sent_ref,
+    hidden_ref,
+    mine_ref,
+    scratch,
+    *,
+    part,
+    slice_at,
+):
+    feats, near = got_ref.shape[0], sent_ref.shape[0]
+    hidden = self_ref.shape[0]
+    pre = got_ref[0, :hidden, :].astype(f32)
+    for f in range(1, feats):
+        pre += got_ref[f, :hidden, :].astype(f32)
     sigma = 1.0 / (1.0 + jnp.exp(-pre))
     slope = sigma * (1.0 + pre * (1.0 - sigma))
-    back_high = jnp.concatenate([got_ref[f, 2 * part : 3 * part, :] for f in range(feats)], axis=0)
-    back_low = jnp.concatenate([got_ref[f, 3 * part :, :] for f in range(feats)], axis=0)
+    scratch[...] = pre * sigma
+    hidden_ref[...] = scratch[...].astype(bf16)
+    mine = scratch[pl.ds(pl.multiple_of(slice_at() * part, part), part), :].astype(bf16)
+    mine_ref[...] = mine
+    back_high = [got_ref[f, hidden : hidden + part, :] for f in range(feats)]
+    back_high = jnp.concatenate(back_high, axis=0)
+    back_low = [got_ref[f, hidden + part :, :] for f in range(feats)]
+    back_low = jnp.concatenate(back_low, axis=0)
     grad = dot(self_ref[...], grad_ref[...], ((1,), (1,)))
     grad += dot(other_ref[...], back_high, ((1,), (0,)))
     grad += dot(other_ref[...], back_low, ((1,), (0,)))
-    both = jnp.concatenate([grad * slope, pre * sigma], axis=0).astype(bf16)
-    for f in range(feats):
-        sent_ref[f] = both
-
-
-def grads_kernel(
-    full_ref, rows_ref, mean_ref, hidden_ref, back_ref, grad_ref, sent_ref, *, part
-):
-    feats, near = full_ref.shape[0], sent_ref.shape[0]
-    half = sent_ref.shape[2]
-    pre = jnp.concatenate([full_ref[f, :part, :] for f in range(feats)], axis=0)
-    hidden = hidden_ref[0, part:, :]
-    back_high = jnp.concatenate(
-        [back_ref[f, 2 * part : 3 * part, :] for f in range(feats)], axis=0
-    )
-    back_low = jnp.concatenate([back_ref[f, 3 * part :, :] for f in range(feats)], axis=0)
+    grad = (grad * slope).astype(bf16)
     rows_t = rows_ref[...].astype(f32).T.astype(bf16)
     mean_t = mean_ref[...].astype(f32).T.astype(bf16)
-    lower = quarters(dot(rows_t, pre, ((1,), (1,))), dot(mean_t, pre, ((1,), (1,))))
+    lower = quarters(dot(rows_t, grad, ((1,), (1,))), dot(mean_t, grad, ((1,), (1,))))
     upper = quarters(
-        dot(hidden, grad_ref[...], ((1,), (0,))),
-        dot(hidden, back_high, ((1,), (1,))) + dot(hidden, back_low, ((1,), (1,))),
+        dot(mine, grad_ref[...], ((1,), (0,))),
+        dot(mine, back_high, ((1,), (1,))) + dot(mine, back_low, ((1,), (1,))),
     )
     rows_each, share = lower.shape[0] // near, upper.shape[0] // near
     for n in range(near):
@@ -261,7 +269,7 @@
         sent_ref[n, rows_each:, :] = upper[n * share : (n + 1) * share]
 
 
-def far_kernel(got_ref, hidden_ref, sent_ref, *, part):
+def far_kernel(got_ref, hidden_ref, sent_ref):
     total = got_ref[0].astype(f32)
     for n in range(1, got_ref.shape[0]):
         total += got_ref[n].astype(f32)
@@ -269,7 +277,7 @@
     sums = total.shape[0]
     for a in range(sent_ref.shape[0]):
         sent_ref[a, :sums, :] = total
-        sent_ref[a, sums:, :] = hidden_ref[0, part:, :]
+        sent_ref[a, sums:, :] = hidden_ref[...]
 
 
 def near_kernel(got_ref, marks_ref, sent_ref, *, sums, part, count, where):
@@ -344,7 +352,6 @@
     near_ids = [(x * na + a) * nb + b for a in range(na) for x in range(nx) for b in range(nb)]
     near_groups = [near_ids[a * near : (a + 1) * near] for a in range(na)]
     far_groups = [list(group) for group in zip(*near_groups)]
-    feat = lax.axis_index("feat")
     capacity = sample_ids.shape[2]
     targets = self_ids.shape[1]
     width = features.shape[1]
@@ -369,10 +376,12 @@
     )
     got = exchange(sent, "node", near_groups)
 
-    marks = got[:, na * capacity + count * part :]
-    sent = in_vmem(
+    sent, marks = in_vmem(
         functools.partial(gather_kernel, capacity=capacity, part=part, count=count),
-        jax.ShapeDtypeStruct((na, targets + part + 8, width), bf16),
+        [
+            jax.ShapeDtypeStruct((na, targets + part + 8, width), bf16),
+            jax.ShapeDtypeStruct((near, na + 8, targets), bf16),
+        ],
         got,
     )
     came = exchange(sent, "node", far_groups)
@@ -381,7 +390,7 @@
     sent, mean_high = in_vmem(
         functools.partial(first_kernel, part=part),
         [
-            jax.ShapeDtypeStruct((feats, 4 * part, targets), bf16),
+            jax.ShapeDtypeStruct((feats, hidden + 2 * part, targets), bf16),
             jax.ShapeDtypeStruct((targets, width), bf16),
         ],
         came,
@@ -389,37 +398,28 @@
         self_one,
         neighbour_one,
     )
-    back = exchange(sent, "feat")
-
-    self_two_part = lax.dynamic_slice_in_dim(self_two, feat * part, part, 0)
-    neighbour_two_part = lax.dynamic_slice_in_dim(neighbour_two, feat * part, part, 0)
-    sent = in_vmem(
-        functools.partial(hidden_kernel, part=part),
-        jax.ShapeDtypeStruct((feats, 2 * part, targets), bf16),
-        back,
-        self_two_part,
-        neighbour_two_part,
-        out_grad,
-    )
-    hidden_part = sent
-    full = exchange(sent, "feat")
-    hidden_t = full[:, part:].reshape(hidden, targets)
+    got = exchange(sent, "feat")
 
     half = hidden // 2
     rows_each, share = 4 * width // near, 4 * part // near
-    sent = in_vmem(
-        functools.partial(grads_kernel, part=part),
-        jax.ShapeDtypeStruct((near, rows_each + share, half), bf16),
-        full,
+    sent, hidden_t, hidden_part = in_vmem(
+        functools.partial(grads_kernel, part=part, slice_at=lambda: lax.axis_index("feat")),
+        [
+            jax.ShapeDtypeStruct((near, rows_each + share, half), bf16),
+            jax.ShapeDtypeStruct((hidden, targets), bf16),
+            jax.ShapeDtypeStruct((part, targets), bf16),
+        ],
+        got,
+        self_two,
+        neighbour_two,
+        out_grad,
         self_rows,
         mean_high,
-        hidden_part,
-        back,
-        out_grad,
+        scratch_shapes=[pltpu.VMEM((hidden, targets), f32)],
     )
     got = exchange(sent, "node", near_groups)
     sent = in_vmem(
-        functools.partial(far_kernel, part=part),
+        far_kernel,
         jax.ShapeDtypeStruct((na, rows_each + share + part, half), bf16),
         got,
         hidden_part,

time: 143 us -> 135 us (0.944)
  blocking collectives: 32.4 us -> 73.7 us
  waiting for transfers between devices: 54.5 us -> 25.5 us
  starting transfers between devices: 42.6 us -> 25.2 us
  Pallas kernels: 9.3 us -> 7.25 us
    all_to_all x3 -> x5, blocking collectives: 32.4 us -> 73.7 us  [exchange(): lax.all_to_all(values, axis, split_axis=0, concat_axis=0, tiled=True, axi...]
    all_to_all x5 -> x2, waiting for transfers between devices: 54.5 us -> 25.5 us  [exchange(): lax.all_to_all(values, axis, split_axis=0, concat_axis=0, tiled=True, axi...]
    all_to_all x5 -> x2, starting transfers between devices: 42.6 us -> 25.2 us  [exchange(): lax.all_to_all(values, axis, split_axis=0, concat_axis=0, tiled=True, axi...]
    pallas_call x8 -> x7, Pallas kernels: 6.45 us -> 4.39 us  [in_vmem(): pl.pallas_call(kernel, out_shape=out_shape, in_specs=[vmem] * len(args),...]
  transfers between devices with their start and end apart: 5 -> 2, of which waited for: 5 -> 2; matrix products, arithmetic and copies ran while one was open for 1% -> 1% of each run, Pallas kernels for 0% -> 0%
where the time goes in v8:
time: 135 us; the launch traced here: 134 us
  blocking collectives  73.7 us (55%)
  waiting for transfers between devices  25.5 us (19%)
  starting transfers between devices  25.2 us (19%)
  Pallas kernels  7.25 us (5%)
    all_to_all x5, blocking collectives, exchange(): lax.all_to_all(values, axis, split_axis=0, concat_axis=0, tiled=True, axi...  73.7 us
    all_to_all x2, waiting for transfers between devices, exchange(): lax.all_to_all(values, axis, split_axis=0, concat_axis=0, tiled=True, axi...  25.5 us
    all_to_all x2, starting transfers between devices, exchange(): lax.all_to_all(values, axis, split_axis=0, concat_axis=0, tiled=True, axi...  25.2 us
    pallas_call x7, Pallas kernels, in_vmem(): pl.pallas_call(kernel, out_shape=out_shape, in_specs=[vmem] * len(args),...  4.39 us
    pallas_call x1, Pallas kernels, pack(): pl.pallas_call(kernel, out_shape=jax.ShapeDtypeStruct((nx * nb, total, fe...  2.86 us
  transfers between devices with their start and end apart: 2, of which 2 were waited for; matrix products, arithmetic and copies ran while one was open for 1% of the time, Pallas kernels for 0%

profile of v8, /device:TPU:1, one launch (start us, length us, event | category | flops | bytes accessed | tf_op | source)
XLA Modules:
  0.0 134.0 jit_solution(10642342802423480911)
XLA Ops:
  0.6 2.9 %shard_map.155 = bf16[8,400,128]{2,1,0:T(8,128)(2,1)} custom-call(s32[32,64]{1,0:T(8,128)} %bitcast.19, s32[32,64]{1,0:T(8,128)} %bitcast.20, s32[64,64]{1,0:T(8,128)} %counts_hbm.1, s32[1,4]{1,0:T(1,128)} %blocks_hbm.1, bf16[512,128]{1,0:T(8,128)(2,1)} %features_hbm.1, bf16[4,128,128]{2,1,0:T(8,128)(2,1)} %bitcast.13, bf16[128,256]{1,0:T(8,128)(2,1)} %grad_ref.1), custom_call_target="tpu_custom_call" | custom-call | tf_op jit(solution)/shard_map/pallas_call | solution.py:144
  3.5 15.5 %all_to_all.35.got_ref = bf16[8,400,128]{2,1,0:T(8,128)(2,1)S(1)} all-to-all(bf16[8,400,128]{2,1,0:T(8,128)(2,1)} %shard_map.155), channel_id=1, replica_groups={{0,1,16,17,32,33,48,49},{2,3,18,19,34,35,50,51},{4,5,20,21,36,37,52,53}..., dimensions={0} | all-to-all | bytes 1638400 | tf_op jit(solution)/shard_map/all_to_all | solution.py:21
  19.0 1.4 %shard_map.156 = (bf16[8,168,128]{2,1,0:T(8,128)(2,1)}, bf16[8,16,128]{2,1,0:T(8,128)(2,1)S(1)}) custom-call(bf16[8,400,128]{2,1,0:T(8,128)(2,1)S(1)} %all_to_all.35.got_ref), custom_call_target="tpu_custom_call" | custom-call | tf_op jit(solution)/shard_map/pallas_call | solution.py:162
  20.5 0.0 copy-start.6
  20.5 16.9 %all-to-all-start.1 = ((bf16[8,168,128]{2,1,0:T(8,128)(2,1)}), bf16[8,168,128]{2,1,0:T(8,128)(2,1)S(1)}, u32[]{:S(2)}, u32[]{:S(2)}) async-start(bf16[8,168,128]{2,1,0:T(8,128)(2,1)} %get-tuple-element.15), calls=%async_computation.1 | async-start | bytes 688128 | tf_op jit(solution)/shard_map/all_to_all | solution.py:21
  37.4 0.0 copy-start.7
  37.4 0.0 copy-done.6
  37.4 0.6 copy-done.7
  38.1 0.0 copy-start.4
  38.1 0.0 copy-start.5
  38.1 0.2 convolution_convert_fusion.rows_ref
  38.3 19.1 %all-to-all-done.1.came_ref = bf16[8,168,128]{2,1,0:T(8,128)(2,1)S(1)} async-done(((bf16[8,168,128]{2,1,0:T(8,128)(2,1)}), bf16[8,168,128]{2,1,0:T(8,128)(2,1)S(1)}, u32[]{:S(2)}, u32[]{:S(2)}) %all-to-all-start.1) | async-done | bytes 344096 | tf_op jit(solution)/shard_map/all_to_all | solution.py:21
  57.4 0.0 copy-done.4
  57.4 0.0 copy-done.5
  57.4 0.4 shard_map.157
  57.8 0.0 copy-start.1
  57.8 0.0 copy-start.2
  57.8 0.0 copy-start.3
  57.8 20.8 %all_to_all.36.got_ref = bf16[8,320,128]{2,1,0:T(8,128)(2,1)S(1)} all-to-all(bf16[8,320,128]{2,1,0:T(8,128)(2,1)S(1)} %get-tuple-element.16), channel_id=1, replica_groups=mesh['feat'=8,'node'=64] {'feat'}, dimensions={0} | all-to-all | bytes 1310720 | tf_op jit(solution)/shard_map/all_to_all | solution.py:21
  78.6 0.0 copy-done.1
  78.6 0.0 copy-done.2
  78.6 0.0 copy-done.3
  78.6 0.5 shard_map.158
  79.1 8.2 %all_to_all.37.got_ref = bf16[8,80,128]{2,1,0:T(8,128)(2,1)S(1)} all-to-all(bf16[8,80,128]{2,1,0:T(8,128)(2,1)S(1)} %get-tuple-element.18), channel_id=1, replica_groups={{0,1,16,17,32,33,48,49},{2,3,18,19,34,35,50,51},{4,5,20,21,36,37,52,53}..., dimensions={0} | all-to-all | bytes 327680 | tf_op jit(solution)/shard_map/all_to_all | solution.py:21
  87.3 19.2 %all_to_all.38.got_ref = bf16[8,112,128]{2,1,0:T(8,128)(2,1)S(1)} all-to-all(bf16[8,112,128]{2,1,0:T(8,128)(2,1)S(1)} %shard_map.159), channel_id=1, replica_groups={{0,2,4,6,8,10,12,14},{1,3,5,7,9,11,13,15},{16,18,20,22,24,26,28,30},{17..., dimensions={0} | all-to-all | bytes 458752 | tf_op jit(solution)/shard_map/all_to_all | solution.py:21
  106.5 0.2 shard_map.160
  106.7 0.0 copy-start
  106.8 10.0 %all_to_all.39.got_ref = bf16[8,208,128]{2,1,0:T(8,128)(2,1)S(1)} all-to-all(bf16[8,208,128]{2,1,0:T(8,128)(2,1)S(1)} %shard_map.160), channel_id=1, replica_groups={{0,1,16,17,32,33,48,49},{2,3,18,19,34,35,50,51},{4,5,20,21,36,37,52,53}..., dimensions={0} | all-to-all | bytes 851968 | tf_op jit(solution)/shard_map/all_to_all | solution.py:21
  116.7 0.0 copy-done
  116.7 0.9 shard_map.161
  117.6 8.3 %all-to-all-start.6 = ((bf16[8,160,128]{2,1,0:T(8,128)(2,1)}), bf16[8,160,128]{2,1,0:T(8,128)(2,1)S(1)}, u32[]{:S(2)}, u32[]{:S(2)}) async-start(bf16[8,160,128]{2,1,0:T(8,128)(2,1)} %shard_map.161), calls=%async_computation.6 | async-start | bytes 655360 | tf_op jit(solution)/shard_map/all_to_all | solution.py:21
  126.0 0.7 pad_maximum_fusion
  126.7 6.4 %all-to-all-done.6.got_ref = bf16[8,160,128]{2,1,0:T(8,128)(2,1)S(1)} async-done(((bf16[8,160,128]{2,1,0:T(8,128)(2,1)}), bf16[8,160,128]{2,1,0:T(8,128)(2,1)S(1)}, u32[]{:S(2)}, u32[]{:S(2)}) %all-to-all-start.6) | async-done | bytes 327712 | tf_op jit(solution)/shard_map/all_to_all | solution.py:21
  133.1 0.9 shard_map.162
  (3 shorter events, 0.1 us)
Async XLA Ops:
  20.5 16.9 %copy-start.6 = (bf16[512,128]{1,0:T(8,128)(2,1)S(1)}, bf16[512,128]{1,0:T(8,128)(2,1)}, u32[]{:S(2)}) copy-start(bf16[512,128]{1,0:T(8,128)(2,1)} %features_hbm.1) | copy-start | bytes 393220
  20.5 36.9 %all-to-all-start.1 = ((bf16[8,168,128]{2,1,0:T(8,128)(2,1)}), bf16[8,168,128]{2,1,0:T(8,128)(2,1)S(1)}, u32[]{:S(2)}, u32[]{:S(2)}) async-start(bf16[8,168,128]{2,1,0:T(8,128)(2,1)} %get-tuple-element.15), calls=%async_computation.1 | async-start | bytes 688128 | tf_op jit(solution)/shard_map/all_to_all | solution.py:21
  37.4 0.7 copy-start.7
  38.1 19.4 %copy-start.4 = (bf16[128,256]{1,0:T(8,128)(2,1)S(1)}, bf16[128,256]{1,0:T(8,128)(2,1)}, u32[]{:S(2)}) copy-start(bf16[128,256]{1,0:T(8,128)(2,1)} %self_ref.3) | copy-start | bytes 196612
  38.1 19.4 %copy-start.5 = (bf16[128,256]{1,0:T(8,128)(2,1)S(1)}, bf16[128,256]{1,0:T(8,128)(2,1)}, u32[]{:S(2)}) copy-start(bf16[128,256]{1,0:T(8,128)(2,1)} %other_ref.3) | copy-start | bytes 196612
  57.8 20.8 %copy-start.1 = (bf16[256,256]{1,0:T(8,128)(2,1)S(1)}, bf16[256,256]{1,0:T(8,128)(2,1)}, u32[]{:S(2)}) copy-start(bf16[256,256]{1,0:T(8,128)(2,1)} %self_ref.5) | copy-start | bytes 393220
  57.8 20.8 %copy-start.2 = (bf16[256,256]{1,0:T(8,128)(2,1)S(1)}, bf16[256,256]{1,0:T(8,128)(2,1)}, u32[]{:S(2)}) copy-start(bf16[256,256]{1,0:T(8,128)(2,1)} %other_ref.5) | copy-start | bytes 393220
  57.8 20.8 %copy-start.3 = (bf16[128,256]{1,0:T(8,128)(2,1)S(1)}, bf16[128,256]{1,0:T(8,128)(2,1)}, u32[]{:S(2)}) copy-start(bf16[128,256]{1,0:T(8,128)(2,1)} %grad_ref.1) | copy-start | bytes 196612
  106.7 10.0 %copy-start = (bf16[1,4,128,128]{3,2,1,0:T(8,128)(2,1)S(1)}, bf16[1,4,128,128]{3,2,1,0:T(8,128)(2,1)}, u32[]{:S(2)}) copy-start(bf16[1,4,128,128]{3,2,1,0:T(8,128)(2,1)} %param.20) | copy-start | bytes 393220
  117.6 15.4 %all-to-all-start.6 = ((bf16[8,160,128]{2,1,0:T(8,128)(2,1)}), bf16[8,160,128]{2,1,0:T(8,128)(2,1)S(1)}, u32[]{:S(2)}, u32[]{:S(2)}) async-start(bf16[8,160,128]{2,1,0:T(8,128)(2,1)} %shard_map.161), calls=%async_computation.6 | async-start | bytes 655360 | tf_op jit(solution)/shard_map/all_to_all | solution.py:21

commit v9 on v8

--- a/solution.py
+++ b/solution.py
@@ -21,12 +21,6 @@
     return lax.all_to_all(
         values, axis, split_axis=0, concat_axis=0, tiled=True, axis_index_groups=groups
     )
-
-
-def pick(table, row_ids):
-    local_ids = jnp.arange(table.shape[0], dtype=jnp.int32)
-    chosen = (row_ids[:, None] == local_ids[None, :]).astype(table.dtype)
-    return dot(chosen, table, ((1,), (0,))).astype(table.dtype)
 
 
 def quarters(first, second):
@@ -51,7 +45,9 @@
     features_hbm,
     tiles_hbm,
     grad_hbm,
-    sent_ref,
+    own_hbm,
+    sent_hbm,
+    own_rows_ref,
     ids_ref,
     slots_ref,
     counts_ref,
@@ -59,9 +55,12 @@
     features_ref,
     tiles_ref,
     grad_ref,
+    own_ref,
+    sent_ref,
     slots_scratch,
     grad_scratch,
     sems,
+    out_sems,
     *,
     nx,
     na,
@@ -79,6 +78,7 @@
                 (features_hbm, features_ref),
                 (tiles_hbm, tiles_ref),
                 (grad_hbm, grad_ref),
+                (own_hbm, own_ref),
             ]
         )
     ]
@@ -113,6 +113,7 @@
         far_rows = jnp.where(row == count + k, blocks[k] // (na * nb) * nb + blocks[k] % nb, far_rows)
     far_rows = far_rows.astype(f32)
     local_ids = lax.broadcasted_iota(jnp.int32, (capacity, locals_), 1)
+    outs = []
     for x in range(nx):
         for b in range(nb):
             to = x * nb + b
@@ -131,26 +132,47 @@
                 at += part
             slot_rows = slots_scratch[pl.ds(owners[0], na, stride=nb), :]
             sent_ref[to, at : at + na + 8, :] = jnp.concatenate([slot_rows, far_rows], 0).astype(bf16)
-
-
-def pack(sample_ids, dest_slots, counts, blocks, features, tiles, grad, nx, na, nb, part, place):
+            out = pltpu.make_async_copy(sent_ref.at[to], sent_hbm.at[to], out_sems.at[to])
+            out.start()
+            outs.append(out)
+    own = jnp.broadcast_to(own_ref[...], (targets, targets)).astype(f32).T.astype(jnp.int32)
+    local_ids = lax.broadcasted_iota(jnp.int32, (targets, targets), 1)
+    chosen = [
+        jnp.where(own == local_ids + start, 1.0, 0.0).astype(bf16)
+        for start in range(0, locals_, targets)
+    ]
+    own_rows = dot(jnp.concatenate(chosen, axis=1), features_ref[...], ((1,), (0,)))
+    own_rows_ref[...] = own_rows.astype(bf16)
+    for out in outs:
+        out.wait()
+
+
+def pack(sample_ids, dest_slots, counts, blocks, features, tiles, grad, own, nx, na, nb, part, place):
     count, targets, _ = tiles.shape
     capacity, nodes = sample_ids.shape
     total = na * capacity + count * part + na + 8
     kernel = functools.partial(pack_kernel, nx=nx, na=na, nb=nb, place=place)
-    args = (sample_ids, dest_slots, counts, blocks, features, tiles, grad)
+    args = (sample_ids, dest_slots, counts, blocks, features, tiles, grad, own)
     held = [pltpu.VMEM(arg.shape, arg.dtype) for arg in args]
     held[3] = pltpu.SMEM(blocks.shape, blocks.dtype)
     return pl.pallas_call(
         kernel,
-        out_shape=jax.ShapeDtypeStruct((nx * nb, total, features.shape[1]), bf16),
+        out_shape=[
+            jax.ShapeDtypeStruct((nx * nb, total, features.shape[1]), bf16),
+            jax.ShapeDtypeStruct((targets, features.shape[1]), bf16),
+        ],
         in_specs=[pl.BlockSpec(memory_space=pltpu.HBM)] * len(args),
-        out_specs=pl.BlockSpec(memory_space=pltpu.VMEM),
+        out_specs=[
+            pl.BlockSpec(memory_space=pltpu.HBM),
+            pl.BlockSpec(memory_space=pltpu.VMEM),
+        ],
         scratch_shapes=held
         + [
+            pltpu.VMEM((nx * nb, total, features.shape[1]), bf16),
             pltpu.VMEM((targets, targets), f32),
             pltpu.VMEM((grad.shape[1], targets), f32),
             pltpu.SemaphoreType.DMA((len(args),)),
+            pltpu.SemaphoreType.DMA((nx * nb,)),
         ],
         compiler_params=pltpu.CompilerParams(vmem_limit_bytes=PACK_LIMIT),
     )(*args)
@@ -316,7 +338,21 @@
         sent_ref[f] = both
 
 
-def last_kernel(got_ref, hidden_ref, self_ref, other_ref, out_ref, first_ref, second_ref, *, part):
+def last_kernel(
+    got_ref,
+    hidden_ref,
+    self_ref,
+    other_ref,
+    lower_ref,
+    out_ref,
+    low_first_ref,
+    low_second_ref,
+    first_ref,
+    second_ref,
+    *,
+    part,
+    rows_each,
+):
     feats = got_ref.shape[0]
     half = first_ref.shape[1] // 2
     agg = jnp.concatenate([got_ref[f, :part, :] for f in range(feats)], axis=0)
@@ -328,6 +364,13 @@
             start = part * (1 + 2 * n)
             ref[at : at + part, :half] = got_ref[f, start : start + part, :].astype(f32)
             ref[at : at + part, half:] = got_ref[f, start + part : start + 2 * part, :].astype(f32)
+    width = low_first_ref.shape[0]
+    for n in range(lower_ref.shape[0]):
+        quarter, at = divmod(n * rows_each, width)
+        ref = (low_first_ref, low_second_ref)[quarter // 2]
+        left = quarter % 2 * half
+        rows = lower_ref[n, :rows_each, :].astype(f32)
+        ref[at : at + rows_each, left : left + half] = rows
 
 
 def shards(
@@ -360,7 +403,7 @@
     tiles = tile_weights[0]
     count = tiles.shape[0]
 
-    sent = pack(
+    sent, self_rows = pack(
         sample_ids[0].T,
         dest_slots[0].T,
         send_counts,
@@ -368,6 +411,7 @@
         features,
         tiles,
         out_grad,
+        self_ids,
         nx,
         na,
         nb,
@@ -386,7 +430,6 @@
     )
     came = exchange(sent, "node", far_groups)
 
-    self_rows = pick(features, self_ids[0])
     sent, mean_high = in_vmem(
         functools.partial(first_kernel, part=part),
         [
@@ -439,7 +482,7 @@
         marks,
     )
     got = exchange(sent, "node", near_groups)
-    lower = got[:, :rows_each].reshape(4, width, half).astype(f32)
+    lower = got
 
     sent = in_vmem(
         functools.partial(second_kernel, rows_each=rows_each, share=share, part=part),
@@ -448,10 +491,12 @@
         tiles,
     )
     got = exchange(sent, "feat")
-    layer_output, upper_self, upper_others = in_vmem(
-        functools.partial(last_kernel, part=part),
+    return in_vmem(
+        functools.partial(last_kernel, part=part, rows_each=rows_each),
         [
             jax.ShapeDtypeStruct((targets, hidden), bf16),
+            jax.ShapeDtypeStruct((width, hidden), f32),
+            jax.ShapeDtypeStruct((width, hidden), f32),
             jax.ShapeDtypeStruct((hidden, hidden), f32),
             jax.ShapeDtypeStruct((hidden, hidden), f32),
         ],
@@ -459,12 +504,8 @@
         hidden_t,
         self_two,
         neighbour_two,
-    )
-
-    def halves(which):
-        return jnp.concatenate([lower[2 * which], lower[2 * which + 1]], axis=1)
-
-    return (layer_output, halves(0), halves(1), upper_self, upper_others)
+        lower,
+    )
 
 
 def solution(mesh):

time: 135 us -> 133 us (0.985)
  blocking collectives: 73.7 us -> 126 us
  waiting for transfers between devices: 25.5 us -> 0 us
  starting transfers between devices: 25.2 us -> 0 us
    all_to_all x5 -> x7, blocking collectives: 73.7 us -> 126 us  [exchange(): lax.all_to_all(values, axis, split_axis=0, concat_axis=0, tiled=True, axi...]
    all_to_all x2 -> x0, waiting for transfers between devices: 25.5 us -> none  [exchange(): lax.all_to_all(values, axis, split_axis=0, concat_axis=0, tiled=True, axi...]
    all_to_all x2 -> x0, starting transfers between devices: 25.2 us -> none  [exchange(): lax.all_to_all(values, axis, split_axis=0, concat_axis=0, tiled=True, axi...]
    pallas_call x7, Pallas kernels: 4.39 us -> 3.02 us  [in_vmem(): pl.pallas_call(kernel, out_shape=out_shape, in_specs=[vmem] * len(args),...]
  transfers between devices with their start and end apart: 2 -> 0, of which waited for: 2 -> 0; matrix products, arithmetic and copies ran while one was open for 1% -> 0% of each run, Pallas kernels for 0% -> 0%
where the time goes in v9:
time: 133 us
  blocking collectives  126 us (95%)
  Pallas kernels  6.31 us (5%)
    all_to_all x7, blocking collectives, exchange(): lax.all_to_all(values, axis, split_axis=0, concat_axis=0, tiled=True, axi...  126 us
    pallas_call x1, Pallas kernels, pack(): pl.pallas_call(kernel, out_shape=[jax.ShapeDtypeStruct((nx * nb, total, f...  3.29 us
    pallas_call x7, Pallas kernels, in_vmem(): pl.pallas_call(kernel, out_shape=out_shape, in_specs=[vmem] * len(args),...  3.02 us

profile of v9, /device:TPU:1, one launch (start us, length us, event | category | flops | bytes accessed | tf_op | source)
XLA Modules:
  0.0 132.8 jit_solution(7448942425485999534)
XLA Ops:
  0.6 3.3 %shard_map.155 = (bf16[8,400,128]{2,1,0:T(8,128)(2,1)}, bf16[128,128]{1,0:T(8,128)(2,1)}) custom-call(s32[32,64]{1,0:T(8,128)} %bitcast.9, s32[32,64]{1,0:T(8,128)} %bitcast.10, s32[64,64]{1,0:T(8,128)} %counts_hbm.1, s32[1,4]{1,0:T(1,128)} %blocks_hbm.1, bf16[512,128]{1,0:T(8,128)(2,1)} %features_hbm.1, bf16[4,128,128]{2,1,0:T(8,128)(2,1)} %bitcast.7, ...), custom_call_target="tpu_custom_call" | custom-call | tf_op jit(solution)/shard_map/pallas_call | solution.py:158
  3.9 15.5 %all_to_all.35.got_ref = bf16[8,400,128]{2,1,0:T(8,128)(2,1)S(1)} all-to-all(bf16[8,400,128]{2,1,0:T(8,128)(2,1)} %get-tuple-element.14), channel_id=1, replica_groups={{0,1,16,17,32,33,48,49},{2,3,18,19,34,35,50,51},{4,5,20,21,36,37,52,53}..., dimensions={0} | all-to-all | bytes 1638400 | tf_op jit(solution)/shard_map/all_to_all | solution.py:21
  19.5 0.7 shard_map.156
  20.2 0.0 copy-start.4
  20.2 0.0 copy-start.5
  20.2 0.0 copy-start.6
  20.2 37.9 %all_to_all.36.came_ref = bf16[8,168,128]{2,1,0:T(8,128)(2,1)S(1)} all-to-all(bf16[8,168,128]{2,1,0:T(8,128)(2,1)S(1)} %get-tuple-element.15), channel_id=1, replica_groups={{0,2,4,6,8,10,12,14},{1,3,5,7,9,11,13,15},{16,18,20,22,24,26,28,30},{17..., dimensions={0} | all-to-all | bytes 688128 | tf_op jit(solution)/shard_map/all_to_all | solution.py:21
  58.1 0.0 copy-done.4
  58.1 0.0 copy-done.5
  58.1 0.0 copy-done.6
  58.1 0.4 shard_map.157
  58.5 0.0 copy-start.1
  58.5 0.0 copy-start.2
  58.5 0.0 copy-start.3
  58.5 20.0 %all_to_all.37.got_ref = bf16[8,320,128]{2,1,0:T(8,128)(2,1)S(1)} all-to-all(bf16[8,320,128]{2,1,0:T(8,128)(2,1)S(1)} %get-tuple-element.17), channel_id=1, replica_groups=mesh['feat'=8,'node'=64] {'feat'}, dimensions={0} | all-to-all | bytes 1310720 | tf_op jit(solution)/shard_map/all_to_all | solution.py:21
  78.5 0.0 copy-done.1
  78.5 0.0 copy-done.2
  78.5 0.0 copy-done.3
  78.5 0.5 shard_map.158
  79.0 8.4 %all_to_all.38.got_ref = bf16[8,80,128]{2,1,0:T(8,128)(2,1)S(1)} all-to-all(bf16[8,80,128]{2,1,0:T(8,128)(2,1)S(1)} %get-tuple-element.19), channel_id=1, replica_groups={{0,1,16,17,32,33,48,49},{2,3,18,19,34,35,50,51},{4,5,20,21,36,37,52,53}..., dimensions={0} | all-to-all | bytes 327680 | tf_op jit(solution)/shard_map/all_to_all | solution.py:21
  87.5 19.2 %all_to_all.39.got_ref = bf16[8,112,128]{2,1,0:T(8,128)(2,1)S(1)} all-to-all(bf16[8,112,128]{2,1,0:T(8,128)(2,1)S(1)} %shard_map.159), channel_id=1, replica_groups={{0,2,4,6,8,10,12,14},{1,3,5,7,9,11,13,15},{16,18,20,22,24,26,28,30},{17..., dimensions={0} | all-to-all | bytes 458752 | tf_op jit(solution)/shard_map/all_to_all | solution.py:21
  106.7 0.2 shard_map.160
  107.0 0.0 copy-start
  107.0 9.6 %all_to_all.40.got_ref.lower_ref = bf16[8,208,128]{2,1,0:T(8,128)(2,1)S(1)} all-to-all(bf16[8,208,128]{2,1,0:T(8,128)(2,1)S(1)} %shard_map.160), channel_id=1, replica_groups={{0,1,16,17,32,33,48,49},{2,3,18,19,34,35,50,51},{4,5,20,21,36,37,52,53}..., dimensions={0} | all-to-all | bytes 851968 | tf_op jit(solution)/shard_map/all_to_all | solution.py:21
  116.6 0.0 copy-done
  116.6 0.2 shard_map.161
  116.8 15.0 %all_to_all.41.got_ref = bf16[8,160,128]{2,1,0:T(8,128)(2,1)S(1)} all-to-all(bf16[8,160,128]{2,1,0:T(8,128)(2,1)S(1)} %shard_map.161), channel_id=1, replica_groups=mesh['feat'=8,'node'=64] {'feat'}, dimensions={0} | all-to-all | bytes 655360 | tf_op jit(solution)/shard_map/all_to_all | solution.py:21
  131.8 1.0 shard_map.162
  (1 shorter events, 0.0 us)
Async XLA Ops:
  20.2 37.9 %copy-start.4 = (bf16[128,128]{1,0:T(8,128)(2,1)S(1)}, bf16[128,128]{1,0:T(8,128)(2,1)}, u32[]{:S(2)}) copy-start(bf16[128,128]{1,0:T(8,128)(2,1)} %get-tuple-element.16.rows_ref) | copy-start | bytes 98308
  20.2 37.9 %copy-start.5 = (bf16[128,256]{1,0:T(8,128)(2,1)S(1)}, bf16[128,256]{1,0:T(8,128)(2,1)}, u32[]{:S(2)}) copy-start(bf16[128,256]{1,0:T(8,128)(2,1)} %self_ref.3) | copy-start | bytes 196612
  20.2 37.9 %copy-start.6 = (bf16[128,256]{1,0:T(8,128)(2,1)S(1)}, bf16[128,256]{1,0:T(8,128)(2,1)}, u32[]{:S(2)}) copy-start(bf16[128,256]{1,0:T(8,128)(2,1)} %other_ref.3) | copy-start | bytes 196612
  58.5 20.1 %copy-start.1 = (bf16[256,256]{1,0:T(8,128)(2,1)S(1)}, bf16[256,256]{1,0:T(8,128)(2,1)}, u32[]{:S(2)}) copy-start(bf16[256,256]{1,0:T(8,128)(2,1)} %self_ref.5) | copy-start | bytes 393220
  58.5 20.0 %copy-start.2 = (bf16[256,256]{1,0:T(8,128)(2,1)S(1)}, bf16[256,256]{1,0:T(8,128)(2,1)}, u32[]{:S(2)}) copy-start(bf16[256,256]{1,0:T(8,128)(2,1)} %other_ref.5) | copy-start | bytes 393220
  58.5 20.0 %copy-start.3 = (bf16[128,256]{1,0:T(8,128)(2,1)S(1)}, bf16[128,256]{1,0:T(8,128)(2,1)}, u32[]{:S(2)}) copy-start(bf16[128,256]{1,0:T(8,128)(2,1)} %grad_ref.1) | copy-start | bytes 196612
  107.0 9.6 %copy-start = (bf16[1,4,128,128]{3,2,1,0:T(8,128)(2,1)S(1)}, bf16[1,4,128,128]{3,2,1,0:T(8,128)(2,1)}, u32[]{:S(2)}) copy-start(bf16[1,4,128,128]{3,2,1,0:T(8,128)(2,1)} %param.20) | copy-start | bytes 393220

commit v10 on v9

--- a/solution.py
+++ b/solution.py
@@ -21,6 +21,12 @@
     return lax.all_to_all(
         values, axis, split_axis=0, concat_axis=0, tiled=True, axis_index_groups=groups
     )
+
+
+def pick(table, row_ids):
+    local_ids = jnp.arange(table.shape[0], dtype=jnp.int32)
+    chosen = (row_ids[:, None] == local_ids[None, :]).astype(table.dtype)
+    return dot(chosen, table, ((1,), (0,))).astype(table.dtype)
 
 
 def quarters(first, second):
@@ -45,9 +51,7 @@
     features_hbm,
     tiles_hbm,
     grad_hbm,
-    own_hbm,
     sent_hbm,
-    own_rows_ref,
     ids_ref,
     slots_ref,
     counts_ref,
@@ -55,7 +59,6 @@
     features_ref,
     tiles_ref,
     grad_ref,
-    own_ref,
     sent_ref,
     slots_scratch,
     grad_scratch,
@@ -78,7 +81,6 @@
                 (features_hbm, features_ref),
                 (tiles_hbm, tiles_ref),
                 (grad_hbm, grad_ref),
-                (own_hbm, own_ref),
             ]
         )
     ]
@@ -135,37 +137,23 @@
             out = pltpu.make_async_copy(sent_ref.at[to], sent_hbm.at[to], out_sems.at[to])
             out.start()
             outs.append(out)
-    own = jnp.broadcast_to(own_ref[...], (targets, targets)).astype(f32).T.astype(jnp.int32)
-    local_ids = lax.broadcasted_iota(jnp.int32, (targets, targets), 1)
-    chosen = [
-        jnp.where(own == local_ids + start, 1.0, 0.0).astype(bf16)
-        for start in range(0, locals_, targets)
-    ]
-    own_rows = dot(jnp.concatenate(chosen, axis=1), features_ref[...], ((1,), (0,)))
-    own_rows_ref[...] = own_rows.astype(bf16)
     for out in outs:
         out.wait()
 
 
-def pack(sample_ids, dest_slots, counts, blocks, features, tiles, grad, own, nx, na, nb, part, place):
+def pack(sample_ids, dest_slots, counts, blocks, features, tiles, grad, nx, na, nb, part, place):
     count, targets, _ = tiles.shape
     capacity, nodes = sample_ids.shape
     total = na * capacity + count * part + na + 8
     kernel = functools.partial(pack_kernel, nx=nx, na=na, nb=nb, place=place)
-    args = (sample_ids, dest_slots, counts, blocks, features, tiles, grad, own)
+    args = (sample_ids, dest_slots, counts, blocks, features, tiles, grad)
     held = [pltpu.VMEM(arg.shape, arg.dtype) for arg in args]
     held[3] = pltpu.SMEM(blocks.shape, blocks.dtype)
     return pl.pallas_call(
         kernel,
-        out_shape=[
-            jax.ShapeDtypeStruct((nx * nb, total, features.shape[1]), bf16),
-            jax.ShapeDtypeStruct((targets, features.shape[1]), bf16),
-        ],
+        out_shape=jax.ShapeDtypeStruct((nx * nb, total, features.shape[1]), bf16),
         in_specs=[pl.BlockSpec(memory_space=pltpu.HBM)] * len(args),
-        out_specs=[
-            pl.BlockSpec(memory_space=pltpu.HBM),
-            pl.BlockSpec(memory_space=pltpu.VMEM),
-        ],
+        out_specs=pl.BlockSpec(memory_space=pltpu.HBM),
         scratch_shapes=held
         + [
             pltpu.VMEM((nx * nb, total, features.shape[1]), bf16),
@@ -246,7 +234,7 @@
 
 def grads_kernel(
     got_ref,
-    self_ref,
+    self_grad_ref,
     other_ref,
     grad_ref,
     rows_ref,
@@ -260,7 +248,7 @@
     slice_at,
 ):
     feats, near = got_ref.shape[0], sent_ref.shape[0]
-    hidden = self_ref.shape[0]
+    hidden = self_grad_ref.shape[0]
     pre = got_ref[0, :hidden, :].astype(f32)
     for f in range(1, feats):
         pre += got_ref[f, :hidden, :].astype(f32)
@@ -274,8 +262,7 @@
     back_high = jnp.concatenate(back_high, axis=0)
     back_low = [got_ref[f, hidden + part :, :] for f in range(feats)]
     back_low = jnp.concatenate(back_low, axis=0)
-    grad = dot(self_ref[...], grad_ref[...], ((1,), (1,)))
-    grad += dot(other_ref[...], back_high, ((1,), (0,)))
+    grad = self_grad_ref[...] + dot(other_ref[...], back_high, ((1,), (0,)))
     grad += dot(other_ref[...], back_low, ((1,), (0,)))
     grad = (grad * slope).astype(bf16)
     rows_t = rows_ref[...].astype(f32).T.astype(bf16)
@@ -403,7 +390,7 @@
     tiles = tile_weights[0]
     count = tiles.shape[0]
 
-    sent, self_rows = pack(
+    sent = pack(
         sample_ids[0].T,
         dest_slots[0].T,
         send_counts,
@@ -411,7 +398,6 @@
         features,
         tiles,
         out_grad,
-        self_ids,
         nx,
         na,
         nb,
@@ -430,6 +416,7 @@
     )
     came = exchange(sent, "node", far_groups)
 
+    self_rows = pick(features, self_ids[0])
     sent, mean_high = in_vmem(
         functools.partial(first_kernel, part=part),
         [
@@ -453,7 +440,7 @@
             jax.ShapeDtypeStruct((part, targets), bf16),
         ],
         got,
-        self_two,
+        dot(self_two, out_grad, ((1,), (1,))),
         neighbour_two,
         out_grad,
         self_rows,

time: 133 us -> 134 us (level)
  blocking collectives: 126 us -> 68 us
  waiting for transfers between devices: 0 us -> 29.8 us
  starting transfers between devices: 0 us -> 26.9 us
    all_to_all x7 -> x5, blocking collectives: 126 us -> 68 us  [exchange(): lax.all_to_all(values, axis, split_axis=0, concat_axis=0, tiled=True, axi...]
    all_to_all x0 -> x2, waiting for transfers between devices: none -> 29.8 us  [exchange(): lax.all_to_all(values, axis, split_axis=0, concat_axis=0, tiled=True, axi...]
    all_to_all x0 -> x2, starting transfers between devices: none -> 26.9 us  [exchange(): lax.all_to_all(values, axis, split_axis=0, concat_axis=0, tiled=True, axi...]
    pallas_call x7, Pallas kernels: 3.02 us -> 4.51 us  [in_vmem(): pl.pallas_call(kernel, out_shape=out_shape, in_specs=[vmem] * len(args),...]
  transfers between devices with their start and end apart: 0 -> 2, of which waited for: 0 -> 2; matrix products, arithmetic and copies ran while one was open for 0% -> 0% of each run, Pallas kernels for 0% -> 0%
where the time goes in v10:
time: 134 us
  blocking collectives  68 us (51%)
  waiting for transfers between devices  29.8 us (22%)
  starting transfers between devices  26.9 us (20%)
  Pallas kernels  7.22 us (5%)
    all_to_all x5, blocking collectives, exchange(): lax.all_to_all(values, axis, split_axis=0, concat_axis=0, tiled=True, axi...  68 us
    all_to_all x2, waiting for transfers between devices, exchange(): lax.all_to_all(values, axis, split_axis=0, concat_axis=0, tiled=True, axi...  29.8 us
    all_to_all x2, starting transfers between devices, exchange(): lax.all_to_all(values, axis, split_axis=0, concat_axis=0, tiled=True, axi...  26.9 us
    pallas_call x7, Pallas kernels, in_vmem(): pl.pallas_call(kernel, out_shape=out_shape, in_specs=[vmem] * len(args),...  4.51 us
    pallas_call x1, Pallas kernels, pack(): pl.pallas_call(kernel, out_shape=jax.ShapeDtypeStruct((nx * nb, total, fe...  2.71 us
  transfers between devices with their start and end apart: 2, of which 2 were waited for; matrix products, arithmetic and copies ran while one was open for 0% of the time, Pallas kernels for 0%

profile of v10, /device:TPU:1, one launch (start us, length us, event | category | flops | bytes accessed | tf_op | source)
XLA Modules:
  0.0 133.7 jit_solution(9533216280645661590)
XLA Ops:
  0.6 2.7 %shard_map.155 = bf16[8,400,128]{2,1,0:T(8,128)(2,1)} custom-call(s32[32,64]{1,0:T(8,128)} %bitcast.13, s32[32,64]{1,0:T(8,128)} %bitcast.14, s32[64,64]{1,0:T(8,128)} %counts_hbm.1, s32[1,4]{1,0:T(1,128)} %blocks_hbm.1, bf16[512,128]{1,0:T(8,128)(2,1)} %features_hbm.1, bf16[4,128,128]{2,1,0:T(8,128)(2,1)} %bitcast.11, bf16[128,256]{1,0:T(8,128)(2,1)} %grad_ref.1), custom_call_target="tpu_custom_call" | custom-call | tf_op jit(solution)/shard_map/pallas_call | solution.py:152
  3.4 15.5 %all_to_all.35.got_ref = bf16[8,400,128]{2,1,0:T(8,128)(2,1)S(1)} all-to-all(bf16[8,400,128]{2,1,0:T(8,128)(2,1)} %shard_map.155), channel_id=1, replica_groups={{0,1,16,17,32,33,48,49},{2,3,18,19,34,35,50,51},{4,5,20,21,36,37,52,53}..., dimensions={0} | all-to-all | bytes 1638400 | tf_op jit(solution)/shard_map/all_to_all | solution.py:21
  18.9 1.4 %shard_map.156 = (bf16[8,168,128]{2,1,0:T(8,128)(2,1)}, bf16[8,16,128]{2,1,0:T(8,128)(2,1)S(1)}) custom-call(bf16[8,400,128]{2,1,0:T(8,128)(2,1)S(1)} %all_to_all.35.got_ref), custom_call_target="tpu_custom_call" | custom-call | tf_op jit(solution)/shard_map/pallas_call | solution.py:172
  20.3 0.0 copy-start.6
  20.3 16.9 %all-to-all-start.1 = ((bf16[8,168,128]{2,1,0:T(8,128)(2,1)}), bf16[8,168,128]{2,1,0:T(8,128)(2,1)S(1)}, u32[]{:S(2)}, u32[]{:S(2)}) async-start(bf16[8,168,128]{2,1,0:T(8,128)(2,1)} %get-tuple-element.12), calls=%async_computation.1 | async-start | bytes 688128 | tf_op jit(solution)/shard_map/all_to_all | solution.py:21
  37.2 0.0 copy-start.7
  37.3 0.0 copy-done.6
  37.3 0.6 copy-done.7
  37.9 0.0 copy-start.4
  37.9 0.0 copy-start.5
  37.9 0.2 convolution_convert_fusion.rows_ref
  38.1 19.1 %all-to-all-done.1.came_ref = bf16[8,168,128]{2,1,0:T(8,128)(2,1)S(1)} async-done(((bf16[8,168,128]{2,1,0:T(8,128)(2,1)}), bf16[8,168,128]{2,1,0:T(8,128)(2,1)S(1)}, u32[]{:S(2)}, u32[]{:S(2)}) %all-to-all-start.1) | async-done | bytes 344096 | tf_op jit(solution)/shard_map/all_to_all | solution.py:21
  57.3 0.0 copy-done.4
  57.3 0.0 copy-done.5
  57.3 1.2 shard_map.157
  58.5 0.0 copy-start
  58.5 0.0 copy-start.2
  58.5 10.0 %all-to-all-start.2 = ((bf16[8,320,128]{2,1,0:T(8,128)(2,1)}), bf16[8,320,128]{2,1,0:T(8,128)(2,1)S(1)}, u32[]{:S(2)}, u32[]{:S(2)}) async-start(bf16[8,320,128]{2,1,0:T(8,128)(2,1)} %get-tuple-element.13), calls=%async_computation.2 | async-start | bytes 1310720 | tf_op jit(solution)/shard_map/all_to_all | solution.py:21
  68.5 0.0 copy-done
  68.5 0.0 copy-done.2
  68.5 0.0 copy-start.3
  68.5 0.2 fusion.1.self_grad_ref
  68.7 10.7 %all-to-all-done.2.got_ref = bf16[8,320,128]{2,1,0:T(8,128)(2,1)S(1)} async-done(((bf16[8,320,128]{2,1,0:T(8,128)(2,1)}), bf16[8,320,128]{2,1,0:T(8,128)(2,1)S(1)}, u32[]{:S(2)}, u32[]{:S(2)}) %all-to-all-start.2) | async-done | bytes 655392 | tf_op jit(solution)/shard_map/all_to_all | solution.py:21
  79.4 0.0 copy-done.3
  79.4 0.4 shard_map.158
  79.8 8.2 %all_to_all.36.got_ref = bf16[8,80,128]{2,1,0:T(8,128)(2,1)S(1)} all-to-all(bf16[8,80,128]{2,1,0:T(8,128)(2,1)S(1)} %get-tuple-element.15), channel_id=1, replica_groups={{0,1,16,17,32,33,48,49},{2,3,18,19,34,35,50,51},{4,5,20,21,36,37,52,53}..., dimensions={0} | all-to-all | bytes 327680 | tf_op jit(solution)/shard_map/all_to_all | solution.py:21
  88.0 19.2 %all_to_all.37.got_ref = bf16[8,112,128]{2,1,0:T(8,128)(2,1)S(1)} all-to-all(bf16[8,112,128]{2,1,0:T(8,128)(2,1)S(1)} %shard_map.159), channel_id=1, replica_groups={{0,2,4,6,8,10,12,14},{1,3,5,7,9,11,13,15},{16,18,20,22,24,26,28,30},{17..., dimensions={0} | all-to-all | bytes 458752 | tf_op jit(solution)/shard_map/all_to_all | solution.py:21
  107.2 0.2 shard_map.160
  107.4 0.0 copy-start.1
  107.5 10.0 %all_to_all.38.got_ref.lower_ref = bf16[8,208,128]{2,1,0:T(8,128)(2,1)S(1)} all-to-all(bf16[8,208,128]{2,1,0:T(8,128)(2,1)S(1)} %shard_map.160), channel_id=1, replica_groups={{0,1,16,17,32,33,48,49},{2,3,18,19,34,35,50,51},{4,5,20,21,36,37,52,53}..., dimensions={0} | all-to-all | bytes 851968 | tf_op jit(solution)/shard_map/all_to_all | solution.py:21
  117.4 0.0 copy-done.1
  117.4 0.2 shard_map.161
  117.6 15.1 %all_to_all.39.got_ref = bf16[8,160,128]{2,1,0:T(8,128)(2,1)S(1)} all-to-all(bf16[8,160,128]{2,1,0:T(8,128)(2,1)S(1)} %shard_map.161), channel_id=1, replica_groups=mesh['feat'=8,'node'=64] {'feat'}, dimensions={0} | all-to-all | bytes 655360 | tf_op jit(solution)/shard_map/all_to_all | solution.py:21
  132.7 1.0 shard_map.162
  (1 shorter events, 0.0 us)
Async XLA Ops:
  20.3 16.9 %copy-start.6 = (bf16[512,128]{1,0:T(8,128)(2,1)S(1)}, bf16[512,128]{1,0:T(8,128)(2,1)}, u32[]{:S(2)}) copy-start(bf16[512,128]{1,0:T(8,128)(2,1)} %features_hbm.1) | copy-start | bytes 393220
  20.3 36.9 %all-to-all-start.1 = ((bf16[8,168,128]{2,1,0:T(8,128)(2,1)}), bf16[8,168,128]{2,1,0:T(8,128)(2,1)S(1)}, u32[]{:S(2)}, u32[]{:S(2)}) async-start(bf16[8,168,128]{2,1,0:T(8,128)(2,1)} %get-tuple-element.12), calls=%async_computation.1 | async-start | bytes 688128 | tf_op jit(solution)/shard_map/all_to_all | solution.py:21
  37.2 0.7 copy-start.7
  37.9 19.4 %copy-start.4 = (bf16[128,256]{1,0:T(8,128)(2,1)S(1)}, bf16[128,256]{1,0:T(8,128)(2,1)}, u32[]{:S(2)}) copy-start(bf16[128,256]{1,0:T(8,128)(2,1)} %self_ref.2) | copy-start | bytes 196612
  37.9 19.4 %copy-start.5 = (bf16[128,256]{1,0:T(8,128)(2,1)S(1)}, bf16[128,256]{1,0:T(8,128)(2,1)}, u32[]{:S(2)}) copy-start(bf16[128,256]{1,0:T(8,128)(2,1)} %other_ref.3) | copy-start | bytes 196612
  58.5 10.0 %copy-start = (bf16[128,256]{1,0:T(8,128)(2,1)S(1)}, bf16[128,256]{1,0:T(8,128)(2,1)}, u32[]{:S(2)}) copy-start(bf16[128,256]{1,0:T(8,128)(2,1)} %grad_ref.1) | copy-start | bytes 196612
  58.5 10.0 %copy-start.2 = (bf16[256,256]{1,0:T(8,128)(2,1)S(1)}, bf16[256,256]{1,0:T(8,128)(2,1)}, u32[]{:S(2)}) copy-start(bf16[256,256]{1,0:T(8,128)(2,1)} %self_ref.3) | copy-start | bytes 393220
  58.5 20.9 %all-to-all-start.2 = ((bf16[8,320,128]{2,1,0:T(8,128)(2,1)}), bf16[8,320,128]{2,1,0:T(8,128)(2,1)S(1)}, u32[]{:S(2)}, u32[]{:S(2)}) async-start(bf16[8,320,128]{2,1,0:T(8,128)(2,1)} %get-tuple-element.13), calls=%async_computation.2 | async-start | bytes 1310720 | tf_op jit(solution)/shard_map/all_to_all | solution.py:21
  68.5 10.9 %copy-start.3 = (bf16[256,256]{1,0:T(8,128)(2,1)S(1)}, bf16[256,256]{1,0:T(8,128)(2,1)}, u32[]{:S(2)}) copy-start(bf16[256,256]{1,0:T(8,128)(2,1)} %other_ref.5) | copy-start | bytes 393220
  107.4 10.0 %copy-start.1 = (bf16[1,4,128,128]{3,2,1,0:T(8,128)(2,1)S(1)}, bf16[1,4,128,128]{3,2,1,0:T(8,128)(2,1)}, u32[]{:S(2)}) copy-start(bf16[1,4,128,128]{3,2,1,0:T(8,128)(2,1)} %param.20) | copy-start | bytes 393220

commit v11 on v10

--- a/solution.py
+++ b/solution.py
@@ -184,7 +184,10 @@
     return high, (values - high.astype(f32)).astype(bf16)
 
 
-def gather_kernel(got_ref, sent_ref, marks_ref, *, capacity, part, count):
+def gather_kernel(
+    got_ref, rows_ref, sent_ref, marks_ref, rows_t_ref, *, capacity, part, count
+):
+    rows_t_ref[...] = rows_ref[...].astype(f32).T.astype(bf16)
     near = got_ref.shape[0]
     far, _, targets = sent_ref.shape
     lanes = targets // capacity
@@ -227,17 +230,15 @@
     pre += dot(high, other_ref[...], ((1,), (0,)))
     pre += dot(low, other_ref[...], ((1,), (0,)))
     back = halve(came[targets : targets + part])
-    all_rows = jnp.concatenate([pre.T.astype(bf16), *back], axis=0)
-    for f in range(sent_ref.shape[0]):
-        sent_ref[f] = all_rows
+    sent_ref[...] = jnp.concatenate([pre.T.astype(bf16), *back], axis=0)
 
 
 def grads_kernel(
     got_ref,
-    self_grad_ref,
+    self_ref,
     other_ref,
     grad_ref,
-    rows_ref,
+    rows_t_ref,
     mean_ref,
     sent_ref,
     hidden_ref,
@@ -248,7 +249,7 @@
     slice_at,
 ):
     feats, near = got_ref.shape[0], sent_ref.shape[0]
-    hidden = self_grad_ref.shape[0]
+    hidden = self_ref.shape[0]
     pre = got_ref[0, :hidden, :].astype(f32)
     for f in range(1, feats):
         pre += got_ref[f, :hidden, :].astype(f32)
@@ -262,12 +263,12 @@
     back_high = jnp.concatenate(back_high, axis=0)
     back_low = [got_ref[f, hidden + part :, :] for f in range(feats)]
     back_low = jnp.concatenate(back_low, axis=0)
-    grad = self_grad_ref[...] + dot(other_ref[...], back_high, ((1,), (0,)))
+    grad = dot(self_ref[...], grad_ref[...], ((1,), (1,)))
+    grad += dot(other_ref[...], back_high, ((1,), (0,)))
     grad += dot(other_ref[...], back_low, ((1,), (0,)))
     grad = (grad * slope).astype(bf16)
-    rows_t = rows_ref[...].astype(f32).T.astype(bf16)
     mean_t = mean_ref[...].astype(f32).T.astype(bf16)
-    lower = quarters(dot(rows_t, grad, ((1,), (1,))), dot(mean_t, grad, ((1,), (1,))))
+    lower = quarters(dot(rows_t_ref[...], grad, ((1,), (1,))), dot(mean_t, grad, ((1,), (1,))))
     upper = quarters(
         dot(mine, grad_ref[...], ((1,), (0,))),
         dot(mine, back_high, ((1,), (1,))) + dot(mine, back_low, ((1,), (1,))),
@@ -405,22 +406,24 @@
         where_am_i,
     )
     got = exchange(sent, "node", near_groups)
-
-    sent, marks = in_vmem(
+    self_rows = pick(features, self_ids[0])
+
+    sent, marks, self_rows_t = in_vmem(
         functools.partial(gather_kernel, capacity=capacity, part=part, count=count),
         [
             jax.ShapeDtypeStruct((na, targets + part + 8, width), bf16),
             jax.ShapeDtypeStruct((near, na + 8, targets), bf16),
+            jax.ShapeDtypeStruct((width, targets), bf16),
         ],
         got,
+        self_rows,
     )
     came = exchange(sent, "node", far_groups)
 
-    self_rows = pick(features, self_ids[0])
     sent, mean_high = in_vmem(
         functools.partial(first_kernel, part=part),
         [
-            jax.ShapeDtypeStruct((feats, hidden + 2 * part, targets), bf16),
+            jax.ShapeDtypeStruct((hidden + 2 * part, targets), bf16),
             jax.ShapeDtypeStruct((targets, width), bf16),
         ],
         came,
@@ -428,7 +431,7 @@
         self_one,
         neighbour_one,
     )
-    got = exchange(sent, "feat")
+    got = lax.all_gather(sent, "feat")
 
     half = hidden // 2
     rows_each, share = 4 * width // near, 4 * part // near
@@ -440,10 +443,10 @@
             jax.ShapeDtypeStruct((part, targets), bf16),
         ],
         got,
-        dot(self_two, out_grad, ((1,), (1,))),
+        self_two,
         neighbour_two,
         out_grad,
-        self_rows,
+        self_rows_t,
         mean_high,
         scratch_shapes=[pltpu.VMEM((hidden, targets), f32)],
     )

time: 134 us -> 132 us (0.985)
  blocking collectives: 68 us -> 110 us
  waiting for transfers between devices: 29.8 us -> 8.35 us
  starting transfers between devices: 26.9 us -> 6.35 us
  Pallas kernels: 7.22 us -> 5.71 us
    all_to_all x5, blocking collectives: 68 us -> 91.4 us  [exchange(): lax.all_to_all(values, axis, split_axis=0, concat_axis=0, tiled=True, axi...]
    all_to_all x2 -> x1, waiting for transfers between devices: 29.8 us -> 8.35 us  [exchange(): lax.all_to_all(values, axis, split_axis=0, concat_axis=0, tiled=True, axi...]
    all_to_all x2 -> x1, starting transfers between devices: 26.9 us -> 6.35 us  [exchange(): lax.all_to_all(values, axis, split_axis=0, concat_axis=0, tiled=True, axi...]
    all_gather x0 -> x1, blocking collectives: none -> 18.5 us  [shards(): got = lax.all_gather(sent, 'feat')]
    pallas_call x7, Pallas kernels: 4.51 us -> 2.99 us  [in_vmem(): pl.pallas_call(kernel, out_shape=out_shape, in_specs=[vmem] * len(args),...]
  transfers between devices with their start and end apart: 2 -> 1, of which waited for: 2 -> 1; matrix products, arithmetic and copies ran while one was open for 0% -> 0% of each run, Pallas kernels for 0% -> 0%
where the time goes in v11:
time: 132 us
  blocking collectives  110 us (83%)
  waiting for transfers between devices  8.35 us (6%)
  starting transfers between devices  6.35 us (5%)
  Pallas kernels  5.71 us (4%)
    all_to_all x5, blocking collectives, exchange(): lax.all_to_all(values, axis, split_axis=0, concat_axis=0, tiled=True, axi...  91.4 us
    all_gather x1, blocking collectives, shards(): got = lax.all_gather(sent, 'feat')  18.5 us
    all_to_all x1, waiting for transfers between devices, exchange(): lax.all_to_all(values, axis, split_axis=0, concat_axis=0, tiled=True, axi...  8.35 us
    all_to_all x1, starting transfers between devices, exchange(): lax.all_to_all(values, axis, split_axis=0, concat_axis=0, tiled=True, axi...  6.35 us
    pallas_call x7, Pallas kernels, in_vmem(): pl.pallas_call(kernel, out_shape=out_shape, in_specs=[vmem] * len(args),...  2.99 us
    pallas_call x1, Pallas kernels, pack(): pl.pallas_call(kernel, out_shape=jax.ShapeDtypeStruct((nx * nb, total, fe...  2.71 us
  transfers between devices with their start and end apart: 1, of which 1 were waited for; matrix products, arithmetic and copies ran while one was open for 0% of the time, Pallas kernels for 0%

profile of v11, /device:TPU:1, one launch (start us, length us, event | category | flops | bytes accessed | tf_op | source)
XLA Modules:
  0.0 131.9 jit_solution(17090842254496976949)
XLA Ops:
  0.6 2.7 %shard_map.155 = bf16[8,400,128]{2,1,0:T(8,128)(2,1)} custom-call(s32[32,64]{1,0:T(8,128)} %bitcast.13, s32[32,64]{1,0:T(8,128)} %bitcast.14, s32[64,64]{1,0:T(8,128)} %counts_hbm.1, s32[1,4]{1,0:T(1,128)} %blocks_hbm.1, bf16[512,128]{1,0:T(8,128)(2,1)} %features_hbm.1, bf16[4,128,128]{2,1,0:T(8,128)(2,1)} %bitcast.11, bf16[128,256]{1,0:T(8,128)(2,1)} %grad_ref.1), custom_call_target="tpu_custom_call" | custom-call | tf_op jit(solution)/shard_map/pallas_call | solution.py:152
  3.4 0.0 copy-start.6
  3.4 6.3 %all-to-all-start = ((bf16[8,400,128]{2,1,0:T(8,128)(2,1)}), bf16[8,400,128]{2,1,0:T(8,128)(2,1)S(1)}, u32[]{:S(2)}, u32[]{:S(2)}) async-start(bf16[8,400,128]{2,1,0:T(8,128)(2,1)} %shard_map.155), calls=%async_computation | async-start | bytes 1638400 | tf_op jit(solution)/shard_map/all_to_all | solution.py:21
  9.7 0.0 copy-start.7
  9.7 0.0 copy-done.6
  9.7 0.6 copy-done.7
  10.4 0.2 convolution_convert_fusion.rows_ref
  10.6 8.3 %all-to-all-done.got_ref = bf16[8,400,128]{2,1,0:T(8,128)(2,1)S(1)} async-done(((bf16[8,400,128]{2,1,0:T(8,128)(2,1)}), bf16[8,400,128]{2,1,0:T(8,128)(2,1)S(1)}, u32[]{:S(2)}, u32[]{:S(2)}) %all-to-all-start) | async-done | bytes 819232 | tf_op jit(solution)/shard_map/all_to_all | solution.py:21
  19.0 0.7 shard_map.156
  19.7 0.0 copy-start.4
  19.7 0.0 copy-start.5
  19.7 37.8 %all_to_all.30.came_ref = bf16[8,168,128]{2,1,0:T(8,128)(2,1)S(1)} all-to-all(bf16[8,168,128]{2,1,0:T(8,128)(2,1)S(1)} %get-tuple-element.13), channel_id=1, replica_groups={{0,2,4,6,8,10,12,14},{1,3,5,7,9,11,13,15},{16,18,20,22,24,26,28,30},{17..., dimensions={0} | all-to-all | bytes 688128 | tf_op jit(solution)/shard_map/all_to_all | solution.py:21
  57.4 0.0 copy-done.4
  57.4 0.0 copy-done.5
  57.4 0.3 shard_map.157
  57.8 0.0 copy-start.1
  57.8 0.0 copy-start.2
  57.8 0.0 copy-start.3
  57.8 18.5 %all-gather = bf16[2560,128]{1,0:T(8,128)(2,1)S(1)} all-gather(bf16[320,128]{1,0:T(8,128)(2,1)S(1)} %get-tuple-element.14), channel_id=2, replica_groups=mesh['feat'=8,'node'=64] {'feat'}, dimensions={0}, use_global_device_ids=true | all-gather | bytes 737280 | tf_op jit(solution)/shard_map/all_gather | solution.py:434
  76.3 0.0 copy-done.1
  76.3 0.0 copy-done.2
  76.3 0.0 copy-done.3
  76.3 0.5 shard_map.158
  76.8 8.6 %all_to_all.31.got_ref = bf16[8,80,128]{2,1,0:T(8,128)(2,1)S(1)} all-to-all(bf16[8,80,128]{2,1,0:T(8,128)(2,1)S(1)} %get-tuple-element.17), channel_id=1, replica_groups={{0,1,16,17,32,33,48,49},{2,3,18,19,34,35,50,51},{4,5,20,21,36,37,52,53}..., dimensions={0} | all-to-all | bytes 327680 | tf_op jit(solution)/shard_map/all_to_all | solution.py:21
  85.5 17.9 %all_to_all.32.got_ref = bf16[8,112,128]{2,1,0:T(8,128)(2,1)S(1)} all-to-all(bf16[8,112,128]{2,1,0:T(8,128)(2,1)S(1)} %shard_map.159), channel_id=1, replica_groups={{0,2,4,6,8,10,12,14},{1,3,5,7,9,11,13,15},{16,18,20,22,24,26,28,30},{17..., dimensions={0} | all-to-all | bytes 458752 | tf_op jit(solution)/shard_map/all_to_all | solution.py:21
  103.4 0.2 shard_map.160
  103.6 0.0 copy-start
  103.6 10.3 %all_to_all.33.got_ref.lower_ref = bf16[8,208,128]{2,1,0:T(8,128)(2,1)S(1)} all-to-all(bf16[8,208,128]{2,1,0:T(8,128)(2,1)S(1)} %shard_map.160), channel_id=1, replica_groups={{0,1,16,17,32,33,48,49},{2,3,18,19,34,35,50,51},{4,5,20,21,36,37,52,53}..., dimensions={0} | all-to-all | bytes 851968 | tf_op jit(solution)/shard_map/all_to_all | solution.py:21
  113.9 0.0 copy-done
  113.9 0.2 shard_map.161
  114.1 16.8 %all_to_all.34.got_ref = bf16[8,160,128]{2,1,0:T(8,128)(2,1)S(1)} all-to-all(bf16[8,160,128]{2,1,0:T(8,128)(2,1)S(1)} %shard_map.161), channel_id=1, replica_groups=mesh['feat'=8,'node'=64] {'feat'}, dimensions={0} | all-to-all | bytes 655360 | tf_op jit(solution)/shard_map/all_to_all | solution.py:21
  130.9 1.0 shard_map.162
  (1 shorter events, 0.0 us)
Async XLA Ops:
  3.4 6.4 %copy-start.6 = (bf16[512,128]{1,0:T(8,128)(2,1)S(1)}, bf16[512,128]{1,0:T(8,128)(2,1)}, u32[]{:S(2)}) copy-start(bf16[512,128]{1,0:T(8,128)(2,1)} %features_hbm.1) | copy-start | bytes 393220
  3.4 15.6 %all-to-all-start = ((bf16[8,400,128]{2,1,0:T(8,128)(2,1)}), bf16[8,400,128]{2,1,0:T(8,128)(2,1)S(1)}, u32[]{:S(2)}, u32[]{:S(2)}) async-start(bf16[8,400,128]{2,1,0:T(8,128)(2,1)} %shard_map.155), calls=%async_computation | async-start | bytes 1638400 | tf_op jit(solution)/shard_map/all_to_all | solution.py:21
  9.7 0.7 copy-start.7
  19.7 37.8 %copy-start.4 = (bf16[128,256]{1,0:T(8,128)(2,1)S(1)}, bf16[128,256]{1,0:T(8,128)(2,1)}, u32[]{:S(2)}) copy-start(bf16[128,256]{1,0:T(8,128)(2,1)} %self_ref.3) | copy-start | bytes 196612
  19.7 37.8 %copy-start.5 = (bf16[128,256]{1,0:T(8,128)(2,1)S(1)}, bf16[128,256]{1,0:T(8,128)(2,1)}, u32[]{:S(2)}) copy-start(bf16[128,256]{1,0:T(8,128)(2,1)} %other_ref.3) | copy-start | bytes 196612
  57.8 18.5 %copy-start.1 = (bf16[256,256]{1,0:T(8,128)(2,1)S(1)}, bf16[256,256]{1,0:T(8,128)(2,1)}, u32[]{:S(2)}) copy-start(bf16[256,256]{1,0:T(8,128)(2,1)} %self_ref.5) | copy-start | bytes 393220
  57.8 18.5 %copy-start.2 = (bf16[256,256]{1,0:T(8,128)(2,1)S(1)}, bf16[256,256]{1,0:T(8,128)(2,1)}, u32[]{:S(2)}) copy-start(bf16[256,256]{1,0:T(8,128)(2,1)} %other_ref.5) | copy-start | bytes 393220
  57.8 18.5 %copy-start.3 = (bf16[128,256]{1,0:T(8,128)(2,1)S(1)}, bf16[128,256]{1,0:T(8,128)(2,1)}, u32[]{:S(2)}) copy-start(bf16[128,256]{1,0:T(8,128)(2,1)} %grad_ref.1) | copy-start | bytes 196612
  103.6 10.4 %copy-start = (bf16[1,4,128,128]{3,2,1,0:T(8,128)(2,1)S(1)}, bf16[1,4,128,128]{3,2,1,0:T(8,128)(2,1)}, u32[]{:S(2)}) copy-start(bf16[1,4,128,128]{3,2,1,0:T(8,128)(2,1)} %param.20) | copy-start | bytes 393220

commit v12 on v11

--- a/solution.py
+++ b/solution.py
@@ -86,8 +86,6 @@
     ]
     for copy in copies:
         copy.start()
-    for copy in copies:
-        copy.wait()
     device, feat = place()
     near = nx * nb
     capacity, nodes = ids_ref.shape
@@ -98,6 +96,22 @@
     lanes = targets // capacity
     near_at = near_index(device, na, nb)
 
+    near_owners = [
+        [(x * na + a) * nb + b for a in range(na)] for x in range(nx) for b in range(nb)
+    ]
+    local_ids = lax.broadcasted_iota(jnp.int32, (capacity, locals_), 1)
+    copies[0].wait()
+    copies[4].wait()
+    for to, owners in enumerate(near_owners):
+        chosen = jnp.concatenate(
+            [jnp.where(ids_ref[:, o : o + 1] == local_ids, 1.0, 0.0).astype(bf16) for o in owners],
+            axis=0,
+        )
+        rows = dot(chosen, features_ref[...], ((1,), (0,)))
+        sent_ref[to, : na * capacity, :] = rows.astype(bf16)
+
+    for n in (1, 2, 3, 5, 6):
+        copies[n].wait()
     used = lax.broadcasted_iota(jnp.int32, (capacity, nodes), 0) < counts_ref[pl.ds(device, 1), :]
     slots = jnp.where(used, slots_ref[...], targets).astype(f32)
     slots = jnp.concatenate([slots] * lanes, axis=0)
@@ -109,34 +123,23 @@
     terms = [dot(grad_t, tiles_ref[k], ((1,), (0,))) for k in range(count)]
     blocks = [blocks_ref[0, k] for k in range(count)]
     row = lax.broadcasted_iota(jnp.int32, (8, targets), 0)
-    far_rows = jnp.zeros((8, targets), jnp.int32)
+    marks = jnp.zeros((8, targets), jnp.int32)
     for k in range(count):
-        far_rows = jnp.where(row == k, blocks[k] % (na * nb) // nb, far_rows)
-        far_rows = jnp.where(row == count + k, blocks[k] // (na * nb) * nb + blocks[k] % nb, far_rows)
-    far_rows = far_rows.astype(f32)
-    local_ids = lax.broadcasted_iota(jnp.int32, (capacity, locals_), 1)
+        marks = jnp.where(row == k, blocks[k] % (na * nb) // nb, marks)
+        marks = jnp.where(row == count + k, near_index(blocks[k], na, nb), marks)
+    marks = marks.astype(f32)
     outs = []
-    for x in range(nx):
-        for b in range(nb):
-            to = x * nb + b
-            owners = [(x * na + a) * nb + b for a in range(na)]
-            chosen = jnp.concatenate(
-                [jnp.where(ids_ref[:, o : o + 1] == local_ids, 1.0, 0.0).astype(bf16) for o in owners],
-                axis=0,
-            )
-            rows = dot(chosen, features_ref[...], ((1,), (0,)))
-            sent_ref[to, : na * capacity, :] = rows.astype(bf16)
-            at = na * capacity
-            for k in range(count):
-                there = blocks[k] // (na * nb) * nb + blocks[k] % nb == to
-                term = jnp.where(there, terms[k], 0.0)
-                sent_ref[to, at : at + part, :] = term.astype(bf16)
-                at += part
-            slot_rows = slots_scratch[pl.ds(owners[0], na, stride=nb), :]
-            sent_ref[to, at : at + na + 8, :] = jnp.concatenate([slot_rows, far_rows], 0).astype(bf16)
-            out = pltpu.make_async_copy(sent_ref.at[to], sent_hbm.at[to], out_sems.at[to])
-            out.start()
-            outs.append(out)
+    for to, owners in enumerate(near_owners):
+        at = na * capacity
+        for k in range(count):
+            term = jnp.where(near_index(blocks[k], na, nb) == to, terms[k], 0.0)
+            sent_ref[to, at : at + part, :] = term.astype(bf16)
+            at += part
+        slot_rows = slots_scratch[pl.ds(owners[0], na, stride=nb), :]
+        sent_ref[to, at : at + na + 8, :] = jnp.concatenate([slot_rows, marks], 0).astype(bf16)
+        out = pltpu.make_async_copy(sent_ref.at[to], sent_hbm.at[to], out_sems.at[to])
+        out.start()
+        outs.append(out)
     for out in outs:
         out.wait()
 
@@ -197,7 +200,8 @@
         marks_ref[n] = got_ref[n, at : at + far + 8, :]
     slots = [sum(marks[h : h + lanes])[:far] for h in range(0, near, lanes)]
     nodes = lax.broadcasted_iota(jnp.int32, (targets, targets), 0).astype(f32)
-    ones = jnp.ones((8, targets), bf16)
+    extra = sent_ref.shape[1] - targets - part
+    ones = jnp.ones((extra, targets), bf16)
     back = [jnp.zeros((part, targets), f32) for _ in range(far)]
     for n in range(near):
         for k in range(count):
@@ -207,7 +211,7 @@
             back = [back[a] + jnp.where(mark == float(a), term, 0.0) for a in range(far)]
     for a in range(far):
         total = jnp.zeros((targets, targets), f32)
-        degree = jnp.zeros((8, targets), f32)
+        degree = jnp.zeros((extra, targets), f32)
         for h in range(near // lanes):
             chosen = jnp.where(slots[h][a : a + 1, :] == nodes, 1.0, 0.0).astype(bf16)
             rows = [
@@ -411,7 +415,7 @@
     sent, marks, self_rows_t = in_vmem(
         functools.partial(gather_kernel, capacity=capacity, part=part, count=count),
         [
-            jax.ShapeDtypeStruct((na, targets + part + 8, width), bf16),
+            jax.ShapeDtypeStruct((na, targets + part + 16, width), bf16),
             jax.ShapeDtypeStruct((near, na + 8, targets), bf16),
             jax.ShapeDtypeStruct((width, targets), bf16),
         ],

time: 132 us -> 134 us (1.015)
  no operation moved by 1% of the time
where the time goes in v12:
time: 134 us; the launch traced here: 133 us
  blocking collectives  111 us (83%)
  waiting for transfers between devices  8.35 us (6%)
  starting transfers between devices  6.35 us (5%)
  Pallas kernels  6.24 us (5%)
    all_to_all x5, blocking collectives, exchange(): lax.all_to_all(values, axis, split_axis=0, concat_axis=0, tiled=True, axi...  91.6 us
    all_gather x1, blocking collectives, shards(): got = lax.all_gather(sent, 'feat')  19.1 us
    all_to_all x1, waiting for transfers between devices, exchange(): lax.all_to_all(values, axis, split_axis=0, concat_axis=0, tiled=True, axi...  8.35 us
    all_to_all x1, starting transfers between devices, exchange(): lax.all_to_all(values, axis, split_axis=0, concat_axis=0, tiled=True, axi...  6.35 us
    pallas_call x7, Pallas kernels, in_vmem(): pl.pallas_call(kernel, out_shape=out_shape, in_specs=[vmem] * len(args),...  3.21 us
    pallas_call x1, Pallas kernels, pack(): pl.pallas_call(kernel, out_shape=jax.ShapeDtypeStruct((nx * nb, total, fe...  3.03 us
  transfers between devices with their start and end apart: 1, of which 1 were waited for; matrix products, arithmetic and copies ran while one was open for 0% of the time, Pallas kernels for 0%

profile of v12, /device:TPU:1, one launch (start us, length us, event | category | flops | bytes accessed | tf_op | source)
XLA Modules:
  0.0 133.3 jit_solution(7554096800616567438)
XLA Ops:
  0.6 3.0 %shard_map.155 = bf16[8,400,128]{2,1,0:T(8,128)(2,1)} custom-call(s32[32,64]{1,0:T(8,128)} %bitcast.13, s32[32,64]{1,0:T(8,128)} %bitcast.14, s32[64,64]{1,0:T(8,128)} %counts_hbm.1, s32[1,4]{1,0:T(1,128)} %blocks_hbm.1, bf16[512,128]{1,0:T(8,128)(2,1)} %features_hbm.1, bf16[4,128,128]{2,1,0:T(8,128)(2,1)} %bitcast.11, bf16[128,256]{1,0:T(8,128)(2,1)} %grad_ref.1), custom_call_target="tpu_custom_call" | custom-call | tf_op jit(solution)/shard_map/pallas_call | solution.py:155
  3.7 0.0 copy-start.6
  3.7 6.3 %all-to-all-start = ((bf16[8,400,128]{2,1,0:T(8,128)(2,1)}), bf16[8,400,128]{2,1,0:T(8,128)(2,1)S(1)}, u32[]{:S(2)}, u32[]{:S(2)}) async-start(bf16[8,400,128]{2,1,0:T(8,128)(2,1)} %shard_map.155), calls=%async_computation | async-start | bytes 1638400 | tf_op jit(solution)/shard_map/all_to_all | solution.py:21
  10.0 0.0 copy-start.7
  10.0 0.0 copy-done.6
  10.0 0.6 copy-done.7
  10.7 0.2 convolution_convert_fusion.rows_ref
  10.9 8.3 %all-to-all-done.got_ref = bf16[8,400,128]{2,1,0:T(8,128)(2,1)S(1)} async-done(((bf16[8,400,128]{2,1,0:T(8,128)(2,1)}), bf16[8,400,128]{2,1,0:T(8,128)(2,1)S(1)}, u32[]{:S(2)}, u32[]{:S(2)}) %all-to-all-start) | async-done | bytes 819232 | tf_op jit(solution)/shard_map/all_to_all | solution.py:21
  19.3 0.9 shard_map.156
  20.2 0.0 copy-start.4
  20.2 0.0 copy-start.5
  20.2 37.9 %all_to_all.30.came_ref = bf16[8,176,128]{2,1,0:T(8,128)(2,1)S(1)} all-to-all(bf16[8,176,128]{2,1,0:T(8,128)(2,1)S(1)} %get-tuple-element.13), channel_id=1, replica_groups={{0,2,4,6,8,10,12,14},{1,3,5,7,9,11,13,15},{16,18,20,22,24,26,28,30},{17..., dimensions={0} | all-to-all | bytes 720896 | tf_op jit(solution)/shard_map/all_to_all | solution.py:21
  58.1 0.0 copy-done.4
  58.1 0.0 copy-done.5
  58.1 0.3 shard_map.157
  58.4 0.0 copy-start.1
  58.4 0.0 copy-start.2
  58.4 0.0 copy-start.3
  58.4 19.1 %all-gather = bf16[2560,128]{1,0:T(8,128)(2,1)S(1)} all-gather(bf16[320,128]{1,0:T(8,128)(2,1)S(1)} %get-tuple-element.14), channel_id=2, replica_groups=mesh['feat'=8,'node'=64] {'feat'}, dimensions={0}, use_global_device_ids=true | all-gather | bytes 737280 | tf_op jit(solution)/shard_map/all_gather | solution.py:438
  77.5 0.0 copy-done.1
  77.5 0.0 copy-done.2
  77.5 0.0 copy-done.3
  77.5 0.5 shard_map.158
  78.1 8.7 %all_to_all.31.got_ref = bf16[8,80,128]{2,1,0:T(8,128)(2,1)S(1)} all-to-all(bf16[8,80,128]{2,1,0:T(8,128)(2,1)S(1)} %get-tuple-element.17), channel_id=1, replica_groups={{0,1,16,17,32,33,48,49},{2,3,18,19,34,35,50,51},{4,5,20,21,36,37,52,53}..., dimensions={0} | all-to-all | bytes 327680 | tf_op jit(solution)/shard_map/all_to_all | solution.py:21
  86.8 17.6 %all_to_all.32.got_ref = bf16[8,112,128]{2,1,0:T(8,128)(2,1)S(1)} all-to-all(bf16[8,112,128]{2,1,0:T(8,128)(2,1)S(1)} %shard_map.159), channel_id=1, replica_groups={{0,2,4,6,8,10,12,14},{1,3,5,7,9,11,13,15},{16,18,20,22,24,26,28,30},{17..., dimensions={0} | all-to-all | bytes 458752 | tf_op jit(solution)/shard_map/all_to_all | solution.py:21
  104.4 0.2 shard_map.160
  104.6 0.0 copy-start
  104.6 10.6 %all_to_all.33.got_ref.lower_ref = bf16[8,208,128]{2,1,0:T(8,128)(2,1)S(1)} all-to-all(bf16[8,208,128]{2,1,0:T(8,128)(2,1)S(1)} %shard_map.160), channel_id=1, replica_groups={{0,1,16,17,32,33,48,49},{2,3,18,19,34,35,50,51},{4,5,20,21,36,37,52,53}..., dimensions={0} | all-to-all | bytes 851968 | tf_op jit(solution)/shard_map/all_to_all | solution.py:21
  115.2 0.0 copy-done
  115.2 0.2 shard_map.161
  115.4 16.9 %all_to_all.34.got_ref = bf16[8,160,128]{2,1,0:T(8,128)(2,1)S(1)} all-to-all(bf16[8,160,128]{2,1,0:T(8,128)(2,1)S(1)} %shard_map.161), channel_id=1, replica_groups=mesh['feat'=8,'node'=64] {'feat'}, dimensions={0} | all-to-all | bytes 655360 | tf_op jit(solution)/shard_map/all_to_all | solution.py:21
  132.3 1.0 shard_map.162
  (1 shorter events, 0.0 us)
Async XLA Ops:
  3.7 6.4 %copy-start.6 = (bf16[512,128]{1,0:T(8,128)(2,1)S(1)}, bf16[512,128]{1,0:T(8,128)(2,1)}, u32[]{:S(2)}) copy-start(bf16[512,128]{1,0:T(8,128)(2,1)} %features_hbm.1) | copy-start | bytes 393220
  3.7 15.6 %all-to-all-start = ((bf16[8,400,128]{2,1,0:T(8,128)(2,1)}), bf16[8,400,128]{2,1,0:T(8,128)(2,1)S(1)}, u32[]{:S(2)}, u32[]{:S(2)}) async-start(bf16[8,400,128]{2,1,0:T(8,128)(2,1)} %shard_map.155), calls=%async_computation | async-start | bytes 1638400 | tf_op jit(solution)/shard_map/all_to_all | solution.py:21
  10.0 0.7 copy-start.7
  20.2 37.9 %copy-start.4 = (bf16[128,256]{1,0:T(8,128)(2,1)S(1)}, bf16[128,256]{1,0:T(8,128)(2,1)}, u32[]{:S(2)}) copy-start(bf16[128,256]{1,0:T(8,128)(2,1)} %self_ref.3) | copy-start | bytes 196612
  20.2 37.9 %copy-start.5 = (bf16[128,256]{1,0:T(8,128)(2,1)S(1)}, bf16[128,256]{1,0:T(8,128)(2,1)}, u32[]{:S(2)}) copy-start(bf16[128,256]{1,0:T(8,128)(2,1)} %other_ref.3) | copy-start | bytes 196612
  58.4 19.1 %copy-start.1 = (bf16[256,256]{1,0:T(8,128)(2,1)S(1)}, bf16[256,256]{1,0:T(8,128)(2,1)}, u32[]{:S(2)}) copy-start(bf16[256,256]{1,0:T(8,128)(2,1)} %self_ref.5) | copy-start | bytes 393220
  58.4 19.1 %copy-start.2 = (bf16[256,256]{1,0:T(8,128)(2,1)S(1)}, bf16[256,256]{1,0:T(8,128)(2,1)}, u32[]{:S(2)}) copy-start(bf16[256,256]{1,0:T(8,128)(2,1)} %other_ref.5) | copy-start | bytes 393220
  58.4 19.1 %copy-start.3 = (bf16[128,256]{1,0:T(8,128)(2,1)S(1)}, bf16[128,256]{1,0:T(8,128)(2,1)}, u32[]{:S(2)}) copy-start(bf16[128,256]{1,0:T(8,128)(2,1)} %grad_ref.1) | copy-start | bytes 196612
  104.6 10.6 %copy-start = (bf16[1,4,128,128]{3,2,1,0:T(8,128)(2,1)S(1)}, bf16[1,4,128,128]{3,2,1,0:T(8,128)(2,1)}, u32[]{:S(2)}) copy-start(bf16[1,4,128,128]{3,2,1,0:T(8,128)(2,1)} %param.20) | copy-start | bytes 393220

commit v13 on v11

--- a/solution.py
+++ b/solution.py
@@ -230,7 +230,17 @@
     pre += dot(high, other_ref[...], ((1,), (0,)))
     pre += dot(low, other_ref[...], ((1,), (0,)))
     back = halve(came[targets : targets + part])
-    sent_ref[...] = jnp.concatenate([pre.T.astype(bf16), *back], axis=0)
+    all_rows = jnp.concatenate([pre.T.astype(bf16), *back], axis=0)
+    for y in range(sent_ref.shape[0]):
+        sent_ref[y] = all_rows
+
+
+def pair_kernel(got_ref, sent_ref, *, hidden):
+    pre = got_ref[0, :hidden, :].astype(f32)
+    for y in range(1, got_ref.shape[0]):
+        pre += got_ref[y, :hidden, :].astype(f32)
+    back = [got_ref[y, hidden:, :] for y in range(got_ref.shape[0])]
+    sent_ref[...] = jnp.concatenate([*halve(pre), *back], axis=0)
 
 
 def grads_kernel(
@@ -248,20 +258,25 @@
     part,
     slice_at,
 ):
-    feats, near = got_ref.shape[0], sent_ref.shape[0]
+    cores, near = got_ref.shape[0], sent_ref.shape[0]
     hidden = self_ref.shape[0]
-    pre = got_ref[0, :hidden, :].astype(f32)
-    for f in range(1, feats):
-        pre += got_ref[f, :hidden, :].astype(f32)
+    pre = got_ref[0, :hidden, :].astype(f32) + got_ref[0, hidden : 2 * hidden, :].astype(f32)
+    for c in range(1, cores):
+        pre += got_ref[c, :hidden, :].astype(f32)
+        pre += got_ref[c, hidden : 2 * hidden, :].astype(f32)
     sigma = 1.0 / (1.0 + jnp.exp(-pre))
     slope = sigma * (1.0 + pre * (1.0 - sigma))
     scratch[...] = pre * sigma
     hidden_ref[...] = scratch[...].astype(bf16)
     mine = scratch[pl.ds(pl.multiple_of(slice_at() * part, part), part), :].astype(bf16)
     mine_ref[...] = mine
-    back_high = [got_ref[f, hidden : hidden + part, :] for f in range(feats)]
+    back_high, back_low = [], []
+    for y in range(hidden // part // cores):
+        at = 2 * (hidden + y * part)
+        for c in range(cores):
+            back_high.append(got_ref[c, at : at + part, :])
+            back_low.append(got_ref[c, at + part : at + 2 * part, :])
     back_high = jnp.concatenate(back_high, axis=0)
-    back_low = [got_ref[f, hidden + part :, :] for f in range(feats)]
     back_low = jnp.concatenate(back_low, axis=0)
     grad = dot(self_ref[...], grad_ref[...], ((1,), (1,)))
     grad += dot(other_ref[...], back_high, ((1,), (0,)))
@@ -383,6 +398,9 @@
     near_ids = [(x * na + a) * nb + b for a in range(na) for x in range(nx) for b in range(nb)]
     near_groups = [near_ids[a * near : (a + 1) * near] for a in range(na)]
     far_groups = [list(group) for group in zip(*near_groups)]
+    cores = 2
+    core_groups = [[y * cores + c for c in range(cores)] for y in range(feats // cores)]
+    y_groups = [list(group) for group in zip(*core_groups)]
     capacity = sample_ids.shape[2]
     targets = self_ids.shape[1]
     width = features.shape[1]
@@ -423,7 +441,7 @@
     sent, mean_high = in_vmem(
         functools.partial(first_kernel, part=part),
         [
-            jax.ShapeDtypeStruct((hidden + 2 * part, targets), bf16),
+            jax.ShapeDtypeStruct((feats // cores, hidden + 2 * part, targets), bf16),
             jax.ShapeDtypeStruct((targets, width), bf16),
         ],
         came,
@@ -431,7 +449,13 @@
         self_one,
         neighbour_one,
     )
-    got = lax.all_gather(sent, "feat")
+    got = exchange(sent, "feat", y_groups)
+    sent = in_vmem(
+        functools.partial(pair_kernel, hidden=hidden),
+        jax.ShapeDtypeStruct((2 * hidden + 2 * part * feats // cores, targets), bf16),
+        got,
+    )
+    got = lax.all_gather(sent, "feat", axis_index_groups=core_groups)
 
     half = hidden // 2
     rows_each, share = 4 * width // near, 4 * part // near

time: 132 us -> 131 us (level)
  blocking collectives: 110 us -> 108 us
    all_gather x1, blocking collectives: 18.5 us -> 8.03 us  [shards(): got = lax.all_gather(sent, 'feat', axis_index_groups=core_groups)]
    all_to_all x5 -> x6, blocking collectives: 91.4 us -> 100 us  [exchange(): lax.all_to_all(values, axis, split_axis=0, concat_axis=0, tiled=True, axi...]
    pallas_call x7 -> x8, Pallas kernels: 2.99 us -> 3.05 us  [in_vmem(): pl.pallas_call(kernel, out_shape=out_shape, in_specs=[vmem] * len(args),...]
where the time goes in v13:
time: 131 us; the launch traced here: 130 us
  blocking collectives  108 us (82%)
  waiting for transfers between devices  8.35 us (6%)
  starting transfers between devices  6.35 us (5%)
  Pallas kernels  5.76 us (4%)
    all_to_all x6, blocking collectives, exchange(): lax.all_to_all(values, axis, split_axis=0, concat_axis=0, tiled=True, axi...  100 us
    all_to_all x1, waiting for transfers between devices, exchange(): lax.all_to_all(values, axis, split_axis=0, concat_axis=0, tiled=True, axi...  8.35 us
    all_gather x1, blocking collectives, shards(): got = lax.all_gather(sent, 'feat', axis_index_groups=core_groups)  8.03 us
    all_to_all x1, starting transfers between devices, exchange(): lax.all_to_all(values, axis, split_axis=0, concat_axis=0, tiled=True, axi...  6.35 us
    pallas_call x8, Pallas kernels, in_vmem(): pl.pallas_call(kernel, out_shape=out_shape, in_specs=[vmem] * len(args),...  3.05 us
    pallas_call x1, Pallas kernels, pack(): pl.pallas_call(kernel, out_shape=jax.ShapeDtypeStruct((nx * nb, total, fe...  2.71 us
  transfers between devices with their start and end apart: 1, of which 1 were waited for; matrix products, arithmetic and copies ran while one was open for 0% of the time, Pallas kernels for 0%

profile of v13, /device:TPU:1, one launch (start us, length us, event | category | flops | bytes accessed | tf_op | source)
XLA Modules:
  0.0 130.3 jit_solution(4809654956096010562)
XLA Ops:
  0.6 2.7 %shard_map.155 = bf16[8,400,128]{2,1,0:T(8,128)(2,1)} custom-call(s32[32,64]{1,0:T(8,128)} %bitcast.13, s32[32,64]{1,0:T(8,128)} %bitcast.14, s32[64,64]{1,0:T(8,128)} %counts_hbm.1, s32[1,4]{1,0:T(1,128)} %blocks_hbm.1, bf16[512,128]{1,0:T(8,128)(2,1)} %features_hbm.1, bf16[4,128,128]{2,1,0:T(8,128)(2,1)} %bitcast.11, bf16[128,256]{1,0:T(8,128)(2,1)} %grad_ref.1), custom_call_target="tpu_custom_call" | custom-call | tf_op jit(solution)/shard_map/pallas_call | solution.py:152
  3.4 0.0 copy-start.6
  3.4 6.3 %all-to-all-start = ((bf16[8,400,128]{2,1,0:T(8,128)(2,1)}), bf16[8,400,128]{2,1,0:T(8,128)(2,1)S(1)}, u32[]{:S(2)}, u32[]{:S(2)}) async-start(bf16[8,400,128]{2,1,0:T(8,128)(2,1)} %shard_map.155), calls=%async_computation | async-start | bytes 1638400 | tf_op jit(solution)/shard_map/all_to_all | solution.py:21
  9.7 0.0 copy-start.7
  9.7 0.0 copy-done.6
  9.7 0.6 copy-done.7
  10.4 0.2 convolution_convert_fusion.rows_ref
  10.6 8.3 %all-to-all-done.got_ref = bf16[8,400,128]{2,1,0:T(8,128)(2,1)S(1)} async-done(((bf16[8,400,128]{2,1,0:T(8,128)(2,1)}), bf16[8,400,128]{2,1,0:T(8,128)(2,1)S(1)}, u32[]{:S(2)}, u32[]{:S(2)}) %all-to-all-start) | async-done | bytes 819232 | tf_op jit(solution)/shard_map/all_to_all | solution.py:21
  19.0 0.7 shard_map.156
  19.7 0.0 copy-start.4
  19.7 0.0 copy-start.5
  19.7 37.8 %all_to_all.35.came_ref = bf16[8,168,128]{2,1,0:T(8,128)(2,1)S(1)} all-to-all(bf16[8,168,128]{2,1,0:T(8,128)(2,1)S(1)} %get-tuple-element.13), channel_id=1, replica_groups={{0,2,4,6,8,10,12,14},{1,3,5,7,9,11,13,15},{16,18,20,22,24,26,28,30},{17..., dimensions={0} | all-to-all | bytes 688128 | tf_op jit(solution)/shard_map/all_to_all | solution.py:21
  57.4 0.0 copy-done.4
  57.4 0.0 copy-done.5
  57.4 0.3 shard_map.157
  57.8 9.9 %all_to_all.36.got_ref = bf16[4,320,128]{2,1,0:T(8,128)(2,1)S(1)} all-to-all(bf16[4,320,128]{2,1,0:T(8,128)(2,1)S(1)} %get-tuple-element.14), channel_id=1, replica_groups={{0,128,256,384},{64,192,320,448},{1,129,257,385},{65,193,321,449},{2,13..., dimensions={0} | all-to-all | bytes 655360 | tf_op jit(solution)/shard_map/all_to_all | solution.py:21
  67.7 0.0 copy-start.1
  67.7 0.0 copy-start.2
  67.7 0.0 copy-start.3
  67.7 8.0 %all-gather = bf16[1536,128]{1,0:T(8,128)(2,1)S(1)} all-gather(bf16[768,128]{1,0:T(8,128)(2,1)S(1)} %shard_map.158), channel_id=2, replica_groups={{0,64},{128,192},{256,320},{384,448},{1,65},{129,193},{257,321},{385,44..., dimensions={0}, use_global_device_ids=true | all-gather | bytes 589824 | tf_op jit(solution)/shard_map/all_gather | solution.py:458
  75.8 0.0 copy-done.1
  75.8 0.0 copy-done.2
  75.8 0.0 copy-done.3
  75.8 0.5 shard_map.159
  76.3 8.5 %all_to_all.37.got_ref = bf16[8,80,128]{2,1,0:T(8,128)(2,1)S(1)} all-to-all(bf16[8,80,128]{2,1,0:T(8,128)(2,1)S(1)} %get-tuple-element.17), channel_id=1, replica_groups={{0,1,16,17,32,33,48,49},{2,3,18,19,34,35,50,51},{4,5,20,21,36,37,52,53}..., dimensions={0} | all-to-all | bytes 327680 | tf_op jit(solution)/shard_map/all_to_all | solution.py:21
  84.8 19.9 %all_to_all.38.got_ref = bf16[8,112,128]{2,1,0:T(8,128)(2,1)S(1)} all-to-all(bf16[8,112,128]{2,1,0:T(8,128)(2,1)S(1)} %shard_map.160), channel_id=1, replica_groups={{0,2,4,6,8,10,12,14},{1,3,5,7,9,11,13,15},{16,18,20,22,24,26,28,30},{17..., dimensions={0} | all-to-all | bytes 458752 | tf_op jit(solution)/shard_map/all_to_all | solution.py:21
  104.7 0.2 shard_map.161
  104.9 0.0 copy-start
  104.9 9.6 %all_to_all.39.got_ref.lower_ref = bf16[8,208,128]{2,1,0:T(8,128)(2,1)S(1)} all-to-all(bf16[8,208,128]{2,1,0:T(8,128)(2,1)S(1)} %shard_map.161), channel_id=1, replica_groups={{0,1,16,17,32,33,48,49},{2,3,18,19,34,35,50,51},{4,5,20,21,36,37,52,53}..., dimensions={0} | all-to-all | bytes 851968 | tf_op jit(solution)/shard_map/all_to_all | solution.py:21
  114.5 0.0 copy-done
  114.5 0.2 shard_map.162
  114.7 14.6 %all_to_all.40.got_ref = bf16[8,160,128]{2,1,0:T(8,128)(2,1)S(1)} all-to-all(bf16[8,160,128]{2,1,0:T(8,128)(2,1)S(1)} %shard_map.162), channel_id=1, replica_groups=mesh['feat'=8,'node'=64] {'feat'}, dimensions={0} | all-to-all | bytes 655360 | tf_op jit(solution)/shard_map/all_to_all | solution.py:21
  129.3 1.0 shard_map.163
  (2 shorter events, 0.1 us)
Async XLA Ops:
  3.4 6.4 %copy-start.6 = (bf16[512,128]{1,0:T(8,128)(2,1)S(1)}, bf16[512,128]{1,0:T(8,128)(2,1)}, u32[]{:S(2)}) copy-start(bf16[512,128]{1,0:T(8,128)(2,1)} %features_hbm.1) | copy-start | bytes 393220
  3.4 15.6 %all-to-all-start = ((bf16[8,400,128]{2,1,0:T(8,128)(2,1)}), bf16[8,400,128]{2,1,0:T(8,128)(2,1)S(1)}, u32[]{:S(2)}, u32[]{:S(2)}) async-start(bf16[8,400,128]{2,1,0:T(8,128)(2,1)} %shard_map.155), calls=%async_computation | async-start | bytes 1638400 | tf_op jit(solution)/shard_map/all_to_all | solution.py:21
  9.7 0.7 copy-start.7
  19.7 37.8 %copy-start.4 = (bf16[128,256]{1,0:T(8,128)(2,1)S(1)}, bf16[128,256]{1,0:T(8,128)(2,1)}, u32[]{:S(2)}) copy-start(bf16[128,256]{1,0:T(8,128)(2,1)} %self_ref.3) | copy-start | bytes 196612
  19.7 37.8 %copy-start.5 = (bf16[128,256]{1,0:T(8,128)(2,1)S(1)}, bf16[128,256]{1,0:T(8,128)(2,1)}, u32[]{:S(2)}) copy-start(bf16[128,256]{1,0:T(8,128)(2,1)} %other_ref.3) | copy-start | bytes 196612
  67.7 8.1 %copy-start.1 = (bf16[256,256]{1,0:T(8,128)(2,1)S(1)}, bf16[256,256]{1,0:T(8,128)(2,1)}, u32[]{:S(2)}) copy-start(bf16[256,256]{1,0:T(8,128)(2,1)} %self_ref.5) | copy-start | bytes 393220
  67.7 8.1 %copy-start.2 = (bf16[256,256]{1,0:T(8,128)(2,1)S(1)}, bf16[256,256]{1,0:T(8,128)(2,1)}, u32[]{:S(2)}) copy-start(bf16[256,256]{1,0:T(8,128)(2,1)} %other_ref.5) | copy-start | bytes 393220
  67.7 8.0 %copy-start.3 = (bf16[128,256]{1,0:T(8,128)(2,1)S(1)}, bf16[128,256]{1,0:T(8,128)(2,1)}, u32[]{:S(2)}) copy-start(bf16[128,256]{1,0:T(8,128)(2,1)} %grad_ref.1) | copy-start | bytes 196612
  104.9 9.6 %copy-start = (bf16[1,4,128,128]{3,2,1,0:T(8,128)(2,1)S(1)}, bf16[1,4,128,128]{3,2,1,0:T(8,128)(2,1)}, u32[]{:S(2)}) copy-start(bf16[1,4,128,128]{3,2,1,0:T(8,128)(2,1)} %param.20) | copy-start | bytes 393220

commit v14 on v13

--- a/solution.py
+++ b/solution.py
@@ -86,8 +86,6 @@
     ]
     for copy in copies:
         copy.start()
-    for copy in copies:
-        copy.wait()
     device, feat = place()
     near = nx * nb
     capacity, nodes = ids_ref.shape
@@ -98,6 +96,33 @@
     lanes = targets // capacity
     near_at = near_index(device, na, nb)
 
+    near_owners = [
+        [(x * na + a) * nb + b for a in range(na)] for x in range(nx) for b in range(nb)
+    ]
+    cut = na * capacity
+    outs = []
+
+    def copy_out(to, start, stop):
+        rows = pl.ds(start, stop - start)
+        out = pltpu.make_async_copy(
+            sent_ref.at[to, rows], sent_hbm.at[to, rows], out_sems.at[len(outs)]
+        )
+        out.start()
+        outs.append(out)
+
+    local_ids = lax.broadcasted_iota(jnp.int32, (capacity, locals_), 1)
+    copies[0].wait()
+    copies[4].wait()
+    for to, owners in enumerate(near_owners):
+        chosen = jnp.concatenate(
+            [jnp.where(ids_ref[:, o : o + 1] == local_ids, 1.0, 0.0).astype(bf16) for o in owners],
+            axis=0,
+        )
+        sent_ref[to, :cut, :] = dot(chosen, features_ref[...], ((1,), (0,))).astype(bf16)
+        copy_out(to, 0, cut)
+
+    for n in (1, 2, 3, 5, 6):
+        copies[n].wait()
     used = lax.broadcasted_iota(jnp.int32, (capacity, nodes), 0) < counts_ref[pl.ds(device, 1), :]
     slots = jnp.where(used, slots_ref[...], targets).astype(f32)
     slots = jnp.concatenate([slots] * lanes, axis=0)
@@ -109,34 +134,20 @@
     terms = [dot(grad_t, tiles_ref[k], ((1,), (0,))) for k in range(count)]
     blocks = [blocks_ref[0, k] for k in range(count)]
     row = lax.broadcasted_iota(jnp.int32, (8, targets), 0)
-    far_rows = jnp.zeros((8, targets), jnp.int32)
+    marks = jnp.zeros((8, targets), jnp.int32)
     for k in range(count):
-        far_rows = jnp.where(row == k, blocks[k] % (na * nb) // nb, far_rows)
-        far_rows = jnp.where(row == count + k, blocks[k] // (na * nb) * nb + blocks[k] % nb, far_rows)
-    far_rows = far_rows.astype(f32)
-    local_ids = lax.broadcasted_iota(jnp.int32, (capacity, locals_), 1)
-    outs = []
-    for x in range(nx):
-        for b in range(nb):
-            to = x * nb + b
-            owners = [(x * na + a) * nb + b for a in range(na)]
-            chosen = jnp.concatenate(
-                [jnp.where(ids_ref[:, o : o + 1] == local_ids, 1.0, 0.0).astype(bf16) for o in owners],
-                axis=0,
-            )
-            rows = dot(chosen, features_ref[...], ((1,), (0,)))
-            sent_ref[to, : na * capacity, :] = rows.astype(bf16)
-            at = na * capacity
-            for k in range(count):
-                there = blocks[k] // (na * nb) * nb + blocks[k] % nb == to
-                term = jnp.where(there, terms[k], 0.0)
-                sent_ref[to, at : at + part, :] = term.astype(bf16)
-                at += part
-            slot_rows = slots_scratch[pl.ds(owners[0], na, stride=nb), :]
-            sent_ref[to, at : at + na + 8, :] = jnp.concatenate([slot_rows, far_rows], 0).astype(bf16)
-            out = pltpu.make_async_copy(sent_ref.at[to], sent_hbm.at[to], out_sems.at[to])
-            out.start()
-            outs.append(out)
+        marks = jnp.where(row == k, blocks[k] % (na * nb) // nb, marks)
+        marks = jnp.where(row == count + k, near_index(blocks[k], na, nb), marks)
+    marks = marks.astype(f32)
+    for to, owners in enumerate(near_owners):
+        at = cut
+        for k in range(count):
+            term = jnp.where(near_index(blocks[k], na, nb) == to, terms[k], 0.0)
+            sent_ref[to, at : at + part, :] = term.astype(bf16)
+            at += part
+        slot_rows = slots_scratch[pl.ds(owners[0], na, stride=nb), :]
+        sent_ref[to, at : at + na + 8, :] = jnp.concatenate([slot_rows, marks], 0).astype(bf16)
+        copy_out(to, cut, at + na + 8)
     for out in outs:
         out.wait()
 
@@ -160,20 +171,21 @@
             pltpu.VMEM((targets, targets), f32),
             pltpu.VMEM((grad.shape[1], targets), f32),
             pltpu.SemaphoreType.DMA((len(args),)),
-            pltpu.SemaphoreType.DMA((nx * nb,)),
+            pltpu.SemaphoreType.DMA((2 * nx * nb,)),
         ],
         compiler_params=pltpu.CompilerParams(vmem_limit_bytes=PACK_LIMIT),
     )(*args)
 
 
-def in_vmem(kernel, out_shape, *args, scratch_shapes=()):
+def in_vmem(kernel, out_shape, *args, scratch_shapes=(), out_space=pltpu.VMEM):
     vmem = pl.BlockSpec(memory_space=pltpu.VMEM)
+    out = pl.BlockSpec(memory_space=out_space)
     many = isinstance(out_shape, (list, tuple))
     return pl.pallas_call(
         kernel,
         out_shape=out_shape,
         in_specs=[vmem] * len(args),
-        out_specs=[vmem] * len(out_shape) if many else vmem,
+        out_specs=[out] * len(out_shape) if many else out,
         scratch_shapes=scratch_shapes,
         compiler_params=pltpu.CompilerParams(vmem_limit_bytes=VMEM_LIMIT),
     )(*args)
@@ -342,38 +354,35 @@
 
 
 def last_kernel(
-    got_ref,
-    hidden_ref,
-    self_ref,
-    other_ref,
-    lower_ref,
-    out_ref,
-    low_first_ref,
-    low_second_ref,
-    first_ref,
-    second_ref,
-    *,
-    part,
-    rows_each,
+    got_ref, hidden_ref, self_ref, other_ref, lower_ref, *refs, part, rows_each
 ):
+    outs, held, sems = refs[:5], refs[5:10], refs[10]
+    out_ref, low_first_ref, low_second_ref, first_ref, second_ref = held
     feats = got_ref.shape[0]
     half = first_ref.shape[1] // 2
-    agg = jnp.concatenate([got_ref[f, :part, :] for f in range(feats)], axis=0)
-    out = dot(hidden_ref[...], self_ref[...], ((0,), (0,))) + dot(agg, other_ref[...], ((0,), (0,)))
-    out_ref[...] = out.astype(bf16)
-    for f in range(feats):
-        at = f * part
-        for n, ref in enumerate([first_ref, second_ref]):
-            start = part * (1 + 2 * n)
-            ref[at : at + part, :half] = got_ref[f, start : start + part, :].astype(f32)
-            ref[at : at + part, half:] = got_ref[f, start + part : start + 2 * part, :].astype(f32)
     width = low_first_ref.shape[0]
+    copies = [pltpu.make_async_copy(held[n], outs[n], sems.at[n]) for n in range(5)]
     for n in range(lower_ref.shape[0]):
         quarter, at = divmod(n * rows_each, width)
         ref = (low_first_ref, low_second_ref)[quarter // 2]
         left = quarter % 2 * half
         rows = lower_ref[n, :rows_each, :].astype(f32)
         ref[at : at + rows_each, left : left + half] = rows
+    copies[1].start()
+    copies[2].start()
+    for n, ref in enumerate([first_ref, second_ref]):
+        start = part * (1 + 2 * n)
+        for f in range(feats):
+            at = f * part
+            ref[at : at + part, :half] = got_ref[f, start : start + part, :].astype(f32)
+            ref[at : at + part, half:] = got_ref[f, start + part : start + 2 * part, :].astype(f32)
+        copies[3 + n].start()
+    agg = jnp.concatenate([got_ref[f, :part, :] for f in range(feats)], axis=0)
+    out = dot(hidden_ref[...], self_ref[...], ((0,), (0,))) + dot(agg, other_ref[...], ((0,), (0,)))
+    out_ref[...] = out.astype(bf16)
+    copies[0].start()
+    for copy in copies:
+        copy.wait()
 
 
 def shards(
@@ -505,20 +514,24 @@
         tiles,
     )
     got = exchange(sent, "feat")
+    shapes = [
+        jax.ShapeDtypeStruct((targets, hidden), bf16),
+        jax.ShapeDtypeStruct((width, hidden), f32),
+        jax.ShapeDtypeStruct((width, hidden), f32),
+        jax.ShapeDtypeStruct((hidden, hidden), f32),
+        jax.ShapeDtypeStruct((hidden, hidden), f32),
+    ]
     return in_vmem(
         functools.partial(last_kernel, part=part, rows_each=rows_each),
-        [
-            jax.ShapeDtypeStruct((targets, hidden), bf16),
-            jax.ShapeDtypeStruct((width, hidden), f32),
-            jax.ShapeDtypeStruct((width, hidden), f32),
-            jax.ShapeDtypeStruct((hidden, hidden), f32),
-            jax.ShapeDtypeStruct((hidden, hidden), f32),
-        ],
+        shapes,
         got,
         hidden_t,
         self_two,
         neighbour_two,
         lower,
+        out_space=pltpu.HBM,
+        scratch_shapes=[pltpu.VMEM(shape.shape, shape.dtype) for shape in shapes]
+        + [pltpu.SemaphoreType.DMA((len(shapes),))],
     )
 
 

time: 131 us -> 131 us (level)
  no operation moved by 1% of the time
where the time goes in v14:
time: 131 us
  blocking collectives  108 us (82%)
  waiting for transfers between devices  8.35 us (6%)
  starting transfers between devices  6.35 us (5%)
  Pallas kernels  6 us (5%)
    all_to_all x6, blocking collectives, exchange(): lax.all_to_all(values, axis, split_axis=0, concat_axis=0, tiled=True, axi...  100 us
    all_to_all x1, waiting for transfers between devices, exchange(): lax.all_to_all(values, axis, split_axis=0, concat_axis=0, tiled=True, axi...  8.35 us
    all_gather x1, blocking collectives, shards(): got = lax.all_gather(sent, 'feat', axis_index_groups=core_groups)  8.02 us
    all_to_all x1, starting transfers between devices, exchange(): lax.all_to_all(values, axis, split_axis=0, concat_axis=0, tiled=True, axi...  6.35 us
    pallas_call x8, Pallas kernels, in_vmem(): pl.pallas_call(kernel, out_shape=out_shape, in_specs=[vmem] * len(args),...  3.09 us
    pallas_call x1, Pallas kernels, pack(): pl.pallas_call(kernel, out_shape=jax.ShapeDtypeStruct((nx * nb, total, fe...  2.9 us
  transfers between devices with their start and end apart: 1, of which 1 were waited for; matrix products, arithmetic and copies ran while one was open for 0% of the time, Pallas kernels for 0%

profile of v14, /device:TPU:1, one launch (start us, length us, event | category | flops | bytes accessed | tf_op | source)
XLA Modules:
  0.0 130.5 jit_solution(11826227909021241146)
XLA Ops:
  0.6 2.9 %shard_map.155 = bf16[8,400,128]{2,1,0:T(8,128)(2,1)} custom-call(s32[32,64]{1,0:T(8,128)} %bitcast.13, s32[32,64]{1,0:T(8,128)} %bitcast.14, s32[64,64]{1,0:T(8,128)} %counts_hbm.1, s32[1,4]{1,0:T(1,128)} %blocks_hbm.1, bf16[512,128]{1,0:T(8,128)(2,1)} %features_hbm.1, bf16[4,128,128]{2,1,0:T(8,128)(2,1)} %bitcast.11, bf16[128,256]{1,0:T(8,128)(2,1)} %grad_ref.1), custom_call_target="tpu_custom_call" | custom-call | tf_op jit(solution)/shard_map/pallas_call | solution.py:163
  3.5 0.0 copy-start.6
  3.6 6.3 %all-to-all-start = ((bf16[8,400,128]{2,1,0:T(8,128)(2,1)}), bf16[8,400,128]{2,1,0:T(8,128)(2,1)S(1)}, u32[]{:S(2)}, u32[]{:S(2)}) async-start(bf16[8,400,128]{2,1,0:T(8,128)(2,1)} %shard_map.155), calls=%async_computation | async-start | bytes 1638400 | tf_op jit(solution)/shard_map/all_to_all | solution.py:21
  9.9 0.0 copy-start.7
  9.9 0.0 copy-done.6
  9.9 0.6 copy-done.7
  10.6 0.2 convolution_convert_fusion.rows_ref
  10.8 8.3 %all-to-all-done.got_ref = bf16[8,400,128]{2,1,0:T(8,128)(2,1)S(1)} async-done(((bf16[8,400,128]{2,1,0:T(8,128)(2,1)}), bf16[8,400,128]{2,1,0:T(8,128)(2,1)S(1)}, u32[]{:S(2)}, u32[]{:S(2)}) %all-to-all-start) | async-done | bytes 819232 | tf_op jit(solution)/shard_map/all_to_all | solution.py:21
  19.1 0.7 shard_map.156
  19.9 0.0 copy-start.4
  19.9 0.0 copy-start.5
  19.9 37.8 %all_to_all.35.came_ref = bf16[8,168,128]{2,1,0:T(8,128)(2,1)S(1)} all-to-all(bf16[8,168,128]{2,1,0:T(8,128)(2,1)S(1)} %get-tuple-element.13), channel_id=1, replica_groups={{0,2,4,6,8,10,12,14},{1,3,5,7,9,11,13,15},{16,18,20,22,24,26,28,30},{17..., dimensions={0} | all-to-all | bytes 688128 | tf_op jit(solution)/shard_map/all_to_all | solution.py:21
  57.6 0.0 copy-done.4
  57.6 0.0 copy-done.5
  57.6 0.3 shard_map.157
  58.0 9.9 %all_to_all.36.got_ref = bf16[4,320,128]{2,1,0:T(8,128)(2,1)S(1)} all-to-all(bf16[4,320,128]{2,1,0:T(8,128)(2,1)S(1)} %get-tuple-element.14), channel_id=1, replica_groups={{0,128,256,384},{64,192,320,448},{1,129,257,385},{65,193,321,449},{2,13..., dimensions={0} | all-to-all | bytes 655360 | tf_op jit(solution)/shard_map/all_to_all | solution.py:21
  67.9 0.0 copy-start.1
  67.9 0.0 copy-start.2
  67.9 0.0 copy-start.3
  67.9 8.0 %all-gather = bf16[1536,128]{1,0:T(8,128)(2,1)S(1)} all-gather(bf16[768,128]{1,0:T(8,128)(2,1)S(1)} %shard_map.158), channel_id=2, replica_groups={{0,64},{128,192},{256,320},{384,448},{1,65},{129,193},{257,321},{385,44..., dimensions={0}, use_global_device_ids=true | all-gather | bytes 589824 | tf_op jit(solution)/shard_map/all_gather | solution.py:467
  76.0 0.0 copy-done.1
  76.0 0.0 copy-done.2
  76.0 0.0 copy-done.3
  76.0 0.5 shard_map.159
  76.5 8.5 %all_to_all.37.got_ref = bf16[8,80,128]{2,1,0:T(8,128)(2,1)S(1)} all-to-all(bf16[8,80,128]{2,1,0:T(8,128)(2,1)S(1)} %get-tuple-element.17), channel_id=1, replica_groups={{0,1,16,17,32,33,48,49},{2,3,18,19,34,35,50,51},{4,5,20,21,36,37,52,53}..., dimensions={0} | all-to-all | bytes 327680 | tf_op jit(solution)/shard_map/all_to_all | solution.py:21
  85.0 19.9 %all_to_all.38.got_ref = bf16[8,112,128]{2,1,0:T(8,128)(2,1)S(1)} all-to-all(bf16[8,112,128]{2,1,0:T(8,128)(2,1)S(1)} %shard_map.160), channel_id=1, replica_groups={{0,2,4,6,8,10,12,14},{1,3,5,7,9,11,13,15},{16,18,20,22,24,26,28,30},{17..., dimensions={0} | all-to-all | bytes 458752 | tf_op jit(solution)/shard_map/all_to_all | solution.py:21
  104.9 0.2 shard_map.161
  105.1 0.0 copy-start
  105.1 9.6 %all_to_all.39.got_ref.lower_ref = bf16[8,208,128]{2,1,0:T(8,128)(2,1)S(1)} all-to-all(bf16[8,208,128]{2,1,0:T(8,128)(2,1)S(1)} %shard_map.161), channel_id=1, replica_groups={{0,1,16,17,32,33,48,49},{2,3,18,19,34,35,50,51},{4,5,20,21,36,37,52,53}..., dimensions={0} | all-to-all | bytes 851968 | tf_op jit(solution)/shard_map/all_to_all | solution.py:21
  114.7 0.0 copy-done
  114.7 0.2 shard_map.162
  114.9 14.6 %all_to_all.40.got_ref = bf16[8,160,128]{2,1,0:T(8,128)(2,1)S(1)} all-to-all(bf16[8,160,128]{2,1,0:T(8,128)(2,1)S(1)} %shard_map.162), channel_id=1, replica_groups=mesh['feat'=8,'node'=64] {'feat'}, dimensions={0} | all-to-all | bytes 655360 | tf_op jit(solution)/shard_map/all_to_all | solution.py:21
  129.5 1.0 shard_map.163
  (2 shorter events, 0.1 us)
Async XLA Ops:
  3.5 6.4 %copy-start.6 = (bf16[512,128]{1,0:T(8,128)(2,1)S(1)}, bf16[512,128]{1,0:T(8,128)(2,1)}, u32[]{:S(2)}) copy-start(bf16[512,128]{1,0:T(8,128)(2,1)} %features_hbm.1) | copy-start | bytes 393220
  3.6 15.6 %all-to-all-start = ((bf16[8,400,128]{2,1,0:T(8,128)(2,1)}), bf16[8,400,128]{2,1,0:T(8,128)(2,1)S(1)}, u32[]{:S(2)}, u32[]{:S(2)}) async-start(bf16[8,400,128]{2,1,0:T(8,128)(2,1)} %shard_map.155), calls=%async_computation | async-start | bytes 1638400 | tf_op jit(solution)/shard_map/all_to_all | solution.py:21
  9.9 0.7 copy-start.7
  19.9 37.8 %copy-start.4 = (bf16[128,256]{1,0:T(8,128)(2,1)S(1)}, bf16[128,256]{1,0:T(8,128)(2,1)}, u32[]{:S(2)}) copy-start(bf16[128,256]{1,0:T(8,128)(2,1)} %self_ref.3) | copy-start | bytes 196612
  19.9 37.8 %copy-start.5 = (bf16[128,256]{1,0:T(8,128)(2,1)S(1)}, bf16[128,256]{1,0:T(8,128)(2,1)}, u32[]{:S(2)}) copy-start(bf16[128,256]{1,0:T(8,128)(2,1)} %other_ref.3) | copy-start | bytes 196612
  67.9 8.1 %copy-start.1 = (bf16[256,256]{1,0:T(8,128)(2,1)S(1)}, bf16[256,256]{1,0:T(8,128)(2,1)}, u32[]{:S(2)}) copy-start(bf16[256,256]{1,0:T(8,128)(2,1)} %self_ref.5) | copy-start | bytes 393220
  67.9 8.1 %copy-start.2 = (bf16[256,256]{1,0:T(8,128)(2,1)S(1)}, bf16[256,256]{1,0:T(8,128)(2,1)}, u32[]{:S(2)}) copy-start(bf16[256,256]{1,0:T(8,128)(2,1)} %other_ref.5) | copy-start | bytes 393220
  67.9 8.0 %copy-start.3 = (bf16[128,256]{1,0:T(8,128)(2,1)S(1)}, bf16[128,256]{1,0:T(8,128)(2,1)}, u32[]{:S(2)}) copy-start(bf16[128,256]{1,0:T(8,128)(2,1)} %grad_ref.1) | copy-start | bytes 196612
  105.1 9.6 %copy-start = (bf16[1,4,128,128]{3,2,1,0:T(8,128)(2,1)S(1)}, bf16[1,4,128,128]{3,2,1,0:T(8,128)(2,1)}, u32[]{:S(2)}) copy-start(bf16[1,4,128,128]{3,2,1,0:T(8,128)(2,1)} %param.20) | copy-start | bytes 393220

commit v15 on v13

--- a/solution.py
+++ b/solution.py
@@ -356,24 +356,31 @@
     part,
     rows_each,
 ):
-    feats = got_ref.shape[0]
+    cores = got_ref.shape[0]
+    feats = first_ref.shape[0] // part
+    rows = got_ref.shape[1] // (feats // cores)
+
+    def slice_rows(f, start):
+        at = f // cores * rows + start
+        return got_ref[f % cores, at : at + part, :]
+
     half = first_ref.shape[1] // 2
-    agg = jnp.concatenate([got_ref[f, :part, :] for f in range(feats)], axis=0)
+    agg = jnp.concatenate([slice_rows(f, 0) for f in range(feats)], axis=0)
     out = dot(hidden_ref[...], self_ref[...], ((0,), (0,))) + dot(agg, other_ref[...], ((0,), (0,)))
     out_ref[...] = out.astype(bf16)
     for f in range(feats):
         at = f * part
         for n, ref in enumerate([first_ref, second_ref]):
             start = part * (1 + 2 * n)
-            ref[at : at + part, :half] = got_ref[f, start : start + part, :].astype(f32)
-            ref[at : at + part, half:] = got_ref[f, start + part : start + 2 * part, :].astype(f32)
+            ref[at : at + part, :half] = slice_rows(f, start).astype(f32)
+            ref[at : at + part, half:] = slice_rows(f, start + part).astype(f32)
     width = low_first_ref.shape[0]
     for n in range(lower_ref.shape[0]):
         quarter, at = divmod(n * rows_each, width)
         ref = (low_first_ref, low_second_ref)[quarter // 2]
         left = quarter % 2 * half
-        rows = lower_ref[n, :rows_each, :].astype(f32)
-        ref[at : at + rows_each, left : left + half] = rows
+        part_rows = lower_ref[n, :rows_each, :].astype(f32)
+        ref[at : at + rows_each, left : left + half] = part_rows
 
 
 def shards(
@@ -500,11 +507,12 @@
 
     sent = in_vmem(
         functools.partial(second_kernel, rows_each=rows_each, share=share, part=part),
-        jax.ShapeDtypeStruct((feats, part + near * share, targets), bf16),
+        jax.ShapeDtypeStruct((feats // cores, part + near * share, targets), bf16),
         got,
         tiles,
     )
-    got = exchange(sent, "feat")
+    got = exchange(sent, "feat", y_groups).reshape(-1, targets)
+    got = lax.all_gather(got, "feat", axis_index_groups=core_groups)
     return in_vmem(
         functools.partial(last_kernel, part=part, rows_each=rows_each),
         [

time: 131 us -> 131 us (level)
    all_gather x0 -> x1, blocking collectives: none -> 7.53 us  [shards(): got = lax.all_gather(got, 'feat', axis_index_groups=core_groups)]
    all_to_all x6, blocking collectives: 100 us -> 92.9 us  [exchange(): lax.all_to_all(values, axis, split_axis=0, concat_axis=0, tiled=True, axi...]
where the time goes in v15:
time: 131 us
  blocking collectives  108 us (82%)
  waiting for transfers between devices  8.35 us (6%)
  starting transfers between devices  6.35 us (5%)
  Pallas kernels  5.75 us (4%)
    all_to_all x6, blocking collectives, exchange(): lax.all_to_all(values, axis, split_axis=0, concat_axis=0, tiled=True, axi...  92.9 us
    all_to_all x1, waiting for transfers between devices, exchange(): lax.all_to_all(values, axis, split_axis=0, concat_axis=0, tiled=True, axi...  8.35 us
    all_gather x1, blocking collectives, shards(): got = lax.all_gather(sent, 'feat', axis_index_groups=core_groups)  8.03 us
    all_gather x1, blocking collectives, shards(): got = lax.all_gather(got, 'feat', axis_index_groups=core_groups)  7.53 us
    all_to_all x1, starting transfers between devices, exchange(): lax.all_to_all(values, axis, split_axis=0, concat_axis=0, tiled=True, axi...  6.35 us
    pallas_call x8, Pallas kernels, in_vmem(): pl.pallas_call(kernel, out_shape=out_shape, in_specs=[vmem] * len(args),...  3.04 us
    pallas_call x1, Pallas kernels, pack(): pl.pallas_call(kernel, out_shape=jax.ShapeDtypeStruct((nx * nb, total, fe...  2.71 us
  transfers between devices with their start and end apart: 1, of which 1 were waited for; matrix products, arithmetic and copies ran while one was open for 0% of the time, Pallas kernels for 0%

profile of v15, /device:TPU:1, one launch (start us, length us, event | category | flops | bytes accessed | tf_op | source)
XLA Modules:
  0.0 130.6 jit_solution(9631598313405697915)
XLA Ops:
  0.6 2.7 %shard_map.155 = bf16[8,400,128]{2,1,0:T(8,128)(2,1)} custom-call(s32[32,64]{1,0:T(8,128)} %bitcast.15, s32[32,64]{1,0:T(8,128)} %bitcast.16, s32[64,64]{1,0:T(8,128)} %counts_hbm.1, s32[1,4]{1,0:T(1,128)} %blocks_hbm.1, bf16[512,128]{1,0:T(8,128)(2,1)} %features_hbm.1, bf16[4,128,128]{2,1,0:T(8,128)(2,1)} %bitcast.12, bf16[128,256]{1,0:T(8,128)(2,1)} %grad_ref.1), custom_call_target="tpu_custom_call" | custom-call | tf_op jit(solution)/shard_map/pallas_call | solution.py:152
  3.4 0.0 copy-start.6
  3.4 6.3 %all-to-all-start = ((bf16[8,400,128]{2,1,0:T(8,128)(2,1)}), bf16[8,400,128]{2,1,0:T(8,128)(2,1)S(1)}, u32[]{:S(2)}, u32[]{:S(2)}) async-start(bf16[8,400,128]{2,1,0:T(8,128)(2,1)} %shard_map.155), calls=%async_computation | async-start | bytes 1638400 | tf_op jit(solution)/shard_map/all_to_all | solution.py:21
  9.7 0.0 copy-start.7
  9.7 0.0 copy-done.6
  9.7 0.6 copy-done.7
  10.4 0.2 convolution_convert_fusion.rows_ref
  10.6 8.3 %all-to-all-done.got_ref = bf16[8,400,128]{2,1,0:T(8,128)(2,1)S(1)} async-done(((bf16[8,400,128]{2,1,0:T(8,128)(2,1)}), bf16[8,400,128]{2,1,0:T(8,128)(2,1)S(1)}, u32[]{:S(2)}, u32[]{:S(2)}) %all-to-all-start) | async-done | bytes 819232 | tf_op jit(solution)/shard_map/all_to_all | solution.py:21
  19.0 0.7 shard_map.156
  19.7 0.0 copy-start.4
  19.7 0.0 copy-start.5
  19.7 37.8 %all_to_all.35.came_ref = bf16[8,168,128]{2,1,0:T(8,128)(2,1)S(1)} all-to-all(bf16[8,168,128]{2,1,0:T(8,128)(2,1)S(1)} %get-tuple-element.13), channel_id=1, replica_groups={{0,2,4,6,8,10,12,14},{1,3,5,7,9,11,13,15},{16,18,20,22,24,26,28,30},{17..., dimensions={0} | all-to-all | bytes 688128 | tf_op jit(solution)/shard_map/all_to_all | solution.py:21
  57.4 0.0 copy-done.4
  57.4 0.0 copy-done.5
  57.4 0.3 shard_map.157
  57.8 9.9 %all_to_all.36.got_ref = bf16[4,320,128]{2,1,0:T(8,128)(2,1)S(1)} all-to-all(bf16[4,320,128]{2,1,0:T(8,128)(2,1)S(1)} %get-tuple-element.14), channel_id=1, replica_groups={{0,128,256,384},{64,192,320,448},{1,129,257,385},{65,193,321,449},{2,13..., dimensions={0} | all-to-all | bytes 655360 | tf_op jit(solution)/shard_map/all_to_all | solution.py:21
  67.7 0.0 copy-start.1
  67.7 0.0 copy-start.2
  67.7 0.0 copy-start.3
  67.7 8.0 %all-gather = bf16[1536,128]{1,0:T(8,128)(2,1)S(1)} all-gather(bf16[768,128]{1,0:T(8,128)(2,1)S(1)} %shard_map.158), channel_id=2, replica_groups={{0,64},{128,192},{256,320},{384,448},{1,65},{129,193},{257,321},{385,44..., dimensions={0}, use_global_device_ids=true | all-gather | bytes 589824 | tf_op jit(solution)/shard_map/all_gather | solution.py:465
  75.8 0.0 copy-done.1
  75.8 0.0 copy-done.2
  75.8 0.0 copy-done.3
  75.8 0.5 shard_map.159
  76.3 8.5 %all_to_all.37.got_ref = bf16[8,80,128]{2,1,0:T(8,128)(2,1)S(1)} all-to-all(bf16[8,80,128]{2,1,0:T(8,128)(2,1)S(1)} %get-tuple-element.17), channel_id=1, replica_groups={{0,1,16,17,32,33,48,49},{2,3,18,19,34,35,50,51},{4,5,20,21,36,37,52,53}..., dimensions={0} | all-to-all | bytes 327680 | tf_op jit(solution)/shard_map/all_to_all | solution.py:21
  84.8 19.9 %all_to_all.38.got_ref = bf16[8,112,128]{2,1,0:T(8,128)(2,1)S(1)} all-to-all(bf16[8,112,128]{2,1,0:T(8,128)(2,1)S(1)} %shard_map.160), channel_id=1, replica_groups={{0,2,4,6,8,10,12,14},{1,3,5,7,9,11,13,15},{16,18,20,22,24,26,28,30},{17..., dimensions={0} | all-to-all | bytes 458752 | tf_op jit(solution)/shard_map/all_to_all | solution.py:21
  104.7 0.2 shard_map.161
  104.9 0.0 copy-start
  104.9 9.6 %all_to_all.39.got_ref.lower_ref = bf16[8,208,128]{2,1,0:T(8,128)(2,1)S(1)} all-to-all(bf16[8,208,128]{2,1,0:T(8,128)(2,1)S(1)} %shard_map.161), channel_id=1, replica_groups={{0,1,16,17,32,33,48,49},{2,3,18,19,34,35,50,51},{4,5,20,21,36,37,52,53}..., dimensions={0} | all-to-all | bytes 851968 | tf_op jit(solution)/shard_map/all_to_all | solution.py:21
  114.5 0.0 copy-done
  114.5 0.2 shard_map.162
  114.7 7.4 %all_to_all.40 = bf16[4,160,128]{2,1,0:T(8,128)(2,1)S(1)} all-to-all(bf16[4,160,128]{2,1,0:T(8,128)(2,1)S(1)} %shard_map.162), channel_id=1, replica_groups={{0,128,256,384},{64,192,320,448},{1,129,257,385},{65,193,321,449},{2,13..., dimensions={0} | all-to-all | bytes 327680 | tf_op jit(solution)/shard_map/all_to_all | solution.py:21
  122.0 7.5 %all_gather.11.got_ref = bf16[2,640,128]{2,1,0:T(8,128)(2,1)S(1)} all-gather(bf16[1,640,128]{2,1,0:T(8,128)(2,1)S(1)} %bitcast.14), channel_id=1, replica_groups={{0,64},{128,192},{256,320},{384,448},{1,65},{129,193},{257,321},{385,44..., dimensions={0}, use_global_device_ids=true | all-gather | bytes 491520 | tf_op jit(solution)/shard_map/all_gather | solution.py:515
  129.6 1.0 shard_map.163
  (2 shorter events, 0.1 us)
Async XLA Ops:
  3.4 6.4 %copy-start.6 = (bf16[512,128]{1,0:T(8,128)(2,1)S(1)}, bf16[512,128]{1,0:T(8,128)(2,1)}, u32[]{:S(2)}) copy-start(bf16[512,128]{1,0:T(8,128)(2,1)} %features_hbm.1) | copy-start | bytes 393220
  3.4 15.6 %all-to-all-start = ((bf16[8,400,128]{2,1,0:T(8,128)(2,1)}), bf16[8,400,128]{2,1,0:T(8,128)(2,1)S(1)}, u32[]{:S(2)}, u32[]{:S(2)}) async-start(bf16[8,400,128]{2,1,0:T(8,128)(2,1)} %shard_map.155), calls=%async_computation | async-start | bytes 1638400 | tf_op jit(solution)/shard_map/all_to_all | solution.py:21
  9.7 0.7 copy-start.7
  19.7 37.8 %copy-start.4 = (bf16[128,256]{1,0:T(8,128)(2,1)S(1)}, bf16[128,256]{1,0:T(8,128)(2,1)}, u32[]{:S(2)}) copy-start(bf16[128,256]{1,0:T(8,128)(2,1)} %self_ref.3) | copy-start | bytes 196612
  19.7 37.8 %copy-start.5 = (bf16[128,256]{1,0:T(8,128)(2,1)S(1)}, bf16[128,256]{1,0:T(8,128)(2,1)}, u32[]{:S(2)}) copy-start(bf16[128,256]{1,0:T(8,128)(2,1)} %other_ref.3) | copy-start | bytes 196612
  67.7 8.1 %copy-start.1 = (bf16[256,256]{1,0:T(8,128)(2,1)S(1)}, bf16[256,256]{1,0:T(8,128)(2,1)}, u32[]{:S(2)}) copy-start(bf16[256,256]{1,0:T(8,128)(2,1)} %self_ref.5) | copy-start | bytes 393220
  67.7 8.1 %copy-start.2 = (bf16[256,256]{1,0:T(8,128)(2,1)S(1)}, bf16[256,256]{1,0:T(8,128)(2,1)}, u32[]{:S(2)}) copy-start(bf16[256,256]{1,0:T(8,128)(2,1)} %other_ref.5) | copy-start | bytes 393220
  67.7 8.0 %copy-start.3 = (bf16[128,256]{1,0:T(8,128)(2,1)S(1)}, bf16[128,256]{1,0:T(8,128)(2,1)}, u32[]{:S(2)}) copy-start(bf16[128,256]{1,0:T(8,128)(2,1)} %grad_ref.1) | copy-start | bytes 196612
  104.9 9.6 %copy-start = (bf16[1,4,128,128]{3,2,1,0:T(8,128)(2,1)S(1)}, bf16[1,4,128,128]{3,2,1,0:T(8,128)(2,1)}, u32[]{:S(2)}) copy-start(bf16[1,4,128,128]{3,2,1,0:T(8,128)(2,1)} %param.20) | copy-start | bytes 393220

commit v16 on v15

--- a/solution.py
+++ b/solution.py
@@ -61,7 +61,6 @@
     grad_ref,
     sent_ref,
     slots_scratch,
-    grad_scratch,
     sems,
     out_sems,
     *,
@@ -84,8 +83,8 @@
             ]
         )
     ]
-    for copy in copies:
-        copy.start()
+    for n in (4, 5, 6, 0, 1, 2, 3):
+        copies[n].start()
     for copy in copies:
         copy.wait()
     device, feat = place()
@@ -104,8 +103,10 @@
     slots = jnp.concatenate([slots, jnp.zeros((targets, targets - nodes), f32)], axis=1).T
     group = lax.broadcasted_iota(jnp.int32, (targets, targets), 1) // capacity
     slots_scratch[...] = jnp.where(group == near_at % lanes, slots, 0.0)
-    grad_scratch[...] = grad_ref[...].astype(f32).T
-    grad_t = grad_scratch[pl.ds(pl.multiple_of(feat * part, part), part), :].astype(bf16)
+    shape = (part, grad_ref.shape[1])
+    column = lax.broadcasted_iota(jnp.int32, shape, 0) + feat * part
+    mine = jnp.where(column == lax.broadcasted_iota(jnp.int32, shape, 1), 1.0, 0.0).astype(bf16)
+    grad_t = dot(mine, grad_ref[...], ((1,), (1,))).astype(bf16)
     terms = [dot(grad_t, tiles_ref[k], ((1,), (0,))) for k in range(count)]
     blocks = [blocks_ref[0, k] for k in range(count)]
     row = lax.broadcasted_iota(jnp.int32, (8, targets), 0)
@@ -158,7 +159,6 @@
         + [
             pltpu.VMEM((nx * nb, total, features.shape[1]), bf16),
             pltpu.VMEM((targets, targets), f32),
-            pltpu.VMEM((grad.shape[1], targets), f32),
             pltpu.SemaphoreType.DMA((len(args),)),
             pltpu.SemaphoreType.DMA((nx * nb,)),
         ],

time: 131 us -> 131 us (level)
  no operation moved by 1% of the time
where the time goes in v16:
time: 131 us
  blocking collectives  108 us (82%)
  waiting for transfers between devices  8.35 us (6%)
  starting transfers between devices  6.35 us (5%)
  Pallas kernels  5.7 us (4%)
    all_to_all x6, blocking collectives, exchange(): lax.all_to_all(values, axis, split_axis=0, concat_axis=0, tiled=True, axi...  92.9 us
    all_to_all x1, waiting for transfers between devices, exchange(): lax.all_to_all(values, axis, split_axis=0, concat_axis=0, tiled=True, axi...  8.35 us
    all_gather x1, blocking collectives, shards(): got = lax.all_gather(sent, 'feat', axis_index_groups=core_groups)  8.03 us
    all_gather x1, blocking collectives, shards(): got = lax.all_gather(got, 'feat', axis_index_groups=core_groups)  7.52 us
    all_to_all x1, starting transfers between devices, exchange(): lax.all_to_all(values, axis, split_axis=0, concat_axis=0, tiled=True, axi...  6.35 us
    pallas_call x8, Pallas kernels, in_vmem(): pl.pallas_call(kernel, out_shape=out_shape, in_specs=[vmem] * len(args),...  3.04 us
    pallas_call x1, Pallas kernels, pack(): pl.pallas_call(kernel, out_shape=jax.ShapeDtypeStruct((nx * nb, total, fe...  2.66 us
  transfers between devices with their start and end apart: 1, of which 1 were waited for; matrix products, arithmetic and copies ran while one was open for 0% of the time, Pallas kernels for 0%

profile of v16, /device:TPU:1, one launch (start us, length us, event | category | flops | bytes accessed | tf_op | source)
XLA Modules:
  0.0 130.5 jit_solution(7293263509434468122)
XLA Ops:
  0.6 2.7 %shard_map.155 = bf16[8,400,128]{2,1,0:T(8,128)(2,1)} custom-call(s32[32,64]{1,0:T(8,128)} %bitcast.15, s32[32,64]{1,0:T(8,128)} %bitcast.16, s32[64,64]{1,0:T(8,128)} %counts_hbm.1, s32[1,4]{1,0:T(1,128)} %blocks_hbm.1, bf16[512,128]{1,0:T(8,128)(2,1)} %features_hbm.1, bf16[4,128,128]{2,1,0:T(8,128)(2,1)} %bitcast.12, bf16[128,256]{1,0:T(8,128)(2,1)} %grad_ref.1), custom_call_target="tpu_custom_call" | custom-call | tf_op jit(solution)/shard_map/pallas_call | solution.py:153
  3.3 0.0 copy-start.6
  3.3 6.3 %all-to-all-start = ((bf16[8,400,128]{2,1,0:T(8,128)(2,1)}), bf16[8,400,128]{2,1,0:T(8,128)(2,1)S(1)}, u32[]{:S(2)}, u32[]{:S(2)}) async-start(bf16[8,400,128]{2,1,0:T(8,128)(2,1)} %shard_map.155), calls=%async_computation | async-start | bytes 1638400 | tf_op jit(solution)/shard_map/all_to_all | solution.py:21
  9.7 0.0 copy-start.7
  9.7 0.0 copy-done.6
  9.7 0.6 copy-done.7
  10.3 0.2 convolution_convert_fusion.rows_ref
  10.6 8.3 %all-to-all-done.got_ref = bf16[8,400,128]{2,1,0:T(8,128)(2,1)S(1)} async-done(((bf16[8,400,128]{2,1,0:T(8,128)(2,1)}), bf16[8,400,128]{2,1,0:T(8,128)(2,1)S(1)}, u32[]{:S(2)}, u32[]{:S(2)}) %all-to-all-start) | async-done | bytes 819232 | tf_op jit(solution)/shard_map/all_to_all | solution.py:21
  18.9 0.7 shard_map.156
  19.6 0.0 copy-start.4
  19.6 0.0 copy-start.5
  19.6 37.8 %all_to_all.35.came_ref = bf16[8,168,128]{2,1,0:T(8,128)(2,1)S(1)} all-to-all(bf16[8,168,128]{2,1,0:T(8,128)(2,1)S(1)} %get-tuple-element.13), channel_id=1, replica_groups={{0,2,4,6,8,10,12,14},{1,3,5,7,9,11,13,15},{16,18,20,22,24,26,28,30},{17..., dimensions={0} | all-to-all | bytes 688128 | tf_op jit(solution)/shard_map/all_to_all | solution.py:21
  57.4 0.0 copy-done.4
  57.4 0.0 copy-done.5
  57.4 0.3 shard_map.157
  57.7 9.9 %all_to_all.36.got_ref = bf16[4,320,128]{2,1,0:T(8,128)(2,1)S(1)} all-to-all(bf16[4,320,128]{2,1,0:T(8,128)(2,1)S(1)} %get-tuple-element.14), channel_id=1, replica_groups={{0,128,256,384},{64,192,320,448},{1,129,257,385},{65,193,321,449},{2,13..., dimensions={0} | all-to-all | bytes 655360 | tf_op jit(solution)/shard_map/all_to_all | solution.py:21
  67.7 0.0 copy-start.1
  67.7 0.0 copy-start.2
  67.7 0.0 copy-start.3
  67.7 8.0 %all-gather = bf16[1536,128]{1,0:T(8,128)(2,1)S(1)} all-gather(bf16[768,128]{1,0:T(8,128)(2,1)S(1)} %shard_map.158), channel_id=2, replica_groups={{0,64},{128,192},{256,320},{384,448},{1,65},{129,193},{257,321},{385,44..., dimensions={0}, use_global_device_ids=true | all-gather | bytes 589824 | tf_op jit(solution)/shard_map/all_gather | solution.py:465
  75.7 0.0 copy-done.1
  75.7 0.0 copy-done.2
  75.7 0.0 copy-done.3
  75.7 0.5 shard_map.159
  76.3 8.4 %all_to_all.37.got_ref = bf16[8,80,128]{2,1,0:T(8,128)(2,1)S(1)} all-to-all(bf16[8,80,128]{2,1,0:T(8,128)(2,1)S(1)} %get-tuple-element.17), channel_id=1, replica_groups={{0,1,16,17,32,33,48,49},{2,3,18,19,34,35,50,51},{4,5,20,21,36,37,52,53}..., dimensions={0} | all-to-all | bytes 327680 | tf_op jit(solution)/shard_map/all_to_all | solution.py:21
  84.7 20.0 %all_to_all.38.got_ref = bf16[8,112,128]{2,1,0:T(8,128)(2,1)S(1)} all-to-all(bf16[8,112,128]{2,1,0:T(8,128)(2,1)S(1)} %shard_map.160), channel_id=1, replica_groups={{0,2,4,6,8,10,12,14},{1,3,5,7,9,11,13,15},{16,18,20,22,24,26,28,30},{17..., dimensions={0} | all-to-all | bytes 458752 | tf_op jit(solution)/shard_map/all_to_all | solution.py:21
  104.6 0.2 shard_map.161
  104.8 0.0 copy-start
  104.9 9.6 %all_to_all.39.got_ref.lower_ref = bf16[8,208,128]{2,1,0:T(8,128)(2,1)S(1)} all-to-all(bf16[8,208,128]{2,1,0:T(8,128)(2,1)S(1)} %shard_map.161), channel_id=1, replica_groups={{0,1,16,17,32,33,48,49},{2,3,18,19,34,35,50,51},{4,5,20,21,36,37,52,53}..., dimensions={0} | all-to-all | bytes 851968 | tf_op jit(solution)/shard_map/all_to_all | solution.py:21
  114.5 0.0 copy-done
  114.5 0.2 shard_map.162
  114.6 7.4 %all_to_all.40 = bf16[4,160,128]{2,1,0:T(8,128)(2,1)S(1)} all-to-all(bf16[4,160,128]{2,1,0:T(8,128)(2,1)S(1)} %shard_map.162), channel_id=1, replica_groups={{0,128,256,384},{64,192,320,448},{1,129,257,385},{65,193,321,449},{2,13..., dimensions={0} | all-to-all | bytes 327680 | tf_op jit(solution)/shard_map/all_to_all | solution.py:21
  122.0 7.5 %all_gather.11.got_ref = bf16[2,640,128]{2,1,0:T(8,128)(2,1)S(1)} all-gather(bf16[1,640,128]{2,1,0:T(8,128)(2,1)S(1)} %bitcast.14), channel_id=1, replica_groups={{0,64},{128,192},{256,320},{384,448},{1,65},{129,193},{257,321},{385,44..., dimensions={0}, use_global_device_ids=true | all-gather | bytes 491520 | tf_op jit(solution)/shard_map/all_gather | solution.py:515
  129.5 1.0 shard_map.163
  (2 shorter events, 0.1 us)
Async XLA Ops:
  3.3 6.4 %copy-start.6 = (bf16[512,128]{1,0:T(8,128)(2,1)S(1)}, bf16[512,128]{1,0:T(8,128)(2,1)}, u32[]{:S(2)}) copy-start(bf16[512,128]{1,0:T(8,128)(2,1)} %features_hbm.1) | copy-start | bytes 393220
  3.3 15.6 %all-to-all-start = ((bf16[8,400,128]{2,1,0:T(8,128)(2,1)}), bf16[8,400,128]{2,1,0:T(8,128)(2,1)S(1)}, u32[]{:S(2)}, u32[]{:S(2)}) async-start(bf16[8,400,128]{2,1,0:T(8,128)(2,1)} %shard_map.155), calls=%async_computation | async-start | bytes 1638400 | tf_op jit(solution)/shard_map/all_to_all | solution.py:21
  9.7 0.7 copy-start.7
  19.6 37.8 %copy-start.4 = (bf16[128,256]{1,0:T(8,128)(2,1)S(1)}, bf16[128,256]{1,0:T(8,128)(2,1)}, u32[]{:S(2)}) copy-start(bf16[128,256]{1,0:T(8,128)(2,1)} %self_ref.3) | copy-start | bytes 196612
  19.6 37.8 %copy-start.5 = (bf16[128,256]{1,0:T(8,128)(2,1)S(1)}, bf16[128,256]{1,0:T(8,128)(2,1)}, u32[]{:S(2)}) copy-start(bf16[128,256]{1,0:T(8,128)(2,1)} %other_ref.3) | copy-start | bytes 196612
  67.7 8.1 %copy-start.1 = (bf16[256,256]{1,0:T(8,128)(2,1)S(1)}, bf16[256,256]{1,0:T(8,128)(2,1)}, u32[]{:S(2)}) copy-start(bf16[256,256]{1,0:T(8,128)(2,1)} %self_ref.5) | copy-start | bytes 393220
  67.7 8.1 %copy-start.2 = (bf16[256,256]{1,0:T(8,128)(2,1)S(1)}, bf16[256,256]{1,0:T(8,128)(2,1)}, u32[]{:S(2)}) copy-start(bf16[256,256]{1,0:T(8,128)(2,1)} %other_ref.5) | copy-start | bytes 393220
  67.7 8.1 %copy-start.3 = (bf16[128,256]{1,0:T(8,128)(2,1)S(1)}, bf16[128,256]{1,0:T(8,128)(2,1)}, u32[]{:S(2)}) copy-start(bf16[128,256]{1,0:T(8,128)(2,1)} %grad_ref.1) | copy-start | bytes 196612
  104.8 9.6 %copy-start = (bf16[1,4,128,128]{3,2,1,0:T(8,128)(2,1)S(1)}, bf16[1,4,128,128]{3,2,1,0:T(8,128)(2,1)}, u32[]{:S(2)}) copy-start(bf16[1,4,128,128]{3,2,1,0:T(8,128)(2,1)} %param.20) | copy-start | bytes 393220

commit v17 on v15

--- a/solution.py
+++ b/solution.py
@@ -203,8 +203,10 @@
         for k in range(count):
             start = far * capacity + k * part
             term = got_ref[n, start : start + part, :].astype(f32)
-            mark = jnp.broadcast_to(marks[n][far + k : far + k + 1, :], (part, targets))
-            back = [back[a] + jnp.where(mark == float(a), term, 0.0) for a in range(far)]
+            mark = marks[n][far + k : far + k + 1, :]
+            back = [
+                back[a] + jnp.where(mark == float(a), 1.0, 0.0) * term for a in range(far)
+            ]
     for a in range(far):
         total = jnp.zeros((targets, targets), f32)
         degree = jnp.zeros((8, targets), f32)

time: 131 us -> 131 us (level)
  no operation moved by 1% of the time
where the time goes in v17:
time: 131 us
  blocking collectives  108 us (82%)
  waiting for transfers between devices  8.35 us (6%)
  starting transfers between devices  6.35 us (5%)
  Pallas kernels  5.74 us (4%)
    all_to_all x6, blocking collectives, exchange(): lax.all_to_all(values, axis, split_axis=0, concat_axis=0, tiled=True, axi...  92.9 us
    all_to_all x1, waiting for transfers between devices, exchange(): lax.all_to_all(values, axis, split_axis=0, concat_axis=0, tiled=True, axi...  8.35 us
    all_gather x1, blocking collectives, shards(): got = lax.all_gather(sent, 'feat', axis_index_groups=core_groups)  8.03 us
    all_gather x1, blocking collectives, shards(): got = lax.all_gather(got, 'feat', axis_index_groups=core_groups)  7.53 us
    all_to_all x1, starting transfers between devices, exchange(): lax.all_to_all(values, axis, split_axis=0, concat_axis=0, tiled=True, axi...  6.35 us
    pallas_call x8, Pallas kernels, in_vmem(): pl.pallas_call(kernel, out_shape=out_shape, in_specs=[vmem] * len(args),...  3.02 us
    pallas_call x1, Pallas kernels, pack(): pl.pallas_call(kernel, out_shape=jax.ShapeDtypeStruct((nx * nb, total, fe...  2.71 us
  transfers between devices with their start and end apart: 1, of which 1 were waited for; matrix products, arithmetic and copies ran while one was open for 0% of the time, Pallas kernels for 0%

profile of v17, /device:TPU:1, one launch (start us, length us, event | category | flops | bytes accessed | tf_op | source)
XLA Modules:
  0.0 130.6 jit_solution(6060196560101924206)
XLA Ops:
  0.6 2.7 %shard_map.155 = bf16[8,400,128]{2,1,0:T(8,128)(2,1)} custom-call(s32[32,64]{1,0:T(8,128)} %bitcast.15, s32[32,64]{1,0:T(8,128)} %bitcast.16, s32[64,64]{1,0:T(8,128)} %counts_hbm.1, s32[1,4]{1,0:T(1,128)} %blocks_hbm.1, bf16[512,128]{1,0:T(8,128)(2,1)} %features_hbm.1, bf16[4,128,128]{2,1,0:T(8,128)(2,1)} %bitcast.12, bf16[128,256]{1,0:T(8,128)(2,1)} %grad_ref.1), custom_call_target="tpu_custom_call" | custom-call | tf_op jit(solution)/shard_map/pallas_call | solution.py:152
  3.4 0.0 copy-start.6
  3.4 6.3 %all-to-all-start = ((bf16[8,400,128]{2,1,0:T(8,128)(2,1)}), bf16[8,400,128]{2,1,0:T(8,128)(2,1)S(1)}, u32[]{:S(2)}, u32[]{:S(2)}) async-start(bf16[8,400,128]{2,1,0:T(8,128)(2,1)} %shard_map.155), calls=%async_computation | async-start | bytes 1638400 | tf_op jit(solution)/shard_map/all_to_all | solution.py:21
  9.7 0.0 copy-start.7
  9.7 0.0 copy-done.6
  9.7 0.6 copy-done.7
  10.4 0.2 convolution_convert_fusion.rows_ref
  10.6 8.3 %all-to-all-done.got_ref = bf16[8,400,128]{2,1,0:T(8,128)(2,1)S(1)} async-done(((bf16[8,400,128]{2,1,0:T(8,128)(2,1)}), bf16[8,400,128]{2,1,0:T(8,128)(2,1)S(1)}, u32[]{:S(2)}, u32[]{:S(2)}) %all-to-all-start) | async-done | bytes 819232 | tf_op jit(solution)/shard_map/all_to_all | solution.py:21
  19.0 0.7 shard_map.156
  19.6 0.0 copy-start.4
  19.7 0.0 copy-start.5
  19.7 37.8 %all_to_all.35.came_ref = bf16[8,168,128]{2,1,0:T(8,128)(2,1)S(1)} all-to-all(bf16[8,168,128]{2,1,0:T(8,128)(2,1)S(1)} %get-tuple-element.13), channel_id=1, replica_groups={{0,2,4,6,8,10,12,14},{1,3,5,7,9,11,13,15},{16,18,20,22,24,26,28,30},{17..., dimensions={0} | all-to-all | bytes 688128 | tf_op jit(solution)/shard_map/all_to_all | solution.py:21
  57.4 0.0 copy-done.4
  57.4 0.0 copy-done.5
  57.4 0.3 shard_map.157
  57.8 9.9 %all_to_all.36.got_ref = bf16[4,320,128]{2,1,0:T(8,128)(2,1)S(1)} all-to-all(bf16[4,320,128]{2,1,0:T(8,128)(2,1)S(1)} %get-tuple-element.14), channel_id=1, replica_groups={{0,128,256,384},{64,192,320,448},{1,129,257,385},{65,193,321,449},{2,13..., dimensions={0} | all-to-all | bytes 655360 | tf_op jit(solution)/shard_map/all_to_all | solution.py:21
  67.7 0.0 copy-start.1
  67.7 0.0 copy-start.2
  67.7 0.0 copy-start.3
  67.7 8.0 %all-gather = bf16[1536,128]{1,0:T(8,128)(2,1)S(1)} all-gather(bf16[768,128]{1,0:T(8,128)(2,1)S(1)} %shard_map.158), channel_id=2, replica_groups={{0,64},{128,192},{256,320},{384,448},{1,65},{129,193},{257,321},{385,44..., dimensions={0}, use_global_device_ids=true | all-gather | bytes 589824 | tf_op jit(solution)/shard_map/all_gather | solution.py:467
  75.8 0.0 copy-done.1
  75.8 0.0 copy-done.2
  75.8 0.0 copy-done.3
  75.8 0.5 shard_map.159
  76.3 8.5 %all_to_all.37.got_ref = bf16[8,80,128]{2,1,0:T(8,128)(2,1)S(1)} all-to-all(bf16[8,80,128]{2,1,0:T(8,128)(2,1)S(1)} %get-tuple-element.17), channel_id=1, replica_groups={{0,1,16,17,32,33,48,49},{2,3,18,19,34,35,50,51},{4,5,20,21,36,37,52,53}..., dimensions={0} | all-to-all | bytes 327680 | tf_op jit(solution)/shard_map/all_to_all | solution.py:21
  84.8 19.9 %all_to_all.38.got_ref = bf16[8,112,128]{2,1,0:T(8,128)(2,1)S(1)} all-to-all(bf16[8,112,128]{2,1,0:T(8,128)(2,1)S(1)} %shard_map.160), channel_id=1, replica_groups={{0,2,4,6,8,10,12,14},{1,3,5,7,9,11,13,15},{16,18,20,22,24,26,28,30},{17..., dimensions={0} | all-to-all | bytes 458752 | tf_op jit(solution)/shard_map/all_to_all | solution.py:21
  104.7 0.2 shard_map.161
  104.9 0.0 copy-start
  104.9 9.6 %all_to_all.39.got_ref.lower_ref = bf16[8,208,128]{2,1,0:T(8,128)(2,1)S(1)} all-to-all(bf16[8,208,128]{2,1,0:T(8,128)(2,1)S(1)} %shard_map.161), channel_id=1, replica_groups={{0,1,16,17,32,33,48,49},{2,3,18,19,34,35,50,51},{4,5,20,21,36,37,52,53}..., dimensions={0} | all-to-all | bytes 851968 | tf_op jit(solution)/shard_map/all_to_all | solution.py:21
  114.5 0.0 copy-done
  114.5 0.2 shard_map.162
  114.7 7.4 %all_to_all.40 = bf16[4,160,128]{2,1,0:T(8,128)(2,1)S(1)} all-to-all(bf16[4,160,128]{2,1,0:T(8,128)(2,1)S(1)} %shard_map.162), channel_id=1, replica_groups={{0,128,256,384},{64,192,320,448},{1,129,257,385},{65,193,321,449},{2,13..., dimensions={0} | all-to-all | bytes 327680 | tf_op jit(solution)/shard_map/all_to_all | solution.py:21
  122.0 7.5 %all_gather.11.got_ref = bf16[2,640,128]{2,1,0:T(8,128)(2,1)S(1)} all-gather(bf16[1,640,128]{2,1,0:T(8,128)(2,1)S(1)} %bitcast.14), channel_id=1, replica_groups={{0,64},{128,192},{256,320},{384,448},{1,65},{129,193},{257,321},{385,44..., dimensions={0}, use_global_device_ids=true | all-gather | bytes 491520 | tf_op jit(solution)/shard_map/all_gather | solution.py:517
  129.6 1.0 shard_map.163
  (2 shorter events, 0.1 us)
Async XLA Ops:
  3.4 6.4 %copy-start.6 = (bf16[512,128]{1,0:T(8,128)(2,1)S(1)}, bf16[512,128]{1,0:T(8,128)(2,1)}, u32[]{:S(2)}) copy-start(bf16[512,128]{1,0:T(8,128)(2,1)} %features_hbm.1) | copy-start | bytes 393220
  3.4 15.6 %all-to-all-start = ((bf16[8,400,128]{2,1,0:T(8,128)(2,1)}), bf16[8,400,128]{2,1,0:T(8,128)(2,1)S(1)}, u32[]{:S(2)}, u32[]{:S(2)}) async-start(bf16[8,400,128]{2,1,0:T(8,128)(2,1)} %shard_map.155), calls=%async_computation | async-start | bytes 1638400 | tf_op jit(solution)/shard_map/all_to_all | solution.py:21
  9.7 0.7 copy-start.7
  19.6 37.8 %copy-start.4 = (bf16[128,256]{1,0:T(8,128)(2,1)S(1)}, bf16[128,256]{1,0:T(8,128)(2,1)}, u32[]{:S(2)}) copy-start(bf16[128,256]{1,0:T(8,128)(2,1)} %self_ref.3) | copy-start | bytes 196612
  19.7 37.8 %copy-start.5 = (bf16[128,256]{1,0:T(8,128)(2,1)S(1)}, bf16[128,256]{1,0:T(8,128)(2,1)}, u32[]{:S(2)}) copy-start(bf16[128,256]{1,0:T(8,128)(2,1)} %other_ref.3) | copy-start | bytes 196612
  67.7 8.1 %copy-start.1 = (bf16[256,256]{1,0:T(8,128)(2,1)S(1)}, bf16[256,256]{1,0:T(8,128)(2,1)}, u32[]{:S(2)}) copy-start(bf16[256,256]{1,0:T(8,128)(2,1)} %self_ref.5) | copy-start | bytes 393220
  67.7 8.1 %copy-start.2 = (bf16[256,256]{1,0:T(8,128)(2,1)S(1)}, bf16[256,256]{1,0:T(8,128)(2,1)}, u32[]{:S(2)}) copy-start(bf16[256,256]{1,0:T(8,128)(2,1)} %other_ref.5) | copy-start | bytes 393220
  67.7 8.0 %copy-start.3 = (bf16[128,256]{1,0:T(8,128)(2,1)S(1)}, bf16[128,256]{1,0:T(8,128)(2,1)}, u32[]{:S(2)}) copy-start(bf16[128,256]{1,0:T(8,128)(2,1)} %grad_ref.1) | copy-start | bytes 196612
  104.9 9.6 %copy-start = (bf16[1,4,128,128]{3,2,1,0:T(8,128)(2,1)S(1)}, bf16[1,4,128,128]{3,2,1,0:T(8,128)(2,1)}, u32[]{:S(2)}) copy-start(bf16[1,4,128,128]{3,2,1,0:T(8,128)(2,1)} %param.20) | copy-start | bytes 393220
